TPU v7x, 512 devices: a whole 4x4x16 slice. The times are simulated.
512 devices in a mesh: dom: 128 (over z, y, x_hi), rel: 4 (over x_lo, core).
Axes of the slice: x: 4 (x_hi: 2, x_lo: 2; x = x_hi * 2 + x_lo), y: 4, z: 16, core: 2. Of those that a mesh axis runs over, the one named last changes fastest.
Arguments:
- entities: float32 [131072, 400], P(('dom', 'rel')), may hold values from -1.5 to 1.5
- entity_state: float32 [131072], P(('dom', 'rel')), may hold values from 0.005 to 0.1
- relations: float32 [2560, 400], replicated, may hold values from -6 to 6
- relation_state: float32 [2560], replicated, may hold values from 0.01 to 0.3
- src_rows: int32 [128, 2, 1024], P('dom', None, 'rel'), may hold values from 0 to 1023
- rel_ids: int32 [128, 2, 1024], P('dom', None, 'rel'), may hold values from 0 to 2559
- dst_rows: int32 [128, 2, 1024], P('dom', None, 'rel'), may hold values from 0 to 1023
- live_count: int32 [128, 2, 4], P('dom', None, 'rel'), may hold values from 1 to 256, as said below
- neg_rows: int32 [128, 2, 1024], P('dom'), may hold values from 0 to 1023
Outputs:
- new_entities: float32 [131072, 400], P(('dom', 'rel'))
- new_entity_state: float32 [131072], P(('dom', 'rel'))
- new_relations: float32 [2560, 400], replicated
- new_relation_state: float32 [2560], replicated
Inputs may be any that keep to these rules, and one draw needn't show every extreme that they name: `live_count`: in each bucket and round exactly one of the 4 slots holds more than 128 live edges and the others at most 64; in every round some bucket has a full slot.
All inputs are finite; a program needn't handle non-finite values.
Results may differ from a plain program's by a relative error of at most 0.0003.
Values sent between devices are 32-bit elements; how exact they have to be, the bound alone decides.
No kernel may reach another device: no remote copies, remote signals or barrier semaphores. Data moves between devices by JAX's collectives and lax.ppermute only.
A program may use at most 128 MiB of HBM per device.

v0:
```python
import jax
import jax.numpy as jnp
from jax import lax
from jax.sharding import PartitionSpec as P

NEG = 1024
ROUNDS = 2
BLOCK = 128


HIGHEST = lax.Precision.HIGHEST
LEARN_RATE = 0.1
EPSILON = 1e-08


def from_partner(block, axis, apart):
    count = lax.axis_size(axis)
    route = []
    for low in range(count):
        high = low | 1 << apart
        if high != low and high < count:
            route += [(low, high), (high, low)]
    return lax.ppermute(block, axis, route)


def complex_product(first, second):
    half = first.shape[-1] // 2
    real_part = first[:, :half] * second[:, :half] - first[:, half:] * second[:, half:]
    imag_part = first[:, :half] * second[:, half:] + first[:, half:] * second[:, :half]
    return jnp.concatenate([real_part, imag_part], axis=1)


def complex_back(upstream, first, second):
    half = first.shape[-1] // 2
    up_real, up_imag = (upstream[:, :half], upstream[:, half:])
    d_first = jnp.concatenate(
        [
            up_real * second[:, :half] + up_imag * second[:, half:],
            up_imag * second[:, :half] - up_real * second[:, half:],
        ],
        axis=1,
    )
    d_second = jnp.concatenate(
        [
            up_real * first[:, :half] + up_imag * first[:, half:],
            up_imag * first[:, :half] - up_real * first[:, half:],
        ],
        axis=1,
    )
    return (d_first, d_second)


def arrange(source_list, kind_list, target_list, count_one):
    return (source_list, kind_list, target_list, count_one[0])


def train_bucket(source_slab, target_slab, table, arranged, negatives, carried):
    source_list, kind_list, target_list, live_total = arranged
    slot_count = source_list.shape[0]
    width = source_slab.shape[1]
    block_rows = min(BLOCK, slot_count)
    neg_table = target_slab[negatives]

    def block_step(block_idx, carry):
        head_rows, tail_rows, kind_rows, neg_sum = carry
        offset = block_idx * block_rows
        source_block = lax.dynamic_slice_in_dim(source_list, offset, block_rows)
        kind_block = lax.dynamic_slice_in_dim(kind_list, offset, block_rows)
        target_block = lax.dynamic_slice_in_dim(target_list, offset, block_rows)
        live_mask = (offset + jnp.arange(block_rows, dtype=jnp.int32) < live_total).astype(
            jnp.float32
        )
        head_vec = source_slab[source_block]
        rel_vec = table[kind_block]
        tail_vec = target_slab[target_block]
        product = complex_product(head_vec, rel_vec)
        pos_score = jnp.sum(product * tail_vec, axis=1)
        scores = jnp.dot(
            product, neg_table.T, precision=HIGHEST, preferred_element_type=jnp.float32
        )
        pos_weight = -jax.nn.sigmoid(-pos_score) * live_mask
        neg_weight = jax.nn.sigmoid(scores) * (live_mask / NEG)[:, None]
        d_product = pos_weight[:, None] * tail_vec + jnp.dot(
            neg_weight, neg_table, precision=HIGHEST, preferred_element_type=jnp.float32
        )
        neg_sum = neg_sum + jnp.dot(
            neg_weight.T, product, precision=HIGHEST, preferred_element_type=jnp.float32
        )
        d_head, d_rel = complex_back(d_product, head_vec, rel_vec)
        head_rows = lax.dynamic_update_slice_in_dim(head_rows, d_head, offset, 0)
        tail_rows = lax.dynamic_update_slice_in_dim(
            tail_rows, pos_weight[:, None] * product, offset, 0
        )
        kind_rows = lax.dynamic_update_slice_in_dim(kind_rows, d_rel, offset, 0)
        return (head_rows, tail_rows, kind_rows, neg_sum)

    block_total = (live_total + block_rows - 1) // block_rows
    empty_rows = jnp.zeros((slot_count, width), jnp.float32)
    start_carry = (
        empty_rows,
        empty_rows,
        empty_rows,
        jnp.zeros((negatives.shape[0], width), jnp.float32),
    )
    head_rows, tail_rows, kind_rows, neg_sum = lax.fori_loop(
        0, block_total, block_step, start_carry
    )
    grad_source = jnp.zeros_like(source_slab).at[source_list].add(head_rows)
    grad_target = (
        jnp.zeros_like(target_slab).at[target_list].add(tail_rows).at[negatives].add(neg_sum)
    )
    carried = carried.at[kind_list].add(kind_rows)
    return (grad_source, grad_target, carried)


def local(
    entities,
    entity_state,
    relations,
    relation_state,
    src_rows,
    rel_ids,
    dst_rows,
    live_count,
    neg_rows,
):
    top_bit = lax.axis_size("dom").bit_length() - 2
    rel_grad = jnp.zeros(relations.shape, jnp.float32)
    quarter, states = (entities, entity_state)
    for round_idx in range(ROUNDS):
        flip_bit = top_bit if round_idx == 0 else 0
        slab = lax.all_gather(quarter, "rel", axis=0, tiled=True)
        other_slab = from_partner(slab, "dom", flip_bit)
        own_lists = (
            src_rows[0, round_idx],
            rel_ids[0, round_idx],
            dst_rows[0, round_idx],
            live_count[0, round_idx],
        )
        own_negatives = neg_rows[0, round_idx]
        grad_source, grad_target, rel_grad = train_bucket(
            slab, other_slab, relations, arrange(*own_lists), own_negatives, rel_grad
        )
        local_grad = grad_source + from_partner(grad_target, "dom", flip_bit)
        gradient = lax.psum_scatter(local_grad, "rel", scatter_dimension=0, tiled=True)
        states = states + jnp.mean(gradient * gradient, axis=-1)
        quarter = quarter - LEARN_RATE * gradient / (jnp.sqrt(states)[:, None] + EPSILON)
    rel_total = lax.psum(rel_grad, ("dom", "rel"))
    new_relation_state = relation_state + jnp.mean(rel_total * rel_total, axis=-1)
    new_relations = relations - LEARN_RATE * rel_total / (
        jnp.sqrt(new_relation_state)[:, None] + EPSILON
    )
    return (quarter, states, new_relations, new_relation_state)


def solution(mesh):
    in_specs = (
        P(("dom", "rel"), None),
        P(("dom", "rel")),
        P(),
        P(),
        P("dom", None, "rel"),
        P("dom", None, "rel"),
        P("dom", None, "rel"),
        P("dom", None, "rel"),
        P("dom", None, None),
    )
    out_specs = (P(("dom", "rel"), None), P(("dom", "rel")), P(), P())
    return jax.shard_map(local, mesh=mesh, in_specs=in_specs, out_specs=out_specs, check_vma=False)
```

profile of v0, /device:TPU:1, one launch (start us, length us, event | category | flops | bytes accessed | tf_op | source)
XLA Modules:
  0.0 1127.2 jit_solution(17267576195860916220)
XLA Ops:
  7.9 40.9 %all-gather.3.cloned.1.call-done = f32[1024,400]{0,1:T(8,128)} async-done(((f32[256,400]{0,1:T(8,128)}), f32[1024,400]{0,1:T(8,128)}) %all-gather.3.cloned.1.call-update) | async-done | bytes 1638416 | tf_op jit(solution)/shard_map/all_gather | solution.py:132
  48.9 12.5 %collective-permute-start = (f32[1024,400]{0,1:T(8,128)}, f32[1024,400]{0,1:T(8,128)}, u32[]{:S(2)}, u32[]{:S(2)}) collective-permute-start(f32[1024,400]{0,1:T(8,128)} %all-gather.3.cloned.1.call-done), channel_id=1, source_target_pairs={{0,256},{256,0},{4,260},{260,4},{8,264},{264,8},{12,268},{268,12},... | collective-permute-start | bytes 4915208 | tf_op jit(solution)/shard_map/ppermute | solution.py:23
  61.4 1.3 fusion.25
  63.3 5.8 copy.82
  69.3 1.8 copy.81
  71.1 98.6 %collective-permute-done = f32[1024,400]{0,1:T(8,128)} collective-permute-done((f32[1024,400]{0,1:T(8,128)}, f32[1024,400]{0,1:T(8,128)}, u32[]{:S(2)}, u32[]{:S(2)}) %collective-permute-start) | collective-permute-done | bytes 1638432 | tf_op jit(solution)/shard_map/ppermute | solution.py:23
  169.7 1.8 copy.83
  171.5 4.9 gather_fusion.6
  178.7 1.4 broadcast.265.clone2
  180.2 21.8 %while.32 = (s32[]{:T(128)}, f32[256,400]{0,1:T(8,128)}, f32[256,400]{0,1:T(8,128)}, f32[256,400]{0,1:T(8,128)}, f32[1024,400]{0,1:T(8,128)}, /*index=5*/s32[]{:...) while((s32[]{:T(128)}, f32[256,400]{0,1:T(8,128)}, ...), condition=%wide.region_2.3_spmd, body=%wide.region_0.2_spmd.sunk | while | flops 1889399936 | bytes 40097872 | solution.py:105
  180.3 2.5 gather_fusion
  183.7 3.4 gather_fusion.1
  187.4 4.0 fusion.54
  193.2 5.2 convolution_add_fusion.8
  198.6 2.0 convolution_add_fusion.9
  200.7 1.2 copy-done.1
  202.0 1.2 copy.84
  203.2 2.8 copy.85
  206.1 2.6 scatter_custom_fusion
  208.6 8.0 scatter_fusion
  216.7 1.7 copy.86
  218.4 34.2 %collective-permute-start.1 = (f32[1024,400]{0,1:T(8,128)}, f32[1024,400]{0,1:T(8,128)}, u32[]{:S(2)}, u32[]{:S(2)}) collective-permute-start(f32[1024,400]{0,1:T(8,128)} %copy.86), channel_id=1, source_target_pairs={{0,256},{256,0},{4,260},{260,4},{8,264},{264,8},{12,268},{268,12},... | collective-permute-start | bytes 4915208 | tf_op jit(solution)/shard_map/ppermute | solution.py:23
  252.8 19.9 %collective-permute-done.1 = f32[1024,400]{0,1:T(8,128)} collective-permute-done((f32[1024,400]{0,1:T(8,128)}, f32[1024,400]{0,1:T(8,128)}, u32[]{:S(2)}, u32[]{:S(2)}) %collective-permute-start.1) | collective-permute-done | bytes 1638432 | tf_op jit(solution)/shard_map/ppermute | solution.py:23
  272.8 1.8 copy.87
  274.6 2.9 scatter_fusion.1
  277.5 1.3 copy-done.6
  279.1 157.6 %reduce-scatter.3.cloned.1.call-done = f32[256,400]{1,0:T(8,128)} async-done(((f32[1024,400]{1,0:T(8,128)}), f32[256,400]{1,0:T(8,128)}) %reduce-scatter.3.cloned.1.call-update) | async-done | bytes 409616 | tf_op jit(solution)/shard_map/reduce_scatter | solution.py:145
  436.7 1.2 multiply_reduce_fusion.4
  437.9 2.0 divide_subtract_fusion.2
  439.9 38.1 %all-gather.5.cloned.1.call-done = f32[1024,400]{1,0:T(8,128)} async-done(((f32[256,400]{1,0:T(8,128)}), f32[1024,400]{1,0:T(8,128)}) %all-gather.5.cloned.1.call-update) | async-done | bytes 1638416 | tf_op jit(solution)/shard_map/all_gather | solution.py:132
  478.0 1.8 copy.90
  479.9 4.3 collective-permute-start.2
  485.1 4.7 scatter_custom_fusion.6
  489.9 30.9 %collective-permute-done.2 = f32[1024,400]{0,1:T(8,128)} collective-permute-done((f32[1024,400]{0,1:T(8,128)S(1)}, f32[1024,400]{0,1:T(8,128)}, u32[]{:S(2)}, u32[]{:S(2)}) %collective-permute-start.2) | collective-permute-done | bytes 1638432 | tf_op jit(solution)/shard_map/ppermute | solution.py:23
  520.7 1.8 copy.94
  522.6 4.9 gather_fusion.7
  529.1 0.8 broadcast.268.clone.4
  529.9 1.4 broadcast.265.clone
  531.2 22.0 %while.33 = (s32[]{:T(128)}, f32[256,400]{0,1:T(8,128)}, f32[256,400]{0,1:T(8,128)}, f32[256,400]{0,1:T(8,128)}, f32[1024,400]{0,1:T(8,128)}, /*index=5*/s32[]{:...) while((s32[]{:T(128)}, f32[256,400]{0,1:T(8,128)}, ...), condition=%wide.region_10.11_spmd, body=%wide.region_8.10_spmd.sunk | while | flops 1889399936 | bytes 40097872 | solution.py:105
  531.5 2.5 gather_fusion.3
  535.0 3.4 gather_fusion.4
  538.7 4.0 fusion.61
  544.6 5.2 convolution_add_fusion.10
  550.0 2.0 convolution_add_fusion.11
  552.1 1.1 copy-done.3
  553.2 1.2 copy.101
  554.4 6.9 scatter_fusion.4
  562.9 1.8 copy.96
  564.6 2.6 scatter_custom_fusion.3
  567.2 8.0 scatter_fusion.2
  575.3 1.7 copy.97
  577.0 4.3 collective-permute-start.3
  581.5 36.9 %collective-permute-done.3 = f32[1024,400]{0,1:T(8,128)} collective-permute-done((f32[1024,400]{0,1:T(8,128)}, f32[1024,400]{0,1:T(8,128)}, u32[]{:S(2)}, u32[]{:S(2)}) %collective-permute-start.3) | collective-permute-done | bytes 1638432 | tf_op jit(solution)/shard_map/ppermute | solution.py:23
  618.4 1.9 copy.98
  620.2 2.9 scatter_fusion.3
  623.1 1.3 copy-done.5
  624.5 453.1 %all-reduce.2.cloned.1.call-done = f32[2560,400]{1,0:T(8,128)} async-done(((f32[2560,400]{1,0:T(8,128)}), f32[2560,400]{1,0:T(8,128)}) %all-reduce.2.cloned.1.call-update) | async-done | bytes 4096016 | tf_op jit(solution)/shard_map/psum | solution.py:148
  1077.5 3.1 multiply_reduce_fusion.2
  1081.6 4.7 divide_subtract_fusion
  1086.3 5.6 copy.104
  1091.9 24.5 %reduce-scatter.5.cloned.1.call-done = f32[256,400]{1,0:T(8,128)} async-done(((f32[1024,400]{1,0:T(8,128)}), f32[256,400]{1,0:T(8,128)}) %reduce-scatter.5.cloned.1.call-update) | async-done | bytes 409616 | tf_op jit(solution)/shard_map/reduce_scatter | solution.py:145
  1116.4 1.2 multiply_reduce_fusion.3
  1118.1 1.2 divide_subtract_fusion.1
  1119.3 0.9 copy.103
  (152 shorter events, 15.3 us)
Async XLA Ops:
  7.2 41.7 %all-gather.3.cloned.1.call-start = ((), (), s32[]{:S(2)}) async-start(), calls=%async_computation.2 | async-start | bytes 2048000 | tf_op jit(solution)/shard_map/all_gather | solution.py:132
  7.9 428.8 %reduce-scatter.3.cloned.1.call-start = ((), (), s32[]{:S(2)}) async-start(), calls=%async_computation.3 | async-start | bytes 2621440 | tf_op jit(solution)/shard_map/reduce_scatter | solution.py:145
  48.9 120.8 %collective-permute-start = (f32[1024,400]{0,1:T(8,128)}, f32[1024,400]{0,1:T(8,128)}, u32[]{:S(2)}, u32[]{:S(2)}) collective-permute-start(f32[1024,400]{0,1:T(8,128)} %all-gather.3.cloned.1.call-done), channel_id=1, source_target_pairs={{0,256},{256,0},{4,260},{260,4},{8,264},{264,8},{12,268},{268,12},... | collective-permute-start | bytes 4915208 | tf_op jit(solution)/shard_map/ppermute | solution.py:23
  63.3 5.9 copy-start.37
  63.3 5.9 copy-start.38
  63.3 5.9 copy-start.39
  63.3 5.9 copy-start.36
  63.3 6.0 copy-start.17
  187.3 4.2 copy-start.7
  187.4 4.1 copy-start.11
  192.4 5.9 copy-start.8
  192.4 5.9 copy-start.12
  192.5 5.9 copy-start.19
  192.5 5.9 copy-start.24
  193.2 5.4 copy-start.22
  193.2 5.4 copy-start
  198.5 2.1 copy-start.20
  198.5 2.1 copy-start.25
  198.6 2.1 copy-start.23
  200.6 1.3 copy-start.1
  216.7 35.9 %copy-start.21 = (f32[256,400]{0,1:T(8,128)S(1)}, f32[256,400]{0,1:T(8,128)}, u32[]{:S(2)}) copy-start(f32[256,400]{0,1:T(8,128)} %get-tuple-element.158) | copy-start | bytes 1228804
  218.4 54.4 %collective-permute-start.1 = (f32[1024,400]{0,1:T(8,128)}, f32[1024,400]{0,1:T(8,128)}, u32[]{:S(2)}, u32[]{:S(2)}) collective-permute-start(f32[1024,400]{0,1:T(8,128)} %copy.86), channel_id=1, source_target_pairs={{0,256},{256,0},{4,260},{260,4},{8,264},{264,8},{12,268},{268,12},... | collective-permute-start | bytes 4915208 | tf_op jit(solution)/shard_map/ppermute | solution.py:23
  277.5 1.3 copy-start.6
  277.5 1.4 copy-start.18
  277.5 160.4 %copy-start.40 = (f32[256]{0:T(256)S(1)}, f32[256]{0:T(256)}, u32[]{:S(2)}) copy-start(f32[256]{0:T(256)} %param.14) | copy-start | bytes 3076
  278.8 199.2 %all-gather.5.cloned.1.call-start = ((), (), s32[]{:S(2)}) async-start(), calls=%async_computation.4 | async-start | bytes 2621440 | tf_op jit(solution)/shard_map/all_gather | solution.py:132
  439.9 45.0 %copy-start.26 = (f32[256,400]{0,1:T(8,128)S(1)}, f32[256,400]{0,1:T(8,128)}, u32[]{:S(2)}) copy-start(f32[256,400]{0,1:T(8,128)} %get-tuple-element.162) | copy-start | bytes 1228804
  439.9 637.7 %all-reduce.2.cloned.1.call-start = ((), (), s32[]{:S(2)}) async-start(), calls=%async_computation.6 | async-start | bytes 10485760 | tf_op jit(solution)/shard_map/psum | solution.py:148
  479.9 40.9 %collective-permute-start.2 = (f32[1024,400]{0,1:T(8,128)S(1)}, f32[1024,400]{0,1:T(8,128)}, u32[]{:S(2)}, u32[]{:S(2)}) collective-permute-start(f32[1024,400]{0,1:T(8,128)S(1)} %copy.90), channel_id=1, source_target_pairs={{0,4},{4,0},{8,12},{12,8},{16,20},{20,16},{24,28},{28,24},{32,36},... | collective-permute-start | bytes 4915208 | tf_op jit(solution)/shard_map/ppermute | solution.py:23
  538.6 4.2 copy-start.9
  538.7 4.1 copy-start.13
  543.7 6.0 copy-start.10
  543.7 6.0 copy-start.14
  543.8 6.0 copy-start.27
  543.8 6.0 copy-start.33
  544.6 5.4 copy-start.30
  544.6 5.4 copy-start.2
  549.9 2.1 copy-start.28
  549.9 2.1 copy-start.34
  550.0 2.1 copy-start.31
  552.0 1.2 copy-start.3
  561.3 1.0 copy-start.32
  561.3 1.6 copy-start.4
  561.3 555.1 %reduce-scatter.5.cloned.1.call-start = ((), (), s32[]{:S(2)}) async-start(), calls=%async_computation.5 | async-start | bytes 2621440 | tf_op jit(solution)/shard_map/reduce_scatter | solution.py:145
  575.3 6.0 copy-start.29
  577.0 41.4 %collective-permute-start.3 = (f32[1024,400]{0,1:T(8,128)}, f32[1024,400]{0,1:T(8,128)}, u32[]{:S(2)}, u32[]{:S(2)}) collective-permute-start(f32[1024,400]{0,1:T(8,128)} %copy.97), channel_id=1, source_target_pairs={{0,4},{4,0},{8,12},{12,8},{16,20},{20,16},{24,28},{28,24},{32,36},... | collective-permute-start | bytes 4915208 | tf_op jit(solution)/shard_map/ppermute | solution.py:23
  623.1 1.3 copy-start.5
  624.5 456.2 %copy-start.35 = (f32[2560]{0:T(1024)S(1)}, f32[2560]{0:T(1024)}, u32[]{:S(2)}) copy-start(f32[2560]{0:T(1024)} %param.16) | copy-start | bytes 30724
  1077.5 4.0 copy-start.15
  1086.3 31.8 %copy-start.16 = (f32[256,400]{1,0:T(8,128)S(1)}, f32[256,400]{1,0:T(8,128)}, u32[]{:S(2)}) copy-start(f32[256,400]{1,0:T(8,128)} %divide_subtract_fusion.2) | copy-start | bytes 1228804
Sparse Core Ops, SparseCore 0:
  10.1 38.7 all-gather.2
  278.9 157.7 reduce-scatter.2
  440.0 37.9 all-gather.4
  561.5 516.0 all-reduce.1
  1080.2 36.1 reduce-scatter.4
where the time goes:
time: 1140 us; the launch traced here: 1130 us
  waiting for transfers between devices  901 us (79%)
  local copies, waits for them, and re-layouts  74.3 us (7%)
  other arithmetic  56.7 us (5%)
  starting transfers between devices  55.8 us (5%)
  matrix products  22.3 us (2%)
  between operations  15.9 us (1%)
    psum x1, waiting for transfers between devices, local(): rel_total = lax.psum(rel_grad, ('dom', 'rel'))  453 us
    ppermute x4, waiting for transfers between devices, from_partner(): return lax.ppermute(block, axis, route)  186 us
    reduce_scatter x2, waiting for transfers between devices, local(): lax.psum_scatter(local_grad, 'rel', scatter_dimension=0, tiled=True)  182 us
    all_gather x2, waiting for transfers between devices, local(): slab = lax.all_gather(quarter, 'rel', axis=0, tiled=True)  79 us
    ppermute x4, starting transfers between devices, from_partner(): return lax.ppermute(block, axis, route)  55.4 us
  transfers between devices with their start and end apart: 9, of which 9 were waited for; matrix products, arithmetic and copies ran while one was open for 4% of the time, Pallas kernels for 0%

commit v1 on v0

v1 whole, which is shorter than its diff:
```python
import functools

import jax
import jax.numpy as jnp
from jax import lax
from jax.experimental import pallas as pl
from jax.experimental.pallas import tpu as pltpu
from jax.sharding import Mesh, PartitionSpec as P

D = 400
HALF = 200
RELATIONS = 2560
NEG = 1024
ROUNDS = 2
CAP = 256
LIGHT = 64
SLOTS = 512
CHUNK = 128
ROWS = 256
QUARTER = RELATIONS // 4
KROWS = 2048
LEARN_RATE = 0.1
EPSILON = 1e-08
REL = ("l", "c")
SPREAD = ("y", "h")
F32, BF16, I32 = jnp.float32, jnp.bfloat16, jnp.int32
VMEM = pl.BlockSpec(memory_space=pltpu.VMEM)
SMEM = pl.BlockSpec(memory_space=pltpu.SMEM)


def flip(block, axis, mask):
    count = lax.axis_size(axis)
    return lax.ppermute(block, axis, [(i, i ^ mask) for i in range(count)])


def split(value):
    high = value.astype(BF16)
    return high, (value - high.astype(F32)).astype(BF16)


def dot(first, second, over):
    return lax.dot_general(first, second, ((over[:1], over[1:]), ((), ())), preferred_element_type=F32)


def dot2(first, second, over):
    return dot(first[0], second, over) + dot(first[1], second, over)


def dot3(first, second, over):
    return dot(first[0], second[0], over) + (dot(first[0], second[1], over) + dot(first[1], second[0], over))


def places(rows, ids, base):
    return lax.broadcasted_iota(I32, (rows, ids.shape[-1]), 0) + base == ids


def hot(rows, ids, base):
    return jnp.where(places(rows, ids, base), 1.0, 0.0).astype(BF16)


def call(kernel, out_shape, in_specs, scratch, flops, moved, **more):
    return pl.pallas_call(
        kernel,
        out_shape=out_shape,
        in_specs=in_specs,
        scratch_shapes=scratch,
        compiler_params=pltpu.CompilerParams(vmem_limit_bytes=40 * 1024 * 1024),
        cost_estimate=pl.CostEstimate(flops=flops, bytes_accessed=moved, transcendentals=0),
        **more,
    )


def shape(*dims):
    return jax.ShapeDtypeStruct(dims, F32)


def lookup_kernel(q_ref, ids_ref, neg_ref, table_ref, out_ref, count_ref, high_ref, low_ref):
    @pl.when(pl.program_id(0) == 0)
    def _():
        high_ref[...], low_ref[...] = split(table_ref[...])

    ids = ids_ref[0]
    total = jnp.zeros((D, SLOTS), F32)
    for part in range(RELATIONS // 512):
        at = slice(512 * part, 512 * part + 512)
        total += dot2((high_ref[:, at], low_ref[:, at]), hot(512, ids, 512 * part), (1, 0))
    out_ref[0] = total
    hits = jnp.where(places(ROWS, neg_ref[0], ROWS * q_ref[0]), 1.0, 0.0)
    count_ref[0] = jnp.sum(hits, axis=1, keepdims=True)


def lookup(q, ids, negatives, table):
    return call(
        lookup_kernel,
        [shape(ROUNDS, D, SLOTS), shape(ROUNDS, ROWS, 1)],
        [
            SMEM,
            pl.BlockSpec((1, 1, SLOTS), lambda t: (t, 0, 0)),
            pl.BlockSpec((1, 1, NEG), lambda t: (t, 0, 0)),
            pl.BlockSpec((D, RELATIONS), lambda t: (0, 0)),
        ],
        [pltpu.VMEM((D, RELATIONS), BF16)] * 2,
        2 * 2 * 2 * D * RELATIONS * SLOTS,
        8 * 1024 * 1024,
        grid=(ROUNDS,),
        out_specs=[
            pl.BlockSpec((1, D, SLOTS), lambda t: (t, 0, 0)),
            pl.BlockSpec((1, ROWS, 1), lambda t: (t, 0, 0)),
        ],
    )(q, ids, negatives, table)


def score_kernel(q_ref, ids_ref, near_ref, far_ref, rel_ref, count_ref, own_ref, back_ref, grad_ref, head_ref, kind_ref, high_ref, low_ref, h_ref, a_ref):
    q = q_ref[0]
    for k in range(4):
        for ref, at in ((near_ref, 256 * k), (far_ref, 256 * k + 128)):
            high_ref[:, at : at + 128], low_ref[:, at : at + 128] = split(ref[k])
    a_ref[...] = dot2((high_ref[...], low_ref[...]), hot(1024, ids_ref[0:1, :], 0), (1, 0))
    a1, a2 = a_ref[:HALF, :], a_ref[HALF:, :]
    w1, w2 = rel_ref[0, :HALF, :], rel_ref[0, HALF:, :]
    h_ref[:HALF, :] = a1 * w1 - a2 * w2
    h_ref[HALF:, :] = a1 * w2 + a2 * w1
    product = split(h_ref[...])
    own = split(own_ref[...])
    scores = dot3(own, product, (0, 0))
    small = jnp.exp(-jnp.abs(scores))
    larger = 1.0 / (1.0 + small)
    smaller = small * larger
    rising = scores >= 0
    target = ids_ref[2:3, :]
    live = jnp.where(target >= 0, 1.0 / NEG, 0.0)
    weight = jnp.where(rising, larger, smaller) * count_ref[0] * live
    weight -= jnp.where(places(ROWS, target, ROWS * q), jnp.where(rising, smaller, larger), 0.0)
    weight = split(weight)
    d_product = dot3(own, weight, (1, 0))
    for k in range(4):
        back_ref[k] = d_product[:, CHUNK * k : CHUNK * k + CHUNK]
    grad_ref[...] = dot3(product, weight, (1, 1))
    mine = pl.ds(pl.multiple_of(CHUNK * q, CHUNK), CHUNK)
    head_ref[...] = a_ref[:, mine]
    kind_ref[...] = rel_ref[0, :, mine]


def score(q, ids, near, far, rel_rows, counts, own, round_idx):
    return call(
        score_kernel,
        [shape(4, D, CHUNK), shape(D, ROWS), shape(D, CHUNK), shape(D, CHUNK)],
        [
            SMEM,
            pl.BlockSpec((4, SLOTS), lambda i: (0, 0)),
            pl.BlockSpec((4, D, CHUNK), lambda i: (0, 0, 0)),
            pl.BlockSpec((4, D, CHUNK), lambda i: (0, 0, 0)),
            pl.BlockSpec((1, D, SLOTS), lambda i: (round_idx, 0, 0)),
            pl.BlockSpec((1, ROWS, 1), lambda i: (round_idx, 0, 0)),
            pl.BlockSpec((D, ROWS), lambda i: (0, 0)),
        ],
        [pltpu.VMEM((D, 1024), BF16)] * 2 + [pltpu.VMEM((D, SLOTS), F32)] * 2,
        2 * 1024 * 1024 * 1024,
        8 * 1024 * 1024,
        grid=(1,),
        out_specs=[
            pl.BlockSpec((4, D, CHUNK), lambda i: (0, 0, 0)),
            pl.BlockSpec((D, ROWS), lambda i: (0, 0)),
            pl.BlockSpec((D, CHUNK), lambda i: (0, 0)),
            pl.BlockSpec((D, CHUNK), lambda i: (0, 0)),
        ],
    )(q, ids, near, far, rel_rows, counts, own)


def back_kernel(parts_ref, head_ref, kind_ref, d_head_ref, d_kind_ref):
    up = (parts_ref[0] + parts_ref[1]) + (parts_ref[2] + parts_ref[3])
    u1, u2 = up[:HALF, :], up[HALF:, :]
    for other_ref, out_ref in ((kind_ref, d_head_ref), (head_ref, d_kind_ref)):
        o1, o2 = other_ref[:HALF, :], other_ref[HALF:, :]
        out_ref[:HALF, :] = u1 * o1 + u2 * o2
        out_ref[HALF:, :] = u2 * o1 - u1 * o2


def back(parts, head, kind):
    return call(
        back_kernel,
        [shape(D, CHUNK)] * 2,
        [VMEM] * 3,
        [],
        10 * D * CHUNK,
        8 * D * CHUNK * 4,
        out_specs=[VMEM] * 2,
    )(parts, head, kind)


def gather_parts(parts_ref, high_ref, low_ref):
    for k in range(4):
        at = slice(CHUNK * k, CHUNK * k + CHUNK)
        high_ref[:, at], low_ref[:, at] = split(parts_ref[k])


def update_kernel(q_ref, ids_ref, parts_ref, grad_ref, own_ref, state_ref, out_ref, out_state_ref, high_ref, low_ref):
    gather_parts(parts_ref, high_ref, low_ref)
    spots = hot(ROWS, ids_ref[3:4, :], ROWS * q_ref[0])
    gradient = grad_ref[...] + dot2((high_ref[...], low_ref[...]), spots, (1, 1))
    state = state_ref[...] + jnp.sum(gradient * gradient, axis=0, keepdims=True) * (1.0 / D)
    out_state_ref[...] = state
    out_ref[...] = own_ref[...] - gradient * (LEARN_RATE / (jnp.sqrt(state) + EPSILON))


def update(q, ids, parts, grad, own, state):
    return call(
        update_kernel,
        [shape(D, ROWS), shape(1, ROWS)],
        [SMEM] + [VMEM] * 5,
        [pltpu.VMEM((D, SLOTS), BF16)] * 2,
        2 * 2 * D * SLOTS * ROWS,
        2 * 1024 * 1024,
        out_specs=[VMEM] * 2,
    )(q, ids, parts, grad, own, state)


def kinds_kernel(first, q_ref, ids_ref, parts_ref, *refs):
    out_ref, high_ref, low_ref = refs[-3:]
    gather_parts(parts_ref, high_ref, low_ref)
    spots = hot(QUARTER, ids_ref[1:2, :], QUARTER * q_ref[0])
    total = dot2((high_ref[...], low_ref[...]), spots, (1, 1))
    for k in range(5):
        at = slice(D * k, D * k + D)
        tile = total[:, 128 * k : 128 * k + 128]
        out_ref[at, :] = tile if first else refs[0][at, :] + tile
    out_ref[5 * D :, :] = jnp.zeros((KROWS - 5 * D, 128), F32)


def kinds(q, ids, parts, before):
    more = [] if before is None else [before]
    return call(
        functools.partial(kinds_kernel, before is None),
        shape(KROWS, 128),
        [SMEM] + [VMEM] * (2 + len(more)),
        [pltpu.VMEM((D, SLOTS), BF16)] * 2,
        2 * 2 * D * SLOTS * QUARTER,
        3 * 1024 * 1024,
        out_specs=VMEM,
    )(q, ids, parts, *more)


def relations_kernel(q_ref, *refs):
    grads, (table_ref, state_ref, out_ref, out_state_ref) = refs[:4], refs[4:]
    for d in range(4):

        @pl.when(pl.program_id(0) == d)
        def _():
            for k in range(5):
                at = slice(128 * k, 128 * k + 128)
                gradient = grads[d][D * k : D * k + D, :]
                state = state_ref[:, at] + jnp.sum(gradient * gradient, axis=0, keepdims=True) * (1.0 / D)
                out_state_ref[:, at] = state
                out_ref[:, at] = table_ref[:, at] - gradient * (LEARN_RATE / (jnp.sqrt(state) + EPSILON))


def update_relations(q, grads, table, state):
    mine = lambda d, q: (0, d ^ q[0])
    whole = lambda d, q: (0, 0)
    return pl.pallas_call(
        relations_kernel,
        out_shape=[shape(D, RELATIONS), shape(1, RELATIONS)],
        grid_spec=pltpu.PrefetchScalarGridSpec(
            num_scalar_prefetch=1,
            grid=(4,),
            in_specs=[pl.BlockSpec((KROWS, 128), whole)] * 4
            + [pl.BlockSpec((D, QUARTER), mine), pl.BlockSpec((1, QUARTER), mine)],
            out_specs=[pl.BlockSpec((D, QUARTER), mine), pl.BlockSpec((1, QUARTER), mine)],
        ),
        compiler_params=pltpu.CompilerParams(vmem_limit_bytes=40 * 1024 * 1024),
        cost_estimate=pl.CostEstimate(flops=10 * D * RELATIONS, bytes_accessed=12 * 1024 * 1024, transcendentals=0),
    )(q, *grads, table, state)


def exchange_lists(src_rows, rel_ids, dst_rows, live_count, neg_rows):
    live = jnp.arange(CAP, dtype=I32)[None, :] < live_count[0]
    lists = jnp.where(live[:, None, :], jnp.stack([src_rows[0], rel_ids[0], dst_rows[0]], axis=1), -1)
    negatives, worked = [], []
    for t, (axis, mask) in enumerate((("z", 8), ("h", 1))):
        sent = jnp.concatenate([lists[t].reshape(6, 128), neg_rows[0, t].reshape(8, 128)], axis=0)
        got = flip(sent, axis, mask)
        worked.append(got[:6])
        negatives.append(got[6:].reshape(1, NEG))
    mine = jnp.concatenate(worked + [lists[:, 0].reshape(4, 128)], axis=0)
    every = lax.all_gather(mine, REL, axis=0).reshape(4, 8, CAP)
    light = jnp.moveaxis(every[:, :, :LIGHT], 0, 1).reshape(8, 4 * LIGHT)
    heavy = jnp.max(every[:, :, LIGHT:], axis=0)
    slots = jnp.concatenate([light, heavy, jnp.full((8, SLOTS - 4 * LIGHT - (CAP - LIGHT)), -1, I32)], axis=1)
    ids = [jnp.concatenate([slots[3 * t : 3 * t + 3], slots[6 + t : 7 + t]], axis=0) for t in range(ROUNDS)]
    return ids, jnp.stack(negatives)


def local(entities, entity_state, relations, relation_state, src_rows, rel_ids, dst_rows, live_count, neg_rows):
    q = lax.axis_index(REL).astype(I32).reshape(1)
    own, state = entities.T, entity_state.reshape(1, ROWS)
    table = relations.T
    ids, negatives = exchange_lists(src_rows, rel_ids, dst_rows, live_count, neg_rows)
    rel_rows, counts = lookup(q, jnp.stack([ids[0][1:2], ids[1][1:2]]), negatives, table)
    total = None
    for t, (axis, mask) in enumerate((("z", 8), ("h", 1))):
        near = lax.all_gather(flip(own[:, :128], axis, mask), REL, axis=0)
        far = lax.all_gather(flip(own[:, 128:], axis, mask), REL, axis=0)
        parts, grad, head, kind = score(q, ids[t], near, far, rel_rows, counts, own, t)
        parts = lax.all_to_all(parts, REL, 0, 0)
        d_head, d_kind = back(parts, head, kind)
        d_heads = lax.all_gather(flip(d_head, axis, mask), REL, axis=0)
        own, state = update(q, ids[t], d_heads, grad, own, state)
        total = kinds(q, ids[t], lax.all_gather(d_kind, REL, axis=0), total)
    shares = lax.all_to_all(total.reshape(8, 256, 128), SPREAD, 0, 0)
    share = jnp.sum(shares, axis=0)
    pieces = lax.all_to_all(share.reshape(16, 16, 128), "z", 0, 0)
    piece = jnp.sum(pieces, axis=0)
    share = lax.all_to_all(jnp.broadcast_to(piece[None], (16, 16, 128)), "z", 0, 0).reshape(256, 128)
    whole = lax.all_to_all(jnp.broadcast_to(share[None], (8, 256, 128)), SPREAD, 0, 0).reshape(KROWS, 128)
    across = flip(whole, "l", 1)
    grads = [whole, flip(whole, "c", 1), across, flip(across, "c", 1)]
    new_table, new_table_state = update_relations(q, grads, table, relation_state.reshape(1, RELATIONS))
    return own.T, state.reshape(ROWS), new_table.T, new_table_state.reshape(RELATIONS)


def solution(mesh):
    fine = Mesh(mesh.devices.reshape(16, 4, 2, 2, 2), ("z", "y", "h", "l", "c"))
    dom, rel = ("z", "y", "h"), REL
    edge = P(dom, None, rel)
    in_specs = (P(dom + rel, None), P(dom + rel), P(), P(), edge, edge, edge, edge, P(dom, None, None))
    out_specs = (P(dom + rel, None), P(dom + rel), P(), P())
    return jax.shard_map(local, mesh=fine, in_specs=in_specs, out_specs=out_specs, check_vma=False)
```

time: 1140 us -> 329 us (0.29); the launches traced: 1130 us -> 328 us
  waiting for transfers between devices: 901 us -> 37.5 us
  blocking collectives: 0 us -> 197 us
  local copies, waits for them, and re-layouts: 74.3 us -> 4.4 us
  other arithmetic: 56.7 us -> 2.28 us
  matrix products: 22.3 us -> 0 us
  Pallas kernels: 0 us -> 18.8 us
  between operations: 15.9 us -> 1 us
    psum x1 -> x0, waiting for transfers between devices: 453 us -> none  [local(): rel_total = lax.psum(rel_grad, ('dom', 'rel'))]
    reduce_scatter x2 -> x0, waiting for transfers between devices: 182 us -> none  [local(): lax.psum_scatter(local_grad, 'rel', scatter_dimension=0, tiled=True)]
    ppermute x4 -> x11, waiting for transfers between devices: 186 us -> 37.5 us  [flip(): return lax.ppermute(block, axis, [(i, i ^ mask) for i in range(count)])]
    all_gather x0 -> x9, blocking collectives: none -> 107 us  [the longest x2 28.4 us: local(): d_heads = lax.all_gather(flip(d_head, axis, mask), REL, axis=0)]
    all_to_all x0 -> x5, blocking collectives: none -> 90.2 us  [the longest x1 22.7 us: local(): shares = lax.all_to_all(total.reshape(8, 256, 128), SPREAD, 0, 0)]
    all_gather x2 -> x0, waiting for transfers between devices: 79 us -> none  [local(): slab = lax.all_gather(quarter, 'rel', axis=0, tiled=True)]
    scatter-add x8 -> x0, other arithmetic: 38.6 us -> none  [the longest x4 21.2 us: train_bucket(): jnp.zeros_like(target_slab).at[target_list].add(tail_rows).at[negatives]]
    gather x10 -> x0, local copies, waits for them, and re-layouts: 23.2 us -> none  [the longest x2 9.77 us: train_bucket(): neg_table = target_slab[negatives]]
  transfers between devices with their start and end apart: 9 -> 12, of which waited for: 9 -> 4; matrix products, arithmetic and copies ran while one was open for 4% -> 0% of each run, Pallas kernels for 0% -> 2%
where the time goes in v1:
time: 329 us; the launch traced here: 328 us
  blocking collectives  197 us (60%)
  starting transfers between devices  67 us (20%)
  waiting for transfers between devices  37.5 us (11%)
  Pallas kernels  18.8 us (6%)
  local copies, waits for them, and re-layouts  4.4 us (1%)
    ppermute x11, starting transfers between devices, flip(): return lax.ppermute(block, axis, [(i, i ^ mask) for i in range(count)])  63.4 us
    ppermute x11, waiting for transfers between devices, flip(): return lax.ppermute(block, axis, [(i, i ^ mask) for i in range(count)])  37.5 us
    all_gather x2, blocking collectives, local(): d_heads = lax.all_gather(flip(d_head, axis, mask), REL, axis=0)  28.4 us
    all_gather x2, blocking collectives, local(): near = lax.all_gather(flip(own[:, :128], axis, mask), REL, axis=0)  27.5 us
    all_gather x2, blocking collectives, local(): total = kinds(q, ids[t], lax.all_gather(d_kind, REL, axis=0), total)  26.2 us
    all_to_all x1, blocking collectives, local(): shares = lax.all_to_all(total.reshape(8, 256, 128), SPREAD, 0, 0)  22.7 us
    all_to_all x1, blocking collectives, local(): pieces = lax.all_to_all(share.reshape(16, 16, 128), 'z', 0, 0)  20.2 us
    all_gather x2, blocking collectives, local(): far = lax.all_gather(flip(own[:, 128:], axis, mask), REL, axis=0)  17.8 us
  transfers between devices with their start and end apart: 12, of which 4 were waited for; matrix products, arithmetic and copies ran while one was open for 0% of the time, Pallas kernels for 2%

profile of v1, /device:TPU:1, one launch (start us, length us, event | category | flops | bytes accessed | tf_op | source)
XLA Modules:
  0.0 327.9 jit_solution(8641949090539262753)
XLA Ops:
  0.6 0.7 iota_compare_fusion
  1.4 0.7 add_select_fusion
  2.1 0.8 fusion.3
  2.9 5.5 %collective-permute-start.1 = (s32[14,128]{1,0:T(8,128)S(1)}, s32[14,128]{1,0:T(8,128)S(1)}, u32[]{:S(2)}, u32[]{:S(2)}) collective-permute-start(s32[14,128]{1,0:T(8,128)S(1)} %pad_add_fusion.1), channel_id=1, source_target_pairs={{0,4},{4,0},{1,5},{5,1},{2,6},{6,2},{3,7},{7,3},{8,12},{12,8},{9,1... | collective-permute-start | bytes 21512 | tf_op jit(solution)/shard_map/ppermute | solution.py:33
  8.4 15.4 %collective-permute-start = (s32[14,128]{1,0:T(8,128)S(1)}, s32[14,128]{1,0:T(8,128)S(1)}, u32[]{:S(2)}, u32[]{:S(2)}) collective-permute-start(s32[14,128]{1,0:T(8,128)S(1)} %pad_add_fusion), channel_id=1, source_target_pairs={{0,256},{32,288},{64,320},{96,352},{128,384},{160,416},{192,448},{... | collective-permute-start | bytes 21512 | tf_op jit(solution)/shard_map/ppermute | solution.py:33
  23.9 1.1 fusion.1
  24.9 1.9 collective-permute-start.3
  26.9 12.1 %collective-permute-start.2 = (f32[400,128]{1,0:T(8,128)S(1)}, f32[400,128]{1,0:T(8,128)S(1)}, u32[]{:S(2)}, u32[]{:S(2)}) collective-permute-start(f32[400,128]{1,0:T(8,128)S(1)} %get-tuple-element.49), channel_id=1, source_target_pairs={{0,256},{32,288},{64,320},{96,352},{128,384},{160,416},{192,448},{... | collective-permute-start | bytes 614408 | tf_op jit(solution)/shard_map/ppermute | solution.py:33
  39.0 0.1 pad.10.clone
  39.1 0.0 collective-permute-done.1
  39.1 0.0 collective-permute-done
  39.1 6.8 %all-gather = s32[64,128]{1,0:T(8,128)S(1)} all-gather(s32[16,128]{1,0:T(8,128)S(1)} %pad_add_fusion.2), channel_id=2, replica_groups=mesh['z'=16,'y'=4,'h'=2,'l'=2,'c'=2] {'l','c'}, dimensions={0}, use_global_device_ids=true | all-gather | bytes 40960 | tf_op jit(solution)/shard_map/all_gather | solution.py:285
  45.9 0.1 slice_reduce_fusion
  46.0 0.1 reshape.62
  46.2 0.0 copy-start
  46.2 2.2 copy-done
  48.3 5.3 %shard_map.120 = (f32[2,400,512]{2,1,0:T(8,128)S(1)}, f32[2,256,1]{2,1,0:T(8,128)S(1)}) custom-call(s32[1]{0:T(128)} %bitcast.q_ref, s32[2,1,512]{2,1,0:T(1,128)S(1)} %pad_add_fusion.6.ids_ref, s32[2,1,1024]{2,1,0:T(1,128)S(1)} %pad_add_fusion.5.neg_ref, f32[400,2560]{1,0:T(8,128)S(1)} %bitcast.39), custom_call_target="tpu_custom_call" | custom-call | flops 4194304000 | bytes 8388608 | tf_op jit(solution)/shard_map/pallas_call | solution.py:93
  53.7 0.0 collective-permute-done.2
  53.7 17.2 %all-gather.1 = f32[1600,128]{1,0:T(8,128)S(1)} all-gather(f32[400,128]{1,0:T(8,128)S(1)} %collective-permute-done.2), channel_id=3, replica_groups=mesh['z'=16,'y'=4,'h'=2,'l'=2,'c'=2] {'l','c'}, dimensions={0}, use_global_device_ids=true | all-gather | bytes 1024000 | tf_op jit(solution)/shard_map/all_gather | solution.py:301
  70.9 0.0 collective-permute-done.3
  70.9 8.9 %all-gather.2 = f32[1600,128]{1,0:T(8,128)S(1)} all-gather(f32[400,128]{1,0:T(8,128)S(1)} %collective-permute-done.3), channel_id=4, replica_groups=mesh['z'=16,'y'=4,'h'=2,'l'=2,'c'=2] {'l','c'}, dimensions={0}, use_global_device_ids=true | all-gather | bytes 1024000 | tf_op jit(solution)/shard_map/all_gather | solution.py:302
  79.8 0.0 copy-done.2
  79.8 3.0 shard_map.121
  82.8 14.1 %all_to_all.30.parts_ref = f32[4,400,128]{2,1,0:T(8,128)S(1)} all-to-all(f32[4,400,128]{2,1,0:T(8,128)S(1)} %get-tuple-element.26), channel_id=1, replica_groups=mesh['z'=16,'y'=4,'h'=2,'l'=2,'c'=2] {'l','c'}, dimensions={0} | all-to-all | bytes 1638400 | tf_op jit(solution)/shard_map/all_to_all | solution.py:304
  96.9 0.1 shard_map.122
  97.0 1.9 collective-permute-start.4
  98.9 14.7 %collective-permute-done.4 = f32[400,128]{1,0:T(8,128)S(1)} collective-permute-done((f32[400,128]{1,0:T(8,128)S(1)}, f32[400,128]{1,0:T(8,128)S(1)}, u32[]{:S(2)}, u32[]{:S(2)}) %collective-permute-start.4) | collective-permute-done | bytes 204832 | tf_op jit(solution)/shard_map/ppermute | solution.py:33
  113.6 19.6 %all-gather.3 = f32[1600,128]{1,0:T(8,128)S(1)} all-gather(f32[400,128]{1,0:T(8,128)S(1)} %collective-permute-done.4), channel_id=5, replica_groups=mesh['z'=16,'y'=4,'h'=2,'l'=2,'c'=2] {'l','c'}, dimensions={0}, use_global_device_ids=true | all-gather | bytes 1024000 | tf_op jit(solution)/shard_map/all_gather | solution.py:306
  133.2 0.0 copy-done.3
  133.2 0.5 shard_map.123
  133.8 3.5 %collective-permute-start.5 = (f32[400,128]{1,0:T(8,128)S(1)}, f32[400,128]{1,0:T(8,128)S(1)}, u32[]{:S(2)}, u32[]{:S(2)}) collective-permute-start(f32[400,128]{1,0:T(8,128)S(1)} %get-tuple-element.47), channel_id=1, source_target_pairs={{0,4},{4,0},{1,5},{5,1},{2,6},{6,2},{3,7},{7,3},{8,12},{12,8},{9,1... | collective-permute-start | bytes 614408 | tf_op jit(solution)/shard_map/ppermute | solution.py:33
  137.3 3.3 %collective-permute-start.6 = (f32[400,128]{1,0:T(8,128)S(1)}, f32[400,128]{1,0:T(8,128)S(1)}, u32[]{:S(2)}, u32[]{:S(2)}) collective-permute-start(f32[400,128]{1,0:T(8,128)S(1)} %get-tuple-element.46), channel_id=1, source_target_pairs={{0,4},{4,0},{1,5},{5,1},{2,6},{6,2},{3,7},{7,3},{8,12},{12,8},{9,1... | collective-permute-start | bytes 614408 | tf_op jit(solution)/shard_map/ppermute | solution.py:33
  140.6 3.1 collective-permute-done.5
  143.7 10.3 %all-gather.4 = f32[1600,128]{1,0:T(8,128)S(1)} all-gather(f32[400,128]{1,0:T(8,128)S(1)} %collective-permute-done.5), channel_id=6, replica_groups=mesh['z'=16,'y'=4,'h'=2,'l'=2,'c'=2] {'l','c'}, dimensions={0}, use_global_device_ids=true | all-gather | bytes 1024000 | tf_op jit(solution)/shard_map/all_gather | solution.py:301
  154.0 0.0 collective-permute-done.6
  154.0 8.9 %all-gather.5 = f32[1600,128]{1,0:T(8,128)S(1)} all-gather(f32[400,128]{1,0:T(8,128)S(1)} %collective-permute-done.6), channel_id=7, replica_groups=mesh['z'=16,'y'=4,'h'=2,'l'=2,'c'=2] {'l','c'}, dimensions={0}, use_global_device_ids=true | all-gather | bytes 1024000 | tf_op jit(solution)/shard_map/all_gather | solution.py:302
  162.9 3.8 %shard_map.124 = (f32[4,400,128]{2,1,0:T(8,128)}, f32[400,256]{1,0:T(8,128)S(1)}, f32[400,128]{1,0:T(8,128)S(1)}, f32[400,128]{1,0:T(8,128)S(1)}) custom-call(s32[1]{0:T(128)} %bitcast.q_ref, s32[4,512]{1,0:T(4,128)S(1)} %pad_add_fusion.3.ids_ref, f32[4,400,128]{2,1,0:T(8,128)S(1)} %bitcast.47, f32[4,400,128]{2,1,0:T(8,128)S(1)} %bitcast.49, ...), custom_call_target="tpu_custom_call" | custom-call | flops 2147483648 | bytes 8388608 | tf_op jit(solution)/shard_map/pallas_call | solution.py:145
  166.7 3.6 %all-to-all-start.1 = ((f32[4,400,128]{2,1,0:T(8,128)}), f32[4,400,128]{2,1,0:T(8,128)S(1)}, u32[]{:S(2)}, u32[]{:S(2)}) async-start(f32[4,400,128]{2,1,0:T(8,128)} %get-tuple-element.32), calls=%async_computation.1 | async-start | bytes 1638400 | tf_op jit(solution)/shard_map/all_to_all | solution.py:304
  170.3 17.1 %all-gather.8 = f32[1600,128]{1,0:T(8,128)S(1)} all-gather(f32[400,128]{1,0:T(8,128)S(1)} %get-tuple-element.41), channel_id=10, replica_groups=mesh['z'=16,'y'=4,'h'=2,'l'=2,'c'=2] {'l','c'}, dimensions={0}, use_global_device_ids=true | all-gather | bytes 1024000 | tf_op jit(solution)/shard_map/all_gather | solution.py:308
  187.4 0.9 shard_map.127.refs_0_
  188.3 0.0 all-to-all-done.1.parts_ref
  188.3 0.1 shard_map.125
  188.4 9.1 %all-gather.7 = f32[1600,128]{1,0:T(8,128)S(1)} all-gather(f32[400,128]{1,0:T(8,128)S(1)} %get-tuple-element.40), channel_id=9, replica_groups=mesh['z'=16,'y'=4,'h'=2,'l'=2,'c'=2] {'l','c'}, dimensions={0}, use_global_device_ids=true | all-gather | bytes 1024000 | tf_op jit(solution)/shard_map/all_gather | solution.py:308
  197.5 0.9 shard_map.128
  198.4 0.0 copy-start.4
  198.4 22.7 %all_to_all.31 = f32[8,256,128]{2,1,0:T(8,128)S(1)} all-to-all(f32[8,256,128]{2,1,0:T(8,128)S(1)} %bitcast.35), channel_id=1, replica_groups=mesh['z'=16,'y'=4,'h'=2,'l'=2,'c'=2] {'y','h'}, dimensions={0} | all-to-all | bytes 2097152 | tf_op jit(solution)/shard_map/all_to_all | solution.py:309
  221.1 0.1 reduce_sum.18
  221.2 20.2 %all_to_all.32 = f32[16,16,128]{2,1,0:T(8,128)S(1)} all-to-all(f32[16,16,128]{2,1,0:T(8,128)S(1)} %bitcast.53), channel_id=1, replica_groups=mesh['z'=16,'y'=4,'h'=2,'l'=2,'c'=2] {'z'}, dimensions={0} | all-to-all | bytes 262144 | tf_op jit(solution)/shard_map/all_to_all | solution.py:311
  241.4 0.0 copy-start.1
  241.5 17.5 %all_to_all.33 = f32[16,16,128]{2,1,0:T(8,128)S(1)} all-to-all(f32[16,16,128]{2,1,0:T(8,128)S(1)} %broadcast_in_dim.33), channel_id=1, replica_groups=mesh['z'=16,'y'=4,'h'=2,'l'=2,'c'=2] {'z'}, dimensions={0} | all-to-all | bytes 262144 | tf_op jit(solution)/shard_map/all_to_all | solution.py:313
  259.0 0.1 broadcast_in_dim.35
  259.1 15.6 %all_to_all.34 = f32[8,256,128]{2,1,0:T(8,128)S(1)} all-to-all(f32[8,256,128]{2,1,0:T(8,128)S(1)} %broadcast_in_dim.35), channel_id=1, replica_groups=mesh['z'=16,'y'=4,'h'=2,'l'=2,'c'=2] {'y','h'}, dimensions={0} | all-to-all | bytes 2097152 | tf_op jit(solution)/shard_map/all_to_all | solution.py:314
  274.7 1.9 collective-permute-start.9
  276.6 7.2 %collective-permute-start.8 = (f32[2048,128]{1,0:T(8,128)S(1)}, f32[2048,128]{1,0:T(8,128)S(1)}, u32[]{:S(2)}, u32[]{:S(2)}) collective-permute-start(f32[2048,128]{1,0:T(8,128)S(1)} %bitcast.37), channel_id=1, source_target_pairs={{0,1},{1,0},{2,3},{3,2},{4,5},{5,4},{6,7},{7,6},{8,9},{9,8},{10,11... | collective-permute-start | bytes 3145736 | tf_op jit(solution)/shard_map/ppermute | solution.py:33
  283.8 12.1 %collective-permute-done.9.refs_2_ = f32[2048,128]{1,0:T(8,128)S(1)} collective-permute-done((f32[2048,128]{1,0:T(8,128)S(1)}, f32[2048,128]{1,0:T(8,128)S(1)}, u32[]{:S(2)}, u32[]{:S(2)}) %collective-permute-start.9) | collective-permute-done | bytes 1048608 | tf_op jit(solution)/shard_map/ppermute | solution.py:33
  295.9 8.1 %collective-permute-start.10 = (f32[2048,128]{1,0:T(8,128)S(1)}, f32[2048,128]{1,0:T(8,128)S(1)}, u32[]{:S(2)}, u32[]{:S(2)}) collective-permute-start(f32[2048,128]{1,0:T(8,128)S(1)} %collective-permute-done.9.refs_2_), channel_id=1, source_target_pairs={{0,1},{1,0},{2,3},{3,2},{4,5},{5,4},{6,7},{7,6},{8,9},{9,8},{10,11... | collective-permute-start | bytes 3145736 | tf_op jit(solution)/shard_map/ppermute | solution.py:33
  304.0 2.5 collective-permute-start.7
  306.6 7.5 %collective-permute-done.7 = f32[400,128]{1,0:T(8,128)S(1)} collective-permute-done((f32[400,128]{1,0:T(8,128)S(1)}, f32[400,128]{1,0:T(8,128)S(1)}, u32[]{:S(2)}, u32[]{:S(2)}) %collective-permute-start.7) | collective-permute-done | bytes 204832 | tf_op jit(solution)/shard_map/ppermute | solution.py:33
  314.1 8.9 %all-gather.6 = f32[1600,128]{1,0:T(8,128)S(1)} all-gather(f32[400,128]{1,0:T(8,128)S(1)} %collective-permute-done.7), channel_id=8, replica_groups=mesh['z'=16,'y'=4,'h'=2,'l'=2,'c'=2] {'l','c'}, dimensions={0}, use_global_device_ids=true | all-gather | bytes 1024000 | tf_op jit(solution)/shard_map/all_gather | solution.py:306
  323.0 1.3 shard_map.126
  324.3 0.0 collective-permute-done.8.refs_1_
  324.3 0.0 collective-permute-done.10.refs_3_
  324.3 3.0 shard_map.129
  327.3 0.6 reduce.2
  (31 shorter events, 0.2 us)
Async XLA Ops:
  2.9 36.2 %collective-permute-start.1 = (s32[14,128]{1,0:T(8,128)S(1)}, s32[14,128]{1,0:T(8,128)S(1)}, u32[]{:S(2)}, u32[]{:S(2)}) collective-permute-start(s32[14,128]{1,0:T(8,128)S(1)} %pad_add_fusion.1), channel_id=1, source_target_pairs={{0,4},{4,0},{1,5},{5,1},{2,6},{6,2},{3,7},{7,3},{8,12},{12,8},{9,1... | collective-permute-start | bytes 21512 | tf_op jit(solution)/shard_map/ppermute | solution.py:33
  8.4 30.7 %collective-permute-start = (s32[14,128]{1,0:T(8,128)S(1)}, s32[14,128]{1,0:T(8,128)S(1)}, u32[]{:S(2)}, u32[]{:S(2)}) collective-permute-start(s32[14,128]{1,0:T(8,128)S(1)} %pad_add_fusion), channel_id=1, source_target_pairs={{0,256},{32,288},{64,320},{96,352},{128,384},{160,416},{192,448},{... | collective-permute-start | bytes 21512 | tf_op jit(solution)/shard_map/ppermute | solution.py:33
  24.9 46.0 %collective-permute-start.3 = (f32[400,128]{1,0:T(8,128)S(1)}, f32[400,128]{1,0:T(8,128)S(1)}, u32[]{:S(2)}, u32[]{:S(2)}) collective-permute-start(f32[400,128]{1,0:T(8,128)S(1)} %get-tuple-element.48), channel_id=1, source_target_pairs={{0,256},{32,288},{64,320},{96,352},{128,384},{160,416},{192,448},{... | collective-permute-start | bytes 614408 | tf_op jit(solution)/shard_map/ppermute | solution.py:33
  26.9 26.9 %collective-permute-start.2 = (f32[400,128]{1,0:T(8,128)S(1)}, f32[400,128]{1,0:T(8,128)S(1)}, u32[]{:S(2)}, u32[]{:S(2)}) collective-permute-start(f32[400,128]{1,0:T(8,128)S(1)} %get-tuple-element.49), channel_id=1, source_target_pairs={{0,256},{32,288},{64,320},{96,352},{128,384},{160,416},{192,448},{... | collective-permute-start | bytes 614408 | tf_op jit(solution)/shard_map/ppermute | solution.py:33
  46.2 2.2 copy-start
  48.3 31.5 %copy-start.2 = (f32[256,400]{0,1:T(8,128)S(1)}, f32[256,400]{0,1:T(8,128)}, u32[]{:S(2)}) copy-start(f32[256,400]{0,1:T(8,128)} %param.9) | copy-start | bytes 1228804
  79.8 53.4 %copy-start.3 = (f32[256]{0:T(256)S(1)}, f32[256]{0:T(256)}, u32[]{:S(2)}) copy-start(f32[256]{0:T(256)} %param.10) | copy-start | bytes 3076
  97.0 16.7 %collective-permute-start.4 = (f32[400,128]{1,0:T(8,128)S(1)}, f32[400,128]{1,0:T(8,128)S(1)}, u32[]{:S(2)}, u32[]{:S(2)}) collective-permute-start(f32[400,128]{1,0:T(8,128)S(1)} %get-tuple-element.29), channel_id=1, source_target_pairs={{0,256},{32,288},{64,320},{96,352},{128,384},{160,416},{192,448},{... | collective-permute-start | bytes 614408 | tf_op jit(solution)/shard_map/ppermute | solution.py:33
  133.8 9.9 %collective-permute-start.5 = (f32[400,128]{1,0:T(8,128)S(1)}, f32[400,128]{1,0:T(8,128)S(1)}, u32[]{:S(2)}, u32[]{:S(2)}) collective-permute-start(f32[400,128]{1,0:T(8,128)S(1)} %get-tuple-element.47), channel_id=1, source_target_pairs={{0,4},{4,0},{1,5},{5,1},{2,6},{6,2},{3,7},{7,3},{8,12},{12,8},{9,1... | collective-permute-start | bytes 614408 | tf_op jit(solution)/shard_map/ppermute | solution.py:33
  137.3 16.7 %collective-permute-start.6 = (f32[400,128]{1,0:T(8,128)S(1)}, f32[400,128]{1,0:T(8,128)S(1)}, u32[]{:S(2)}, u32[]{:S(2)}) collective-permute-start(f32[400,128]{1,0:T(8,128)S(1)} %get-tuple-element.46), channel_id=1, source_target_pairs={{0,4},{4,0},{1,5},{5,1},{2,6},{6,2},{3,7},{7,3},{8,12},{12,8},{9,1... | collective-permute-start | bytes 614408 | tf_op jit(solution)/shard_map/ppermute | solution.py:33
  166.7 21.6 %all-to-all-start.1 = ((f32[4,400,128]{2,1,0:T(8,128)}), f32[4,400,128]{2,1,0:T(8,128)S(1)}, u32[]{:S(2)}, u32[]{:S(2)}) async-start(f32[4,400,128]{2,1,0:T(8,128)} %get-tuple-element.32), calls=%async_computation.1 | async-start | bytes 1638400 | tf_op jit(solution)/shard_map/all_to_all | solution.py:304
  198.4 108.2 %copy-start.4 = (f32[2560]{0:T(1024)S(1)}, f32[2560]{0:T(1024)}, u32[]{:S(2)}) copy-start(f32[2560]{0:T(1024)} %param.12) | copy-start | bytes 30724
  241.4 82.8 %copy-start.1 = (f32[2560,400]{0,1:T(8,128)S(1)}, f32[2560,400]{0,1:T(8,128)}, u32[]{:S(2)}) copy-start(f32[2560,400]{0,1:T(8,128)} %param.11) | copy-start | bytes 12288004
  274.7 21.2 %collective-permute-start.9 = (f32[2048,128]{1,0:T(8,128)S(1)}, f32[2048,128]{1,0:T(8,128)S(1)}, u32[]{:S(2)}, u32[]{:S(2)}) collective-permute-start(f32[2048,128]{1,0:T(8,128)S(1)} %bitcast.36), channel_id=1, source_target_pairs={{0,2},{2,0},{1,3},{3,1},{4,6},{6,4},{5,7},{7,5},{8,10},{10,8},{9,1... | collective-permute-start | bytes 3145736 | tf_op jit(solution)/shard_map/ppermute | solution.py:33
  276.6 47.7 %collective-permute-start.8 = (f32[2048,128]{1,0:T(8,128)S(1)}, f32[2048,128]{1,0:T(8,128)S(1)}, u32[]{:S(2)}, u32[]{:S(2)}) collective-permute-start(f32[2048,128]{1,0:T(8,128)S(1)} %bitcast.37), channel_id=1, source_target_pairs={{0,1},{1,0},{2,3},{3,2},{4,5},{5,4},{6,7},{7,6},{8,9},{9,8},{10,11... | collective-permute-start | bytes 3145736 | tf_op jit(solution)/shard_map/ppermute | solution.py:33
  295.9 28.4 %collective-permute-start.10 = (f32[2048,128]{1,0:T(8,128)S(1)}, f32[2048,128]{1,0:T(8,128)S(1)}, u32[]{:S(2)}, u32[]{:S(2)}) collective-permute-start(f32[2048,128]{1,0:T(8,128)S(1)} %collective-permute-done.9.refs_2_), channel_id=1, source_target_pairs={{0,1},{1,0},{2,3},{3,2},{4,5},{5,4},{6,7},{7,6},{8,9},{9,8},{10,11... | collective-permute-start | bytes 3145736 | tf_op jit(solution)/shard_map/ppermute | solution.py:33
  304.0 10.1 %collective-permute-start.7 = (f32[400,128]{1,0:T(8,128)S(1)}, f32[400,128]{1,0:T(8,128)S(1)}, u32[]{:S(2)}, u32[]{:S(2)}) collective-permute-start(f32[400,128]{1,0:T(8,128)S(1)} %get-tuple-element.35), channel_id=1, source_target_pairs={{0,4},{4,0},{1,5},{5,1},{2,6},{6,2},{3,7},{7,3},{8,12},{12,8},{9,1... | collective-permute-start | bytes 614408 | tf_op jit(solution)/shard_map/ppermute | solution.py:33

commit v2 on v1

v2 whole, which is shorter than its diff:
```python
import functools

import jax
import jax.numpy as jnp
from jax import lax
from jax.experimental import pallas as pl
from jax.experimental.pallas import tpu as pltpu
from jax.sharding import Mesh, PartitionSpec as P

D = 400
HALF = 200
RELATIONS = 2560
NEG = 1024
CAP = 256
LIGHT = 64
SLOTS = 512
PAIR = 256
CHUNK = 128
ROWS = 256
QUARTER = RELATIONS // 4
PART = 512
KROWS = 2048
LETTER = D + 16
LEARN_RATE = 0.1
EPSILON = 1e-08
REL = ("l", "c")
SPREAD = ("y", "h")
F32, BF16, I32 = jnp.float32, jnp.bfloat16, jnp.int32
SMEM = pl.BlockSpec(memory_space=pltpu.SMEM)
tied = lax.optimization_barrier


def flip(block, axis, mask=1):
    count = lax.axis_size(axis)
    return lax.ppermute(block, axis, [(i, i ^ mask) for i in range(count)])


def split(value):
    high = value.astype(BF16)
    return high, (value - high.astype(F32)).astype(BF16)


def dot(first, second, over):
    return lax.dot_general(first, second, ((over[:1], over[1:]), ((), ())), preferred_element_type=F32)


def dot2(first, second, over):
    return dot(first[0], second, over) + dot(first[1], second, over)


def dot3(first, second, over):
    return dot(first[0], second[0], over) + (dot(first[0], second[1], over) + dot(first[1], second[0], over))


def places(rows, ids, base):
    return lax.broadcasted_iota(I32, (rows, ids.shape[-1]), 0) + base == ids


def hot(rows, ids, base):
    return jnp.where(places(rows, ids, base), 1.0, 0.0).astype(BF16)


def times(out_ref, at, a1, a2, w1, w2):
    out_ref[:HALF, at] = a1 * w1 - a2 * w2
    out_ref[HALF:D, at] = a1 * w2 + a2 * w1


def back(out_ref, at, u1, u2, o1, o2):
    out_ref[:HALF, at] = u1 * o1 + u2 * o2
    out_ref[HALF:D, at] = u2 * o1 - u1 * o2


def shape(*dims):
    return jax.ShapeDtypeStruct(dims, F32)


def whole(*dims):
    return pl.BlockSpec(dims, lambda *_: (0,) * len(dims))


def call(kernel, out_shape, in_specs, out_specs, scratch, flops, moved, grid=(1,), room=40, **more):
    return pl.pallas_call(
        kernel,
        out_shape=out_shape,
        grid_spec=pltpu.PrefetchScalarGridSpec(
            num_scalar_prefetch=1, grid=grid, in_specs=in_specs, out_specs=out_specs, scratch_shapes=scratch
        ),
        compiler_params=pltpu.CompilerParams(vmem_limit_bytes=room * 1024 * 1024),
        cost_estimate=pl.CostEstimate(flops=flops, bytes_accessed=moved, transcendentals=0),
        **more,
    )


def lookup_kernel(s_ref, ids_ref, table_ref, out_ref):
    step = pl.program_id(0)
    table = split(table_ref[...])
    for k in range(ids_ref.shape[0]):
        found = dot2(table, hot(PART, ids_ref[k], PART * step), (1, 0))

        @pl.when(step == 0)
        def _():
            out_ref[k] = found

        @pl.when(step > 0)
        def _():
            out_ref[k] += found


def lookup(s, ids, table):
    lists, _, width = ids.shape
    return call(
        lookup_kernel,
        shape(lists, D, width),
        [whole(lists, 1, width), pl.BlockSpec((D, PART), lambda i, s: (0, i))],
        whole(lists, D, width),
        [],
        4 * D * RELATIONS * lists * width,
        5 * 1024 * 1024,
        grid=(RELATIONS // PART,),
        room=56,
    )(s, ids, table)


def chunk_rows(q, ids, near_ref, far_ref):
    first = q & 2
    total = jnp.zeros((D, CHUNK), F32)
    for ref, base in ((near_ref, first), (far_ref, first ^ 2)):
        for k in range(2):
            total += dot2(split(ref[k]), hot(ROWS, ids, ROWS * (base + k)), (1, 0))
    return total


def heads_kernel(s_ref, ids_ref, near_ref, far_ref, out_ref):
    out_ref[...] = chunk_rows(s_ref[0], ids_ref[...], near_ref, far_ref)


def letter_kernel(s_ref, ids_ref, near_ref, far_ref, rel_ref, target_ref, neg_ref, head_ref, out_ref):
    head_ref[...] = chunk_rows(s_ref[0], ids_ref[...], near_ref, far_ref)
    every = slice(None)
    times(out_ref, every, head_ref[:HALF, :], head_ref[HALF:, :], rel_ref[0, :HALF, :], rel_ref[0, HALF:, :])
    out_ref[D : D + 8, :] = jnp.broadcast_to(target_ref[...], (8, CHUNK)).astype(F32)
    out_ref[D + 8 :, :] = neg_ref[...].astype(F32)


HEADS_IN = [whole(1, CHUNK), whole(2, D, ROWS), whole(2, D, ROWS)]
HEADS_COST = (4 * D * 1024 * CHUNK, 2 * 1024 * 1024)


def heads(s, ids, near, far):
    return call(heads_kernel, shape(D, CHUNK), HEADS_IN, whole(D, CHUNK), [], *HEADS_COST)(s, ids, near, far)


def letter(s, ids, near, far, rel_rows, target, negatives):
    return call(
        letter_kernel,
        [shape(D, CHUNK), shape(LETTER, CHUNK)],
        HEADS_IN + [whole(1, D, CHUNK), whole(1, CHUNK), whole(8, 128)],
        [whole(D, CHUNK), whole(LETTER, CHUNK)],
        [],
        *HEADS_COST,
    )(s, ids, near, far, rel_rows, target, negatives)


def weigh(s_ref, h_ref, target, negatives, own_ref, other_ref, keep_ref, send_ref, grad_ref, grad_send_ref):
    q = s_ref[0]
    product = split(h_ref[...])
    live = jnp.where(target >= 0, 1.0 / NEG, 0.0)
    d_product = jnp.zeros((D, PAIR), F32)
    for k, (ref, out_ref) in enumerate(((own_ref, grad_ref), (other_ref, grad_send_ref))):
        base = ROWS * (q ^ (2 * k))
        hits = jnp.zeros((ROWS, 128), F32)
        for row in range(8):
            hits += jnp.where(places(ROWS, negatives[row : row + 1, :], base), 1.0, 0.0)
        rows = split(ref[...])
        scores = dot3(rows, product, (0, 0))
        small = jnp.exp(-jnp.abs(scores))
        larger = 1.0 / (1.0 + small)
        smaller = small * larger
        rising = scores >= 0
        weight = jnp.where(rising, larger, smaller) * jnp.sum(hits, axis=1, keepdims=True) * live
        weight -= jnp.where(places(ROWS, target, base), jnp.where(rising, smaller, larger), 0.0)
        weight = split(weight)
        d_product += dot3(rows, weight, (1, 0))
        out_ref[...] = dot3(product, weight, (1, 1))
    h_ref[...] = d_product
    core = q & 1
    keep_ref[...] = h_ref[:, pl.ds(pl.multiple_of(CHUNK * core, CHUNK), CHUNK)]
    send_ref[...] = h_ref[:, pl.ds(pl.multiple_of(CHUNK * (1 - core), CHUNK), CHUNK)]


def answer_kernel(s_ref, letters_ref, own_ref, other_ref, keep_ref, send_ref, grad_ref, grad_send_ref, h_ref):
    for k in range(2):
        h_ref[:, CHUNK * k : CHUNK * k + CHUNK] = letters_ref[k, :D, :]
    target = jnp.concatenate([letters_ref[k, D : D + 1, :] for k in range(2)], axis=1).astype(I32)
    negatives = letters_ref[0, D + 8 :, :].astype(I32)
    weigh(s_ref, h_ref, target, negatives, own_ref, other_ref, keep_ref, send_ref, grad_ref, grad_send_ref)


def answer(s, letters, own, other):
    return call(
        answer_kernel,
        [shape(D, CHUNK)] * 2 + [shape(D, ROWS)] * 2,
        [whole(2, LETTER, CHUNK), whole(D, ROWS), whole(D, ROWS)],
        [whole(D, CHUNK)] * 2 + [whole(D, ROWS)] * 2,
        [pltpu.VMEM((D, PAIR), F32)],
        1024 * 1024 * 1024,
        5 * 1024 * 1024,
    )(s, letters, own, other)


def score_kernel(s_ref, target_ref, neg_ref, a_ref, rel_ref, own_ref, other_ref, keep_ref, send_ref, grad_ref, grad_send_ref, head_ref, kind_ref, h_ref):
    first = s_ref[1]
    for k in range(2):
        at = slice(CHUNK * k, CHUNK * k + CHUNK)
        a1, a2 = a_ref[first + k, :HALF, :], a_ref[first + k, HALF:, :]
        times(h_ref, at, a1, a2, rel_ref[0, :HALF, at], rel_ref[0, HALF:, at])
    weigh(s_ref, h_ref, target_ref[...], neg_ref[...], own_ref, other_ref, keep_ref, send_ref, grad_ref, grad_send_ref)
    core = s_ref[0] & 1
    head_ref[...] = a_ref[first + core]
    kind_ref[...] = rel_ref[0, :, pl.ds(pl.multiple_of(CHUNK * core, CHUNK), CHUNK)]


def score(s, target, negatives, head_rows, rel_rows, own, other):
    return call(
        score_kernel,
        [shape(D, CHUNK)] * 2 + [shape(D, ROWS)] * 2 + [shape(D, CHUNK)] * 2,
        [
            whole(1, PAIR),
            whole(8, 128),
            whole(4, D, CHUNK),
            whole(1, D, PAIR),
            whole(D, ROWS),
            whole(D, ROWS),
        ],
        [whole(D, CHUNK)] * 2 + [whole(D, ROWS)] * 2 + [whole(D, CHUNK)] * 2,
        [pltpu.VMEM((D, PAIR), F32)],
        1024 * 1024 * 1024,
        5 * 1024 * 1024,
    )(s, target, negatives, head_rows, rel_rows, own, other)


def back_kernel(s_ref, keep_ref, got_ref, head_ref, kind_ref, d_head_ref, d_kind_ref):
    up = keep_ref[...] + got_ref[...]
    for other_ref, out_ref in ((kind_ref, d_head_ref), (head_ref, d_kind_ref)):
        back(out_ref, slice(None), up[:HALF, :], up[HALF:, :], other_ref[:HALF, :], other_ref[HALF:, :])


def chunk_back(s, keep, got, head, kind):
    chunk = whole(D, CHUNK)
    return call(back_kernel, [shape(D, CHUNK)] * 2, [chunk] * 4, [chunk] * 2, [], 10 * D * CHUNK, 32 * D * CHUNK)(
        s, keep, got, head, kind
    )


def step_rows(gradient, own_ref, state_ref, out_ref, out_state_ref):
    state = state_ref[...] + jnp.sum(gradient * gradient, axis=0, keepdims=True) * (1.0 / D)
    out_state_ref[...] = state
    out_ref[...] = own_ref[...] - gradient * (LEARN_RATE / (jnp.sqrt(state) + EPSILON))


def chunk_at(k):
    return slice(CHUNK * k, CHUNK * k + CHUNK)


def answered_kernel(s_ref, ids_ref, answers_ref, rel_ref, grad_ref, got_ref, own_ref, state_ref, out_ref, out_state_ref, high_ref, low_ref, d_ref):
    for k in range(4):
        at = chunk_at(k % 2)
        w1, w2 = rel_ref[k // 2, :HALF, at], rel_ref[k // 2, HALF:, at]
        back(d_ref, slice(None), answers_ref[k, :HALF, :], answers_ref[k, HALF:, :], w1, w2)
        high_ref[:, chunk_at(k)], low_ref[:, chunk_at(k)] = split(d_ref[...])
    spots = hot(ROWS, ids_ref[...], ROWS * s_ref[0])
    gradient = grad_ref[...] + got_ref[...] + dot2((high_ref[...], low_ref[...]), spots, (1, 1))
    step_rows(gradient, own_ref, state_ref, out_ref, out_state_ref)


ROWS_SPECS = [whole(D, ROWS), whole(1, ROWS)]
PARTS = [pltpu.VMEM((D, SLOTS), BF16)] * 2


def update_answered(s, ids, answers, rel_rows, grad, got, own, state):
    return call(
        answered_kernel,
        [shape(D, ROWS), shape(1, ROWS)],
        [whole(1, SLOTS), whole(4, D, CHUNK), whole(2, D, PAIR), whole(D, ROWS), whole(D, ROWS)] + ROWS_SPECS,
        ROWS_SPECS,
        PARTS + [pltpu.VMEM((D, CHUNK), F32)],
        4 * D * SLOTS * ROWS,
        4 * 1024 * 1024,
    )(s, ids, answers, rel_rows, grad, got, own, state)


def join_kernel(s_ref, ids_ref, parts_ref, grad_ref, send_ref, out_ref, out_send_ref):
    parts = [split(parts_ref[k]) for k in range(2)]
    for flipped, ref, to_ref in ((0, grad_ref, out_ref), (2, send_ref, out_send_ref)):
        base = ROWS * (s_ref[0] ^ flipped)
        total = ref[...]
        for k in range(2):
            total += dot2(parts[k], hot(ROWS, ids_ref[:, chunk_at(k)], base), (1, 1))
        to_ref[...] = total


def join(s, ids, parts, grad, grad_send):
    return call(
        join_kernel,
        [shape(D, ROWS)] * 2,
        [whole(1, PAIR), whole(2, D, CHUNK), whole(D, ROWS), whole(D, ROWS)],
        [whole(D, ROWS)] * 2,
        [],
        4 * D * PAIR * 2 * ROWS,
        3 * 1024 * 1024,
    )(s, ids, parts, grad, grad_send)


def update_kernel(s_ref, grad_ref, got_ref, own_ref, state_ref, out_ref, out_state_ref):
    step_rows(grad_ref[...] + got_ref[...], own_ref, state_ref, out_ref, out_state_ref)


def update(s, grad, got, own, state):
    ins = [whole(D, ROWS)] * 2 + ROWS_SPECS
    return call(update_kernel, [shape(D, ROWS), shape(1, ROWS)], ins, ROWS_SPECS, [], 8 * D * ROWS, 16 * D * ROWS)(
        s, grad, got, own, state
    )


def count_in(s_ref, ids_ref, before_ref, out_ref, high_ref, low_ref):
    spots = hot(QUARTER, ids_ref[...], QUARTER * s_ref[0])
    total = dot2((high_ref[...], low_ref[...]), spots, (1, 1))
    for k in range(5):
        at = slice(D * k, D * k + D)
        tile = total[:, 128 * k : 128 * k + 128]
        out_ref[at, :] = tile if before_ref is None else before_ref[at, :] + tile
    out_ref[5 * D :, :] = jnp.zeros((KROWS - 5 * D, 128), F32)


def kinds_answered_kernel(s_ref, ids_ref, answers_ref, heads_ref, out_ref, high_ref, low_ref, d_ref):
    for k in range(4):
        a1, a2 = heads_ref[k, :HALF, :], heads_ref[k, HALF:, :]
        back(d_ref, slice(None), answers_ref[k, :HALF, :], answers_ref[k, HALF:, :], a1, a2)
        high_ref[:, chunk_at(k)], low_ref[:, chunk_at(k)] = split(d_ref[...])
    count_in(s_ref, ids_ref, None, out_ref, high_ref, low_ref)


def kinds_kernel(s_ref, ids_ref, parts_ref, before_ref, out_ref, high_ref, low_ref):
    for k in range(4):
        high_ref[:, chunk_at(k)], low_ref[:, chunk_at(k)] = split(parts_ref[k])
    count_in(s_ref, ids_ref, before_ref, out_ref, high_ref, low_ref)


KINDS_COST = (4 * D * SLOTS * QUARTER, 3 * 1024 * 1024)


def kinds_answered(s, ids, answers, heads):
    ins = [whole(1, SLOTS)] + [whole(4, D, CHUNK)] * 2
    scratch = PARTS + [pltpu.VMEM((D, CHUNK), F32)]
    return call(kinds_answered_kernel, shape(KROWS, 128), ins, whole(KROWS, 128), scratch, *KINDS_COST)(
        s, ids, answers, heads
    )


def kinds(s, ids, parts, before):
    ins = [whole(1, SLOTS), whole(4, D, CHUNK), whole(KROWS, 128)]
    return call(kinds_kernel, shape(KROWS, 128), ins, whole(KROWS, 128), PARTS, *KINDS_COST)(s, ids, parts, before)


def relations_kernel(core_ref, grad_ref, table_ref, state_ref, *refs):
    out_ref, out_state_ref = refs[-2:]
    for k in range(5):
        at = slice(128 * k, 128 * k + 128)
        gradient = grad_ref[0, D * k : D * k + D, :]
        state = state_ref[:, at] + jnp.sum(gradient * gradient, axis=0, keepdims=True) * (1.0 / D)
        out_state_ref[:, at] = state
        out_ref[:, at] = table_ref[:, at] - gradient * (LEARN_RATE / (jnp.sqrt(state) + EPSILON))


def update_relations(core, grads, table, state, before):
    mine = lambda l, core: (0, 2 * l + core[0])
    blocks = [pl.BlockSpec((D, QUARTER), mine), pl.BlockSpec((1, QUARTER), mine)]
    return call(
        relations_kernel,
        [shape(D, RELATIONS), shape(1, RELATIONS)],
        [pl.BlockSpec((1, KROWS, 128), lambda l, core: (l, 0, 0))] + blocks + [pl.BlockSpec(memory_space=pl.ANY)] * len(before),
        blocks,
        [],
        5 * D * RELATIONS,
        6 * 1024 * 1024,
        grid=(2,),
        room=56,
        input_output_aliases={4: 0, 5: 1} if before else {},
    )(core, grads, table, state, *before)


def slot_lists(src_rows, rel_ids, dst_rows, live_count):
    live = jnp.arange(CAP, dtype=I32)[None, :] < live_count[0]
    lists = jnp.where(live[:, None, :], jnp.stack([src_rows[0], rel_ids[0], dst_rows[0]], axis=1), -1)
    every = lax.all_gather(lists.reshape(12, 128), REL, axis=0).reshape(4, 6, CAP)
    light = jnp.moveaxis(every[:, :, :LIGHT], 0, 1).reshape(6, 4 * LIGHT)
    heavy = jnp.max(every[:, :, LIGHT:], axis=0)
    empty = jnp.full((6, SLOTS - 4 * LIGHT - (CAP - LIGHT)), -1, I32)
    return jnp.concatenate([light, heavy, empty], axis=1)


def local(entities, entity_state, relations, relation_state, src_rows, rel_ids, dst_rows, live_count, neg_rows):
    place = lax.axis_index(REL).astype(I32)
    core, chip, side = place & 1, place // 2, lax.axis_index("h").astype(I32)
    s = place.reshape(1)
    own, state = entities.T, entity_state.reshape(1, ROWS)
    table = relations.T
    pick = lambda lists, rows, at: lax.dynamic_slice_in_dim(lists.reshape(rows, -1), at, 1, 0)

    slots = slot_lists(src_rows, rel_ids, dst_rows, live_count)
    own, slots = tied((own, slots))
    other = flip(own, "l")
    near = lax.all_gather(own, "c", axis=0)
    chunk_ids, chunk_kinds, chunk_targets = [pick(slots[k], 4, place) for k in range(3)]
    chunk_rel = lookup(s, chunk_kinds[None], table)
    far = lax.all_gather(other, "c", axis=0)
    head, mail = letter(s, chunk_ids, near, far, chunk_rel, chunk_targets, neg_rows[0, 0].reshape(8, 128))
    mail, head, bucket_kinds = tied((mail, head, slots[1]))
    rel_rows = lookup(s, bucket_kinds.reshape(2, 1, PAIR), table)
    mail, head_rows, rel_rows = tied((flip(mail, "z", 8), lax.all_gather(head, REL, axis=0), rel_rows))
    keep, send, grad, grad_send = answer(s, lax.all_gather(mail, "c", axis=0), own, other)
    reply = keep + flip(send, "c")
    sent = jnp.concatenate([slots[4:6].reshape(8, 128), neg_rows[0, 1].reshape(8, 128)], axis=0)
    reply, sent = tied((reply, sent))
    got = flip(sent, "h")
    kind_ids, target_ids, negatives = got[:4].reshape(1, SLOTS), got[4:8], got[8:]
    later_rows = lookup(s, pick(kind_ids, 2, chip)[None], table)
    reply, grad_got, later_rows = tied((flip(reply, "z", 8), flip(grad_send, "l"), later_rows))
    answers = lax.all_gather(reply, REL, axis=0)
    own, state = update_answered(s, slots[0:1], answers, rel_rows, grad, grad_got, own, state)
    total = kinds_answered(s, slots[1:2], answers, head_rows)

    other = flip(own, "l")
    near = lax.all_gather(own, "c", axis=0)
    other, total = tied((other, total))
    chunk = heads(s, pick(slots[3], 4, place), near, lax.all_gather(other, "c", axis=0))
    head_rows = lax.all_gather(chunk, ("h", "c"), axis=0)
    beyond = jnp.stack([place, 2 * (1 - side)])
    keep, send, grad, grad_send, head, kind = score(beyond, pick(target_ids, 2, chip), negatives, head_rows, later_rows, own, other)
    d_head, d_kind = chunk_back(s, keep, flip(send, "c"), head, kind)
    d_kinds, d_head = tied((lax.all_gather(d_kind, REL, axis=0), flip(d_head, "h")))
    total = kinds(s, kind_ids, d_kinds, total)

    shares = lax.all_to_all(total.reshape(8, 256, 128), SPREAD, 0, 0)
    pieces = lax.all_to_all(jnp.sum(shares, axis=0).reshape(16, 16, 128), "z", 0, 0)
    grad, grad_send = join(s, pick(slots[3], 2, chip), lax.all_gather(d_head, "c", axis=0), grad, grad_send)
    pieces, grad, grad_send = tied((pieces, grad, grad_send))
    piece = jnp.sum(pieces, axis=0)
    share = lax.all_to_all(jnp.broadcast_to(piece[None], (16, 16, 128)), "z", 0, 0).reshape(256, 128)
    share, grad_got = tied((share, flip(grad_send, "l")))
    own, state = update(s, grad, grad_got, own, state)
    half = lax.all_to_all(jnp.broadcast_to(share[None], (16, 256, 128)), ("l",) + SPREAD, 0, 0).reshape(2, KROWS, 128)
    half, own, state = tied((half, own, state))
    table_state = relation_state.reshape(1, RELATIONS)
    first = update_relations(core.reshape(1), half, table, table_state, [])
    new_table, new_table_state = update_relations((1 - core).reshape(1), flip(half, "c"), table, table_state, first)
    return own.T, state.reshape(ROWS), new_table.T, new_table_state.reshape(RELATIONS)


def solution(mesh):
    fine = Mesh(mesh.devices.reshape(16, 4, 2, 2, 2), ("z", "y", "h", "l", "c"))
    dom, rel = ("z", "y", "h"), REL
    edge = P(dom, None, rel)
    in_specs = (P(dom + rel, None), P(dom + rel), P(), P(), edge, edge, edge, edge, P(dom, None, None))
    out_specs = (P(dom + rel, None), P(dom + rel), P(), P())
    return jax.shard_map(local, mesh=fine, in_specs=in_specs, out_specs=out_specs, check_vma=False)
```

time: 329 us -> 277 us (0.84)
  blocking collectives: 197 us -> 93.2 us
  waiting for transfers between devices: 37.5 us -> 59.4 us
  Pallas kernels: 18.8 us -> 35.3 us
  starting transfers between devices: 67 us -> 74.5 us
  local copies, waits for them, and re-layouts: 4.4 us -> 9.03 us
    all_to_all x4 -> x0, blocking collectives: 67.4 us -> none  [the longest x1 20.2 us: local(): pieces = lax.all_to_all(share.reshape(16, 16, 128), 'z', 0, 0)]
    all_gather x9 -> x11, blocking collectives: 107 us -> 70.3 us  [the longest x1 12 us: local(): lax.all_gather(d_kind, REL, axis=0)]
    all_to_all x1 -> x3, waiting for transfers between devices: 0.01 us -> 33.9 us  [the longest x1 24.6 us: local(): lax.all_to_all(jnp.broadcast_to(share[None], (16, 256, 128)), ('l',) + SP...]
    all_to_all x1 -> x3, starting transfers between devices: 3.62 us -> 32.9 us  [the longest x1 23 us: local(): lax.all_to_all(jnp.sum(shares, axis=0).reshape(16, 16, 128), 'z', 0, 0)]
    ppermute x11, starting transfers between devices: 63.4 us -> 41.6 us  [flip(): return lax.ppermute(block, axis, [(i, i ^ mask) for i in range(count)])]
    pallas_call x10 -> x15, Pallas kernels: 18.8 us -> 35.3 us  [the longest x3 19.1 us: lookup(): call(lookup_kernel, shape(lists, D, width), [whole(lists, 1, width), pl.B...]
    ppermute x11, waiting for transfers between devices: 37.5 us -> 25.6 us  [flip(): return lax.ppermute(block, axis, [(i, i ^ mask) for i in range(count)])]
  transfers between devices with their start and end apart: 12 -> 14, of which waited for: 4 -> 9; matrix products, arithmetic and copies ran while one was open for 0% -> 1% of each run, Pallas kernels for 2% -> 9%
where the time goes in v2:
time: 277 us; the launch traced here: 276 us
  blocking collectives  93.2 us (34%)
  starting transfers between devices  74.5 us (27%)
  waiting for transfers between devices  59.4 us (21%)
  Pallas kernels  35.3 us (13%)
  local copies, waits for them, and re-layouts  9.03 us (3%)
  other arithmetic  3.75 us (1%)
    ppermute x11, starting transfers between devices, flip(): return lax.ppermute(block, axis, [(i, i ^ mask) for i in range(count)])  41.6 us
    ppermute x11, waiting for transfers between devices, flip(): return lax.ppermute(block, axis, [(i, i ^ mask) for i in range(count)])  25.6 us
    all_to_all x1, waiting for transfers between devices, local(): lax.all_to_all(jnp.broadcast_to(share[None], (16, 256, 128)), ('l',) + SP...  24.6 us
    all_to_all x1, blocking collectives, local(): shares = lax.all_to_all(total.reshape(8, 256, 128), SPREAD, 0, 0)  23 us
    all_to_all x1, starting transfers between devices, local(): lax.all_to_all(jnp.sum(shares, axis=0).reshape(16, 16, 128), 'z', 0, 0)  23 us
    pallas_call x3, Pallas kernels, lookup(): call(lookup_kernel, shape(lists, D, width), [whole(lists, 1, width), pl.B...  19.1 us
    all_gather x1, blocking collectives, local(): lax.all_gather(d_kind, REL, axis=0)  12 us
    all_gather x1, blocking collectives, slot_lists(): lax.all_gather(lists.reshape(12, 128), REL, axis=0).reshape(4, 6, CAP)  11.9 us
  transfers between devices with their start and end apart: 14, of which 9 were waited for; matrix products, arithmetic and copies ran while one was open for 1% of the time, Pallas kernels for 9%

profile of v2, /device:TPU:1, one launch (start us, length us, event | category | flops | bytes accessed | tf_op | source)
XLA Modules:
  0.0 276.3 jit_solution(13419713138560949423)
XLA Ops:
  0.7 0.8 iota_compare_fusion
  1.4 0.7 add_select_fusion
  2.2 11.9 %all_gather.63 = s32[4,12,128]{2,1,0:T(8,128)S(1)} all-gather(s32[1,12,128]{2,1,0:T(8,128)S(1)} %select_n.31), channel_id=1, replica_groups=mesh['z'=16,'y'=4,'h'=2,'l'=2,'c'=2] {'l','c'}, dimensions={0}, use_global_device_ids=true | all-gather | bytes 30720 | tf_op jit(solution)/shard_map/all_gather | solution.py:395
  14.2 0.1 reshape.104
  14.3 1.9 collective-permute-start
  16.3 0.5 fusion.1.ids_ref
  16.8 5.4 %shard_map.120.rel_ref = f32[1,400,128]{2,1,0:T(8,128)} custom-call(s32[1]{0:T(128)} %bitcast.s_ref, s32[1,1,128]{2,1,0:T(1,128)} %fusion.1.ids_ref, f32[400,2560]{1,0:T(8,128)} %bitcast.65), custom_call_target="tpu_custom_call" | custom-call | flops 524288000 | bytes 5242880 | tf_op jit(solution)/shard_map/pallas_call | solution.py:111
  22.2 2.4 all-gather
  24.6 2.7 collective-permute-done.other_ref
  27.3 3.0 %all-gather.1 = f32[800,256]{1,0:T(8,128)S(1)} all-gather(f32[400,256]{1,0:T(8,128)S(1)} %collective-permute-done.other_ref), channel_id=3, replica_groups=mesh['z'=16,'y'=4,'h'=2,'l'=2,'c'=2] {'c'}, dimensions={0}, use_global_device_ids=true | all-gather | bytes 1228800 | tf_op jit(solution)/shard_map/all_gather | solution.py:416
  30.3 0.9 copy-done.2
  31.2 0.6 shard_map.121
  31.9 10.1 %collective-permute-start.1 = (f32[416,128]{1,0:T(8,128)S(1)}, f32[416,128]{1,0:T(8,128)S(1)}, u32[]{:S(2)}, u32[]{:S(2)}) collective-permute-start(f32[416,128]{1,0:T(8,128)S(1)} %get-tuple-element.57), channel_id=1, source_target_pairs={{0,256},{32,288},{64,320},{96,352},{128,384},{160,416},{192,448},{... | collective-permute-start | bytes 638984 | tf_op jit(solution)/shard_map/ppermute | solution.py:35
  41.9 9.3 %all-gather.2 = f32[1600,128]{1,0:T(8,128)S(1)} all-gather(f32[400,128]{1,0:T(8,128)S(1)} %get-tuple-element.58), channel_id=4, replica_groups=mesh['z'=16,'y'=4,'h'=2,'l'=2,'c'=2] {'l','c'}, dimensions={0}, use_global_device_ids=true | all-gather | bytes 1024000 | tf_op jit(solution)/shard_map/all_gather | solution.py:420
  51.2 8.2 %shard_map.122.rel_ref = f32[2,400,256]{2,1,0:T(8,128)} custom-call(s32[1]{0:T(128)} %bitcast.s_ref, s32[2,1,256]{2,1,0:T(1,128)} %bitcast.63, f32[400,2560]{1,0:T(8,128)} %bitcast.66), custom_call_target="tpu_custom_call" | custom-call | flops 2097152000 | bytes 5242880 | tf_op jit(solution)/shard_map/pallas_call | solution.py:111
  59.4 2.1 all-gather.3
  61.5 1.9 shard_map.123
  63.4 0.7 copy-done.3
  64.1 0.8 copy-done.11
  64.9 2.2 collective-permute-start.2
  67.1 1.2 collective-permute-done.2
  68.4 4.4 %collective-permute-start.3 = (s32[16,128]{1,0:T(8,128)S(1)}, s32[16,128]{1,0:T(8,128)S(1)}, u32[]{:S(2)}, u32[]{:S(2)}) collective-permute-start(s32[16,128]{1,0:T(8,128)S(1)} %pad_add_fusion), channel_id=1, source_target_pairs={{0,4},{4,0},{1,5},{5,1},{2,6},{6,2},{3,7},{7,3},{8,12},{12,8},{9,1... | collective-permute-start | bytes 24584 | tf_op jit(solution)/shard_map/ppermute | solution.py:35
  72.8 2.1 collective-permute-start.5
  75.0 6.1 %collective-permute-start.4 = (f32[400,128]{1,0:T(8,128)S(1)}, f32[400,128]{1,0:T(8,128)S(1)}, u32[]{:S(2)}, u32[]{:S(2)}) collective-permute-start(f32[400,128]{1,0:T(8,128)S(1)} %add.20), channel_id=1, source_target_pairs={{0,256},{32,288},{64,320},{96,352},{128,384},{160,416},{192,448},{... | collective-permute-start | bytes 614408 | tf_op jit(solution)/shard_map/ppermute | solution.py:35
  81.2 0.6 fusion.ids_ref
  81.7 5.5 %shard_map.124.rel_ref = f32[1,400,256]{2,1,0:T(8,128)} custom-call(s32[1]{0:T(128)} %bitcast.s_ref, s32[1,1,256]{2,1,0:T(1,128)} %fusion.ids_ref, f32[400,2560]{1,0:T(8,128)} %bitcast.67), custom_call_target="tpu_custom_call" | custom-call | flops 1048576000 | bytes 5242880 | tf_op jit(solution)/shard_map/pallas_call | solution.py:111
  87.3 4.3 %collective-permute-done.4 = f32[400,128]{1,0:T(8,128)S(1)} collective-permute-done((f32[400,128]{1,0:T(8,128)S(1)}, f32[400,128]{1,0:T(8,128)S(1)}, u32[]{:S(2)}, u32[]{:S(2)}) %collective-permute-start.4) | collective-permute-done | bytes 204832 | tf_op jit(solution)/shard_map/ppermute | solution.py:35
  91.5 10.5 %all-gather.4 = f32[1600,128]{1,0:T(8,128)S(1)} all-gather(f32[400,128]{1,0:T(8,128)S(1)} %collective-permute-done.4), channel_id=6, replica_groups=mesh['z'=16,'y'=4,'h'=2,'l'=2,'c'=2] {'l','c'}, dimensions={0}, use_global_device_ids=true | all-gather | bytes 1024000 | tf_op jit(solution)/shard_map/all_gather | solution.py:429
  102.1 1.0 copy-done.6
  103.1 0.6 shard_map.125
  103.7 2.3 collective-permute-start.6
  106.0 1.0 shard_map.126.before_ref
  107.0 2.5 all-gather.5
  109.4 7.2 %collective-permute-done.6.other_ref = f32[400,256]{1,0:T(8,128)S(1)} collective-permute-done((f32[400,256]{1,0:T(8,128)S(1)}, f32[400,256]{1,0:T(8,128)S(1)}, u32[]{:S(2)}, u32[]{:S(2)}) %collective-permute-start.6) | collective-permute-done | bytes 409632 | tf_op jit(solution)/shard_map/ppermute | solution.py:35
  116.6 3.0 %all-gather.6 = f32[800,256]{1,0:T(8,128)S(1)} all-gather(f32[400,256]{1,0:T(8,128)S(1)} %collective-permute-done.6.other_ref), channel_id=8, replica_groups=mesh['z'=16,'y'=4,'h'=2,'l'=2,'c'=2] {'c'}, dimensions={0}, use_global_device_ids=true | all-gather | bytes 1228800 | tf_op jit(solution)/shard_map/all_gather | solution.py:436
  119.6 0.6 shard_map.127
  120.2 10.4 %all-gather.7 = f32[1600,128]{1,0:T(8,128)S(1)} all-gather(f32[400,128]{1,0:T(8,128)S(1)} %shard_map.127), channel_id=9, replica_groups=mesh['z'=16,'y'=4,'h'=2,'l'=2,'c'=2] {'h','c'}, dimensions={0}, use_global_device_ids=true | all-gather | bytes 1024000 | tf_op jit(solution)/shard_map/all_gather | solution.py:437
  130.6 2.5 shard_map.128
  133.1 2.1 collective-permute-start.7
  135.1 1.3 collective-permute-done.7.got_ref
  136.5 2.4 collective-permute-start.8
  138.9 12.0 %all-gather.8 = f32[1600,128]{1,0:T(8,128)S(1)} all-gather(f32[400,128]{1,0:T(8,128)S(1)} %get-tuple-element.78), channel_id=10, replica_groups=mesh['z'=16,'y'=4,'h'=2,'l'=2,'c'=2] {'l','c'}, dimensions={0}, use_global_device_ids=true | all-gather | bytes 1024000 | tf_op jit(solution)/shard_map/all_gather | solution.py:441
  150.9 0.9 shard_map.130
  151.8 23.0 %all_to_all.20 = f32[8,256,128]{2,1,0:T(8,128)S(1)} all-to-all(f32[8,256,128]{2,1,0:T(8,128)S(1)} %bitcast.45), channel_id=1, replica_groups=mesh['z'=16,'y'=4,'h'=2,'l'=2,'c'=2] {'y','h'}, dimensions={0} | all-to-all | bytes 2097152 | tf_op jit(solution)/shard_map/all_to_all | solution.py:444
  174.8 0.7 reduce_sum.18
  175.5 23.0 %all-to-all-start.1 = ((f32[16,16,128]{2,1,0:T(8,128)}), f32[16,16,128]{2,1,0:T(8,128)S(1)}, u32[]{:S(2)}, u32[]{:S(2)}) async-start(f32[16,16,128]{2,1,0:T(8,128)} %bitcast.31), calls=%async_computation.1 | async-start | bytes 262144 | tf_op jit(solution)/shard_map/all_to_all | solution.py:445
  198.5 3.3 %all-gather.9 = f32[800,128]{1,0:T(8,128)S(1)} all-gather(f32[400,128]{1,0:T(8,128)S(1)} %collective-permute-done.8), channel_id=11, replica_groups=mesh['z'=16,'y'=4,'h'=2,'l'=2,'c'=2] {'c'}, dimensions={0}, use_global_device_ids=true | all-gather | bytes 614400 | tf_op jit(solution)/shard_map/all_gather | solution.py:446
  201.8 0.6 shard_map.131
  202.4 8.1 %all-to-all-done.1 = f32[16,16,128]{2,1,0:T(8,128)S(1)} async-done(((f32[16,16,128]{2,1,0:T(8,128)}), f32[16,16,128]{2,1,0:T(8,128)S(1)}, u32[]{:S(2)}, u32[]{:S(2)}) %all-to-all-start.1) | async-done | bytes 131104 | tf_op jit(solution)/shard_map/all_to_all | solution.py:445
  210.5 0.7 broadcast_in_dim.40
  211.1 5.5 %all-to-all-start.2 = ((f32[16,16,128]{2,1,0:T(8,128)}), f32[16,16,128]{2,1,0:T(8,128)S(1)}, u32[]{:S(2)}, u32[]{:S(2)}) async-start(f32[16,16,128]{2,1,0:T(8,128)} %broadcast_in_dim.40), calls=%async_computation.2 | async-start | bytes 262144 | tf_op jit(solution)/shard_map/all_to_all | solution.py:449
  216.6 1.9 collective-permute-start.9
  218.6 8.9 %collective-permute-done.9.got_ref = f32[400,256]{1,0:T(8,128)S(1)} collective-permute-done((f32[400,256]{1,0:T(8,128)S(1)}, f32[400,256]{1,0:T(8,128)S(1)}, u32[]{:S(2)}, u32[]{:S(2)}) %collective-permute-start.9) | collective-permute-done | bytes 409632 | tf_op jit(solution)/shard_map/ppermute | solution.py:35
  227.5 1.2 all-to-all-done.2
  228.6 1.5 broadcast_in_dim.41
  230.1 4.4 %all-to-all-start.3 = ((f32[16,256,128]{2,1,0:T(8,128)}), f32[16,256,128]{2,1,0:T(8,128)}, u32[]{:S(2)}, u32[]{:S(2)}) async-start(f32[16,256,128]{2,1,0:T(8,128)} %broadcast_in_dim.41), calls=%async_computation.3 | async-start | bytes 4194304 | tf_op jit(solution)/shard_map/all_to_all | solution.py:452
  234.6 0.9 shard_map.132
  235.5 24.6 %all-to-all-done.3 = f32[16,256,128]{2,1,0:T(8,128)} async-done(((f32[16,256,128]{2,1,0:T(8,128)}), f32[16,256,128]{2,1,0:T(8,128)}, u32[]{:S(2)}, u32[]{:S(2)}) %all-to-all-start.3) | async-done | bytes 2097184 | tf_op jit(solution)/shard_map/all_to_all | solution.py:452
  260.1 6.1 %collective-permute-start.10 = (f32[2,2048,128]{2,1,0:T(8,128)}, f32[2,2048,128]{2,1,0:T(8,128)S(1)}, u32[]{:S(2)}, u32[]{:S(2)}) collective-permute-start(f32[2,2048,128]{2,1,0:T(8,128)} %bitcast.34.grad_ref), channel_id=1, source_target_pairs={{0,1},{1,0},{2,3},{3,2},{4,5},{5,4},{6,7},{7,6},{8,9},{9,8},{10,11... | collective-permute-start | bytes 6291464 | tf_op jit(solution)/shard_map/ppermute | solution.py:35
  266.2 0.6 reshape.116.state_ref
  266.9 3.4 %shard_map.133 = (f32[400,2560]{1,0:T(8,128)}, f32[1,2560]{1,0:T(1,128)}) custom-call(s32[1]{0:T(128)} %bitcast.38.core_ref, f32[2,2048,128]{2,1,0:T(8,128)} %bitcast.34.grad_ref, f32[400,2560]{1,0:T(8,128)} %bitcast.68, f32[1,2560]{1,0:T(1,128)} %reshape.116.state_ref), custom_call_target="tpu_custom_call" | custom-call | flops 5120000 | bytes 6291456 | tf_op jit(solution)/shard_map/pallas_call | solution.py:378
  270.2 1.3 copy-done.12
  271.6 3.4 %shard_map.134 = (f32[400,2560]{1,0:T(8,128)}, f32[1,2560]{1,0:T(1,128)}) custom-call(s32[1]{0:T(128)} %bitcast.37.core_ref, f32[2,2048,128]{2,1,0:T(8,128)} %copy-done.12, f32[400,2560]{1,0:T(8,128)} %bitcast.69, f32[1,2560]{1,0:T(1,128)} %reshape.116.state_ref, ...), custom_call_target="tpu_custom_call", output_to_operand_aliasing={{0}: (4, {}), {1}: (5, {})} | custom-call | flops 5120000 | bytes 6291456 | tf_op jit(solution)/shard_map/pallas_call | solution.py:378
  274.9 1.3 reduce.1
  (57 shorter events, 0.6 us)
Async XLA Ops:
  0.6 21.6 %copy-start = (f32[256,400]{0,1:T(8,128)S(1)}, f32[256,400]{0,1:T(8,128)}, u32[]{:S(2)}) copy-start(f32[256,400]{0,1:T(8,128)} %param.9) | copy-start | bytes 1228804
  0.6 23.9 %copy-start.14 = (s32[1,2,1024]{2,1,0:T(2,128)S(1)}, s32[1,2,1024]{2,1,0:T(2,128)}, u32[]{:S(2)}) copy-start(s32[1,2,1024]{2,1,0:T(2,128)} %param.17) | copy-start | bytes 24580
  14.3 13.0 %collective-permute-start = (f32[400,256]{1,0:T(8,128)}, f32[400,256]{1,0:T(8,128)S(1)}, u32[]{:S(2)}, u32[]{:S(2)}) collective-permute-start(f32[400,256]{1,0:T(8,128)} %bitcast.52), channel_id=1, source_target_pairs={{0,2},{2,0},{1,3},{3,1},{4,6},{6,4},{5,7},{7,5},{8,10},{10,8},{9,1... | collective-permute-start | bytes 1228808 | tf_op jit(solution)/shard_map/ppermute | solution.py:35
  16.3 15.6 %copy-start.8 = (s32[1,512]{1,0:T(1,128)}, s32[1,512]{1,0:T(1,128)S(1)}, u32[]{:S(2)}) copy-start(s32[1,512]{1,0:T(1,128)S(1)} %get-tuple-element.105.ids_ref) | copy-start | bytes 6148
  30.3 0.9 copy-start.2
  31.9 27.5 %collective-permute-start.1 = (f32[416,128]{1,0:T(8,128)S(1)}, f32[416,128]{1,0:T(8,128)S(1)}, u32[]{:S(2)}, u32[]{:S(2)}) collective-permute-start(f32[416,128]{1,0:T(8,128)S(1)} %get-tuple-element.57), channel_id=1, source_target_pairs={{0,256},{32,288},{64,320},{96,352},{128,384},{160,416},{192,448},{... | collective-permute-start | bytes 638984 | tf_op jit(solution)/shard_map/ppermute | solution.py:35
  63.4 0.8 copy-start.3
  64.1 0.8 copy-start.11
  64.9 37.2 %copy-start.1 = (f32[2,400,256]{2,1,0:T(8,128)S(1)}, f32[2,400,256]{2,1,0:T(8,128)}, u32[]{:S(2)}) copy-start(f32[2,400,256]{2,1,0:T(8,128)} %shard_map.122.rel_ref) | copy-start | bytes 2457604
  64.9 37.2 %copy-start.10 = (f32[256]{0:T(256)S(1)}, f32[256]{0:T(256)}, u32[]{:S(2)}) copy-start(f32[256]{0:T(256)} %param.10) | copy-start | bytes 3076
  64.9 3.5 %collective-permute-start.2 = (f32[400,128]{1,0:T(8,128)S(1)}, f32[400,128]{1,0:T(8,128)S(1)}, u32[]{:S(2)}, u32[]{:S(2)}) collective-permute-start(f32[400,128]{1,0:T(8,128)S(1)} %get-tuple-element.62), channel_id=1, source_target_pairs={{0,1},{1,0},{2,3},{3,2},{4,5},{5,4},{6,7},{7,6},{8,9},{9,8},{10,11... | collective-permute-start | bytes 614408 | tf_op jit(solution)/shard_map/ppermute | solution.py:35
  68.4 12.7 %collective-permute-start.3 = (s32[16,128]{1,0:T(8,128)S(1)}, s32[16,128]{1,0:T(8,128)S(1)}, u32[]{:S(2)}, u32[]{:S(2)}) collective-permute-start(s32[16,128]{1,0:T(8,128)S(1)} %pad_add_fusion), channel_id=1, source_target_pairs={{0,4},{4,0},{1,5},{5,1},{2,6},{6,2},{3,7},{7,3},{8,12},{12,8},{9,1... | collective-permute-start | bytes 24584 | tf_op jit(solution)/shard_map/ppermute | solution.py:35
  72.8 18.7 %collective-permute-start.5 = (f32[400,256]{1,0:T(8,128)}, f32[400,256]{1,0:T(8,128)S(1)}, u32[]{:S(2)}, u32[]{:S(2)}) collective-permute-start(f32[400,256]{1,0:T(8,128)} %copy-done.11), channel_id=1, source_target_pairs={{0,2},{2,0},{1,3},{3,1},{4,6},{6,4},{5,7},{7,5},{8,10},{10,8},{9,1... | collective-permute-start | bytes 1228808 | tf_op jit(solution)/shard_map/ppermute | solution.py:35
  75.0 16.5 %collective-permute-start.4 = (f32[400,128]{1,0:T(8,128)S(1)}, f32[400,128]{1,0:T(8,128)S(1)}, u32[]{:S(2)}, u32[]{:S(2)}) collective-permute-start(f32[400,128]{1,0:T(8,128)S(1)} %add.20), channel_id=1, source_target_pairs={{0,256},{32,288},{64,320},{96,352},{128,384},{160,416},{192,448},{... | collective-permute-start | bytes 614408 | tf_op jit(solution)/shard_map/ppermute | solution.py:35
  81.2 20.9 %copy-start.4 = (f32[400,256]{1,0:T(8,128)S(1)}, f32[400,256]{1,0:T(8,128)}, u32[]{:S(2)}) copy-start(f32[400,256]{1,0:T(8,128)} %copy-done.3) | copy-start | bytes 1228804
  81.7 24.3 %copy-start.9 = (s32[1,512]{1,0:T(1,128)S(1)}, s32[1,512]{1,0:T(1,128)}, u32[]{:S(2)}) copy-start(s32[1,512]{1,0:T(1,128)} %copy-done.8) | copy-start | bytes 6148
  91.5 10.5 %copy-start.5 = (f32[400,256]{1,0:T(8,128)}, f32[400,256]{1,0:T(8,128)S(1)}, u32[]{:S(2)}) copy-start(f32[400,256]{1,0:T(8,128)S(1)} %collective-permute-done.5.got_ref) | copy-start | bytes 1228804
  102.1 1.0 copy-start.6
  103.7 26.9 %copy-start.7 = (f32[1,400,256]{2,1,0:T(8,128)S(1)}, f32[1,400,256]{2,1,0:T(8,128)}, u32[]{:S(2)}) copy-start(f32[1,400,256]{2,1,0:T(8,128)} %shard_map.124.rel_ref) | copy-start | bytes 1228804
  103.7 12.9 %collective-permute-start.6 = (f32[400,256]{1,0:T(8,128)S(1)}, f32[400,256]{1,0:T(8,128)S(1)}, u32[]{:S(2)}, u32[]{:S(2)}) collective-permute-start(f32[400,256]{1,0:T(8,128)S(1)} %get-tuple-element.70.own_ref), channel_id=1, source_target_pairs={{0,2},{2,0},{1,3},{3,1},{4,6},{6,4},{5,7},{7,5},{8,10},{10,8},{9,1... | collective-permute-start | bytes 1228808 | tf_op jit(solution)/shard_map/ppermute | solution.py:35
  133.1 3.3 %collective-permute-start.7 = (f32[400,128]{1,0:T(8,128)S(1)}, f32[400,128]{1,0:T(8,128)S(1)}, u32[]{:S(2)}, u32[]{:S(2)}) collective-permute-start(f32[400,128]{1,0:T(8,128)S(1)} %get-tuple-element.75), channel_id=1, source_target_pairs={{0,1},{1,0},{2,3},{3,2},{4,5},{5,4},{6,7},{7,6},{8,9},{9,8},{10,11... | collective-permute-start | bytes 614408 | tf_op jit(solution)/shard_map/ppermute | solution.py:35
  136.5 14.4 %collective-permute-start.8 = (f32[400,128]{1,0:T(8,128)S(1)}, f32[400,128]{1,0:T(8,128)S(1)}, u32[]{:S(2)}, u32[]{:S(2)}) collective-permute-start(f32[400,128]{1,0:T(8,128)S(1)} %get-tuple-element.79), channel_id=1, source_target_pairs={{0,4},{4,0},{1,5},{5,1},{2,6},{6,2},{3,7},{7,3},{8,12},{12,8},{9,1... | collective-permute-start | bytes 614408 | tf_op jit(solution)/shard_map/ppermute | solution.py:35
  175.5 35.0 %all-to-all-start.1 = ((f32[16,16,128]{2,1,0:T(8,128)}), f32[16,16,128]{2,1,0:T(8,128)S(1)}, u32[]{:S(2)}, u32[]{:S(2)}) async-start(f32[16,16,128]{2,1,0:T(8,128)} %bitcast.31), calls=%async_computation.1 | async-start | bytes 262144 | tf_op jit(solution)/shard_map/all_to_all | solution.py:445
  210.4 55.8 %copy-start.13 = (f32[2560]{0:T(1024)S(1)}, f32[2560]{0:T(1024)}, u32[]{:S(2)}) copy-start(f32[2560]{0:T(1024)} %param.12) | copy-start | bytes 30724
  211.1 17.5 %all-to-all-start.2 = ((f32[16,16,128]{2,1,0:T(8,128)}), f32[16,16,128]{2,1,0:T(8,128)S(1)}, u32[]{:S(2)}, u32[]{:S(2)}) async-start(f32[16,16,128]{2,1,0:T(8,128)} %broadcast_in_dim.40), calls=%async_computation.2 | async-start | bytes 262144 | tf_op jit(solution)/shard_map/all_to_all | solution.py:449
  216.6 10.8 %collective-permute-start.9 = (f32[400,256]{1,0:T(8,128)S(1)}, f32[400,256]{1,0:T(8,128)S(1)}, u32[]{:S(2)}, u32[]{:S(2)}) collective-permute-start(f32[400,256]{1,0:T(8,128)S(1)} %get-tuple-element.88), channel_id=1, source_target_pairs={{0,2},{2,0},{1,3},{3,1},{4,6},{6,4},{5,7},{7,5},{8,10},{10,8},{9,1... | collective-permute-start | bytes 1228808 | tf_op jit(solution)/shard_map/ppermute | solution.py:35
  230.1 30.0 %all-to-all-start.3 = ((f32[16,256,128]{2,1,0:T(8,128)}), f32[16,256,128]{2,1,0:T(8,128)}, u32[]{:S(2)}, u32[]{:S(2)}) async-start(f32[16,256,128]{2,1,0:T(8,128)} %broadcast_in_dim.41), calls=%async_computation.3 | async-start | bytes 4194304 | tf_op jit(solution)/shard_map/all_to_all | solution.py:452
  260.1 10.1 %collective-permute-start.10 = (f32[2,2048,128]{2,1,0:T(8,128)}, f32[2,2048,128]{2,1,0:T(8,128)S(1)}, u32[]{:S(2)}, u32[]{:S(2)}) collective-permute-start(f32[2,2048,128]{2,1,0:T(8,128)} %bitcast.34.grad_ref), channel_id=1, source_target_pairs={{0,1},{1,0},{2,3},{3,2},{4,5},{5,4},{6,7},{7,6},{8,9},{9,8},{10,11... | collective-permute-start | bytes 6291464 | tf_op jit(solution)/shard_map/ppermute | solution.py:35
  270.2 1.4 copy-start.12

commit v3 on v2

--- a/solution.py
+++ b/solution.py
@@ -16,11 +16,14 @@
 SLOTS = 512
 PAIR = 256
 CHUNK = 128
+USED = 112
+SENT = 352
+TAIL = D - SENT
 ROWS = 256
 QUARTER = RELATIONS // 4
 PART = 512
 KROWS = 2048
-LETTER = D + 16
+LETTER = SENT + 16
 LEARN_RATE = 0.1
 EPSILON = 1e-08
 REL = ("l", "c")
@@ -68,6 +71,29 @@
 def back(out_ref, at, u1, u2, o1, o2):
     out_ref[:HALF, at] = u1 * o1 + u2 * o2
     out_ref[HALF:D, at] = u2 * o1 - u1 * o2
+
+
+def pack(out_ref, value):
+    lanes = lax.broadcasted_iota(I32, (TAIL, CHUNK), 1)
+    out_ref[:SENT, :] = value[:SENT, :]
+    for group in range(USED // 16):
+        at = slice(TAIL * group, TAIL * group + TAIL)
+        moved = pltpu.roll(value[SENT:, :], (USED - 16 * group) % CHUNK, 1)
+        out_ref[at, :] = jnp.where(lanes >= USED, moved, value[at, :])
+
+
+def unpack(out_ref, at, value):
+    lanes = lax.broadcasted_iota(I32, (TAIL, CHUNK), 1)
+    out_ref[:SENT, at] = value
+    rest = jnp.zeros((TAIL, CHUNK), F32)
+    for group in range(USED // 16):
+        moved = pltpu.roll(value[TAIL * group : TAIL * group + TAIL, :], (16 * group - USED) % CHUNK, 1)
+        rest = jnp.where(lanes // 16 == group, moved, rest)
+    out_ref[SENT:, at] = rest
+
+
+EVERY = slice(None)
+WORK = pltpu.VMEM((D, CHUNK), F32)
 
 
 def shape(*dims):
@@ -131,15 +157,16 @@
 
 
 def heads_kernel(s_ref, ids_ref, near_ref, far_ref, out_ref):
-    out_ref[...] = chunk_rows(s_ref[0], ids_ref[...], near_ref, far_ref)
-
-
-def letter_kernel(s_ref, ids_ref, near_ref, far_ref, rel_ref, target_ref, neg_ref, head_ref, out_ref):
-    head_ref[...] = chunk_rows(s_ref[0], ids_ref[...], near_ref, far_ref)
-    every = slice(None)
-    times(out_ref, every, head_ref[:HALF, :], head_ref[HALF:, :], rel_ref[0, :HALF, :], rel_ref[0, HALF:, :])
-    out_ref[D : D + 8, :] = jnp.broadcast_to(target_ref[...], (8, CHUNK)).astype(F32)
-    out_ref[D + 8 :, :] = neg_ref[...].astype(F32)
+    pack(out_ref, chunk_rows(s_ref[0], ids_ref[...], near_ref, far_ref))
+
+
+def letter_kernel(s_ref, ids_ref, near_ref, far_ref, rel_ref, target_ref, neg_ref, head_ref, out_ref, work_ref, a_ref):
+    a_ref[...] = chunk_rows(s_ref[0], ids_ref[...], near_ref, far_ref)
+    pack(head_ref, a_ref[...])
+    times(work_ref, EVERY, a_ref[:HALF, :], a_ref[HALF:, :], rel_ref[0, :HALF, :], rel_ref[0, HALF:, :])
+    pack(out_ref, work_ref[...])
+    out_ref[SENT : SENT + 8, :] = jnp.broadcast_to(target_ref[...], (8, CHUNK)).astype(F32)
+    out_ref[SENT + 8 :, :] = neg_ref[...].astype(F32)
 
 
 HEADS_IN = [whole(1, CHUNK), whole(2, D, ROWS), whole(2, D, ROWS)]
@@ -147,16 +174,16 @@
 
 
 def heads(s, ids, near, far):
-    return call(heads_kernel, shape(D, CHUNK), HEADS_IN, whole(D, CHUNK), [], *HEADS_COST)(s, ids, near, far)
+    return call(heads_kernel, shape(SENT, CHUNK), HEADS_IN, whole(SENT, CHUNK), [], *HEADS_COST)(s, ids, near, far)
 
 
 def letter(s, ids, near, far, rel_rows, target, negatives):
     return call(
         letter_kernel,
-        [shape(D, CHUNK), shape(LETTER, CHUNK)],
+        [shape(SENT, CHUNK), shape(LETTER, CHUNK)],
         HEADS_IN + [whole(1, D, CHUNK), whole(1, CHUNK), whole(8, 128)],
-        [whole(D, CHUNK), whole(LETTER, CHUNK)],
-        [],
+        [whole(SENT, CHUNK), whole(LETTER, CHUNK)],
+        [WORK] * 2,
         *HEADS_COST,
     )(s, ids, near, far, rel_rows, target, negatives)
 
@@ -184,72 +211,74 @@
         out_ref[...] = dot3(product, weight, (1, 1))
     h_ref[...] = d_product
     core = q & 1
-    keep_ref[...] = h_ref[:, pl.ds(pl.multiple_of(CHUNK * core, CHUNK), CHUNK)]
-    send_ref[...] = h_ref[:, pl.ds(pl.multiple_of(CHUNK * (1 - core), CHUNK), CHUNK)]
+    pack(keep_ref, h_ref[:, pl.ds(pl.multiple_of(CHUNK * core, CHUNK), CHUNK)])
+    pack(send_ref, h_ref[:, pl.ds(pl.multiple_of(CHUNK * (1 - core), CHUNK), CHUNK)])
 
 
 def answer_kernel(s_ref, letters_ref, own_ref, other_ref, keep_ref, send_ref, grad_ref, grad_send_ref, h_ref):
     for k in range(2):
-        h_ref[:, CHUNK * k : CHUNK * k + CHUNK] = letters_ref[k, :D, :]
-    target = jnp.concatenate([letters_ref[k, D : D + 1, :] for k in range(2)], axis=1).astype(I32)
-    negatives = letters_ref[0, D + 8 :, :].astype(I32)
+        unpack(h_ref, slice(CHUNK * k, CHUNK * k + CHUNK), letters_ref[k, :SENT, :])
+    target = jnp.concatenate([letters_ref[k, SENT : SENT + 1, :] for k in range(2)], axis=1).astype(I32)
+    negatives = letters_ref[0, SENT + 8 :, :].astype(I32)
     weigh(s_ref, h_ref, target, negatives, own_ref, other_ref, keep_ref, send_ref, grad_ref, grad_send_ref)
 
 
 def answer(s, letters, own, other):
     return call(
         answer_kernel,
-        [shape(D, CHUNK)] * 2 + [shape(D, ROWS)] * 2,
+        [shape(SENT, CHUNK)] * 2 + [shape(D, ROWS)] * 2,
         [whole(2, LETTER, CHUNK), whole(D, ROWS), whole(D, ROWS)],
-        [whole(D, CHUNK)] * 2 + [whole(D, ROWS)] * 2,
+        [whole(SENT, CHUNK)] * 2 + [whole(D, ROWS)] * 2,
         [pltpu.VMEM((D, PAIR), F32)],
         1024 * 1024 * 1024,
         5 * 1024 * 1024,
     )(s, letters, own, other)
 
 
-def score_kernel(s_ref, target_ref, neg_ref, a_ref, rel_ref, own_ref, other_ref, keep_ref, send_ref, grad_ref, grad_send_ref, head_ref, kind_ref, h_ref):
+def score_kernel(s_ref, target_ref, neg_ref, a_ref, rel_ref, own_ref, other_ref, keep_ref, send_ref, grad_ref, grad_send_ref, head_ref, kind_ref, h_ref, work_ref):
     first = s_ref[1]
     for k in range(2):
         at = slice(CHUNK * k, CHUNK * k + CHUNK)
-        a1, a2 = a_ref[first + k, :HALF, :], a_ref[first + k, HALF:, :]
-        times(h_ref, at, a1, a2, rel_ref[0, :HALF, at], rel_ref[0, HALF:, at])
+        unpack(work_ref, at, a_ref[first + k])
+        times(h_ref, at, work_ref[:HALF, at], work_ref[HALF:, at], rel_ref[0, :HALF, at], rel_ref[0, HALF:, at])
     weigh(s_ref, h_ref, target_ref[...], neg_ref[...], own_ref, other_ref, keep_ref, send_ref, grad_ref, grad_send_ref)
     core = s_ref[0] & 1
-    head_ref[...] = a_ref[first + core]
-    kind_ref[...] = rel_ref[0, :, pl.ds(pl.multiple_of(CHUNK * core, CHUNK), CHUNK)]
+    mine = pl.ds(pl.multiple_of(CHUNK * core, CHUNK), CHUNK)
+    head_ref[...] = work_ref[:, mine]
+    kind_ref[...] = rel_ref[0, :, mine]
 
 
 def score(s, target, negatives, head_rows, rel_rows, own, other):
     return call(
         score_kernel,
-        [shape(D, CHUNK)] * 2 + [shape(D, ROWS)] * 2 + [shape(D, CHUNK)] * 2,
+        [shape(SENT, CHUNK)] * 2 + [shape(D, ROWS)] * 2 + [shape(D, CHUNK)] * 2,
         [
             whole(1, PAIR),
             whole(8, 128),
-            whole(4, D, CHUNK),
+            whole(4, SENT, CHUNK),
             whole(1, D, PAIR),
             whole(D, ROWS),
             whole(D, ROWS),
         ],
-        [whole(D, CHUNK)] * 2 + [whole(D, ROWS)] * 2 + [whole(D, CHUNK)] * 2,
-        [pltpu.VMEM((D, PAIR), F32)],
+        [whole(SENT, CHUNK)] * 2 + [whole(D, ROWS)] * 2 + [whole(D, CHUNK)] * 2,
+        [pltpu.VMEM((D, PAIR), F32)] * 2,
         1024 * 1024 * 1024,
         5 * 1024 * 1024,
     )(s, target, negatives, head_rows, rel_rows, own, other)
 
 
-def back_kernel(s_ref, keep_ref, got_ref, head_ref, kind_ref, d_head_ref, d_kind_ref):
-    up = keep_ref[...] + got_ref[...]
+def back_kernel(s_ref, keep_ref, got_ref, head_ref, kind_ref, d_head_ref, d_kind_ref, up_ref, work_ref):
+    unpack(up_ref, EVERY, keep_ref[...] + got_ref[...])
     for other_ref, out_ref in ((kind_ref, d_head_ref), (head_ref, d_kind_ref)):
-        back(out_ref, slice(None), up[:HALF, :], up[HALF:, :], other_ref[:HALF, :], other_ref[HALF:, :])
+        back(work_ref, EVERY, up_ref[:HALF, :], up_ref[HALF:, :], other_ref[:HALF, :], other_ref[HALF:, :])
+        pack(out_ref, work_ref[...])
 
 
 def chunk_back(s, keep, got, head, kind):
-    chunk = whole(D, CHUNK)
-    return call(back_kernel, [shape(D, CHUNK)] * 2, [chunk] * 4, [chunk] * 2, [], 10 * D * CHUNK, 32 * D * CHUNK)(
-        s, keep, got, head, kind
-    )
+    sent, chunk = whole(SENT, CHUNK), whole(D, CHUNK)
+    out = [shape(SENT, CHUNK)] * 2
+    ins = [sent] * 2 + [chunk] * 2
+    return call(back_kernel, out, ins, [sent] * 2, [WORK] * 2, 10 * D * CHUNK, 32 * D * CHUNK)(s, keep, got, head, kind)
 
 
 def step_rows(gradient, own_ref, state_ref, out_ref, out_state_ref):
@@ -262,11 +291,12 @@
     return slice(CHUNK * k, CHUNK * k + CHUNK)
 
 
-def answered_kernel(s_ref, ids_ref, answers_ref, rel_ref, grad_ref, got_ref, own_ref, state_ref, out_ref, out_state_ref, high_ref, low_ref, d_ref):
+def answered_kernel(s_ref, ids_ref, answers_ref, rel_ref, grad_ref, got_ref, own_ref, state_ref, out_ref, out_state_ref, high_ref, low_ref, d_ref, up_ref):
     for k in range(4):
         at = chunk_at(k % 2)
         w1, w2 = rel_ref[k // 2, :HALF, at], rel_ref[k // 2, HALF:, at]
-        back(d_ref, slice(None), answers_ref[k, :HALF, :], answers_ref[k, HALF:, :], w1, w2)
+        unpack(up_ref, EVERY, answers_ref[k])
+        back(d_ref, EVERY, up_ref[:HALF, :], up_ref[HALF:, :], w1, w2)
         high_ref[:, chunk_at(k)], low_ref[:, chunk_at(k)] = split(d_ref[...])
     spots = hot(ROWS, ids_ref[...], ROWS * s_ref[0])
     gradient = grad_ref[...] + got_ref[...] + dot2((high_ref[...], low_ref[...]), spots, (1, 1))
@@ -281,31 +311,30 @@
     return call(
         answered_kernel,
         [shape(D, ROWS), shape(1, ROWS)],
-        [whole(1, SLOTS), whole(4, D, CHUNK), whole(2, D, PAIR), whole(D, ROWS), whole(D, ROWS)] + ROWS_SPECS,
+        [whole(1, SLOTS), whole(4, SENT, CHUNK), whole(2, D, PAIR), whole(D, ROWS), whole(D, ROWS)] + ROWS_SPECS,
         ROWS_SPECS,
-        PARTS + [pltpu.VMEM((D, CHUNK), F32)],
+        PARTS + [WORK] * 2,
         4 * D * SLOTS * ROWS,
         4 * 1024 * 1024,
     )(s, ids, answers, rel_rows, grad, got, own, state)
 
 
-def join_kernel(s_ref, ids_ref, parts_ref, grad_ref, send_ref, out_ref, out_send_ref):
-    parts = [split(parts_ref[k]) for k in range(2)]
+def join_kernel(s_ref, ids_ref, parts_ref, grad_ref, send_ref, out_ref, out_send_ref, work_ref):
+    for k in range(2):
+        unpack(work_ref, chunk_at(k), parts_ref[k])
+    parts = split(work_ref[...])
     for flipped, ref, to_ref in ((0, grad_ref, out_ref), (2, send_ref, out_send_ref)):
         base = ROWS * (s_ref[0] ^ flipped)
-        total = ref[...]
-        for k in range(2):
-            total += dot2(parts[k], hot(ROWS, ids_ref[:, chunk_at(k)], base), (1, 1))
-        to_ref[...] = total
+        to_ref[...] = ref[...] + dot2(parts, hot(ROWS, ids_ref[...], base), (1, 1))
 
 
 def join(s, ids, parts, grad, grad_send):
     return call(
         join_kernel,
         [shape(D, ROWS)] * 2,
-        [whole(1, PAIR), whole(2, D, CHUNK), whole(D, ROWS), whole(D, ROWS)],
+        [whole(1, PAIR), whole(2, SENT, CHUNK), whole(D, ROWS), whole(D, ROWS)],
         [whole(D, ROWS)] * 2,
-        [],
+        [pltpu.VMEM((D, PAIR), F32)],
         4 * D * PAIR * 2 * ROWS,
         3 * 1024 * 1024,
     )(s, ids, parts, grad, grad_send)
@@ -332,17 +361,19 @@
     out_ref[5 * D :, :] = jnp.zeros((KROWS - 5 * D, 128), F32)
 
 
-def kinds_answered_kernel(s_ref, ids_ref, answers_ref, heads_ref, out_ref, high_ref, low_ref, d_ref):
+def kinds_answered_kernel(s_ref, ids_ref, answers_ref, heads_ref, out_ref, high_ref, low_ref, d_ref, up_ref, a_ref):
     for k in range(4):
-        a1, a2 = heads_ref[k, :HALF, :], heads_ref[k, HALF:, :]
-        back(d_ref, slice(None), answers_ref[k, :HALF, :], answers_ref[k, HALF:, :], a1, a2)
+        unpack(a_ref, EVERY, heads_ref[k])
+        unpack(up_ref, EVERY, answers_ref[k])
+        back(d_ref, EVERY, up_ref[:HALF, :], up_ref[HALF:, :], a_ref[:HALF, :], a_ref[HALF:, :])
         high_ref[:, chunk_at(k)], low_ref[:, chunk_at(k)] = split(d_ref[...])
     count_in(s_ref, ids_ref, None, out_ref, high_ref, low_ref)
 
 
-def kinds_kernel(s_ref, ids_ref, parts_ref, before_ref, out_ref, high_ref, low_ref):
+def kinds_kernel(s_ref, ids_ref, parts_ref, before_ref, out_ref, high_ref, low_ref, work_ref):
     for k in range(4):
-        high_ref[:, chunk_at(k)], low_ref[:, chunk_at(k)] = split(parts_ref[k])
+        unpack(work_ref, EVERY, parts_ref[k])
+        high_ref[:, chunk_at(k)], low_ref[:, chunk_at(k)] = split(work_ref[...])
     count_in(s_ref, ids_ref, before_ref, out_ref, high_ref, low_ref)
 
 
@@ -350,42 +381,48 @@
 
 
 def kinds_answered(s, ids, answers, heads):
-    ins = [whole(1, SLOTS)] + [whole(4, D, CHUNK)] * 2
-    scratch = PARTS + [pltpu.VMEM((D, CHUNK), F32)]
+    ins = [whole(1, SLOTS)] + [whole(4, SENT, CHUNK)] * 2
+    scratch = PARTS + [WORK] * 3
     return call(kinds_answered_kernel, shape(KROWS, 128), ins, whole(KROWS, 128), scratch, *KINDS_COST)(
         s, ids, answers, heads
     )
 
 
 def kinds(s, ids, parts, before):
-    ins = [whole(1, SLOTS), whole(4, D, CHUNK), whole(KROWS, 128)]
-    return call(kinds_kernel, shape(KROWS, 128), ins, whole(KROWS, 128), PARTS, *KINDS_COST)(s, ids, parts, before)
+    ins = [whole(1, SLOTS), whole(4, SENT, CHUNK), whole(KROWS, 128)]
+    return call(kinds_kernel, shape(KROWS, 128), ins, whole(KROWS, 128), PARTS + [WORK], *KINDS_COST)(s, ids, parts, before)
 
 
 def relations_kernel(core_ref, grad_ref, table_ref, state_ref, *refs):
     out_ref, out_state_ref = refs[-2:]
+
+    @pl.when(pl.program_id(0) == 0)
+    def _():
+        out_state_ref[...] = refs[1][...] if len(refs) > 2 else state_ref[...]
+
     for k in range(5):
         at = slice(128 * k, 128 * k + 128)
+        row = pl.ds(5 * (2 * pl.program_id(0) + core_ref[0]) + k, 1)
         gradient = grad_ref[0, D * k : D * k + D, :]
-        state = state_ref[:, at] + jnp.sum(gradient * gradient, axis=0, keepdims=True) * (1.0 / D)
-        out_state_ref[:, at] = state
+        state = state_ref[row, :] + jnp.sum(gradient * gradient, axis=0, keepdims=True) * (1.0 / D)
+        out_state_ref[row, :] = state
         out_ref[:, at] = table_ref[:, at] - gradient * (LEARN_RATE / (jnp.sqrt(state) + EPSILON))
 
 
 def update_relations(core, grads, table, state, before):
-    mine = lambda l, core: (0, 2 * l + core[0])
-    blocks = [pl.BlockSpec((D, QUARTER), mine), pl.BlockSpec((1, QUARTER), mine)]
+    mine = pl.BlockSpec((D, QUARTER), lambda l, core: (0, 2 * l + core[0]))
+    states = whole(RELATIONS // 128, 128)
     return call(
         relations_kernel,
-        [shape(D, RELATIONS), shape(1, RELATIONS)],
-        [pl.BlockSpec((1, KROWS, 128), lambda l, core: (l, 0, 0))] + blocks + [pl.BlockSpec(memory_space=pl.ANY)] * len(before),
-        blocks,
+        [shape(D, RELATIONS), shape(RELATIONS // 128, 128)],
+        [pl.BlockSpec((1, KROWS, 128), lambda l, core: (l, 0, 0)), mine, states]
+        + ([pl.BlockSpec(memory_space=pl.ANY), states] if before else []),
+        [mine, states],
         [],
         5 * D * RELATIONS,
         6 * 1024 * 1024,
         grid=(2,),
-        room=56,
-        input_output_aliases={4: 0, 5: 1} if before else {},
+        input_output_aliases={4: 0} if before else {},
     )(core, grads, table, state, *before)
 
 
@@ -395,8 +432,8 @@
     every = lax.all_gather(lists.reshape(12, 128), REL, axis=0).reshape(4, 6, CAP)
     light = jnp.moveaxis(every[:, :, :LIGHT], 0, 1).reshape(6, 4 * LIGHT)
     heavy = jnp.max(every[:, :, LIGHT:], axis=0)
-    empty = jnp.full((6, SLOTS - 4 * LIGHT - (CAP - LIGHT)), -1, I32)
-    return jnp.concatenate([light, heavy, empty], axis=1)
+    chunks = jnp.concatenate([light, heavy], axis=1).reshape(6, 4, USED)
+    return jnp.pad(chunks, ((0, 0), (0, 0), (0, CHUNK - USED)), constant_values=-1).reshape(6, SLOTS)
 
 
 def local(entities, entity_state, relations, relation_state, src_rows, rel_ids, dst_rows, live_count, neg_rows):
@@ -451,7 +488,7 @@
     own, state = update(s, grad, grad_got, own, state)
     half = lax.all_to_all(jnp.broadcast_to(share[None], (16, 256, 128)), ("l",) + SPREAD, 0, 0).reshape(2, KROWS, 128)
     half, own, state = tied((half, own, state))
-    table_state = relation_state.reshape(1, RELATIONS)
+    table_state = relation_state.reshape(RELATIONS // 128, 128)
     first = update_relations(core.reshape(1), half, table, table_state, [])
     new_table, new_table_state = update_relations((1 - core).reshape(1), flip(half, "c"), table, table_state, first)
     return own.T, state.reshape(ROWS), new_table.T, new_table_state.reshape(RELATIONS)

time: 277 us -> 267 us (0.964)
  starting transfers between devices: 74.5 us -> 66.1 us
  waiting for transfers between devices: 59.4 us -> 62.9 us
    ppermute x11, starting transfers between devices: 41.6 us -> 37.3 us  [flip(): return lax.ppermute(block, axis, [(i, i ^ mask) for i in range(count)])]
    ppermute x11, waiting for transfers between devices: 25.6 us -> 28.9 us  [flip(): return lax.ppermute(block, axis, [(i, i ^ mask) for i in range(count)])]
    all_to_all x1, starting transfers between devices: 23 us -> 19.7 us  [local(): lax.all_to_all(jnp.sum(shares, axis=0).reshape(16, 16, 128), 'z', 0, 0)]
  transfers between devices with their start and end apart: 14 -> 14, of which waited for: 9 -> 9; matrix products, arithmetic and copies ran while one was open for 1% -> 0% of each run, Pallas kernels for 9% -> 9%
where the time goes in v3:
time: 267 us; the launch traced here: 265 us
  blocking collectives  90.5 us (34%)
  starting transfers between devices  66.1 us (25%)
  waiting for transfers between devices  62.9 us (24%)
  Pallas kernels  33.9 us (13%)
  local copies, waits for them, and re-layouts  8.49 us (3%)
    ppermute x11, starting transfers between devices, flip(): return lax.ppermute(block, axis, [(i, i ^ mask) for i in range(count)])  37.3 us
    ppermute x11, waiting for transfers between devices, flip(): return lax.ppermute(block, axis, [(i, i ^ mask) for i in range(count)])  28.9 us
    all_to_all x1, waiting for transfers between devices, local(): lax.all_to_all(jnp.broadcast_to(share[None], (16, 256, 128)), ('l',) + SP...  24.6 us
    all_to_all x1, blocking collectives, local(): shares = lax.all_to_all(total.reshape(8, 256, 128), SPREAD, 0, 0)  23 us
    all_to_all x1, starting transfers between devices, local(): lax.all_to_all(jnp.sum(shares, axis=0).reshape(16, 16, 128), 'z', 0, 0)  19.7 us
    pallas_call x3, Pallas kernels, lookup(): call(lookup_kernel, shape(lists, D, width), [whole(lists, 1, width), pl.B...  19.1 us
    all_gather x1, blocking collectives, slot_lists(): lax.all_gather(lists.reshape(12, 128), REL, axis=0).reshape(4, 6, CAP)  11.9 us
    all_gather x1, blocking collectives, local(): lax.all_gather(d_kind, REL, axis=0)  10.9 us
  transfers between devices with their start and end apart: 14, of which 9 were waited for; matrix products, arithmetic and copies ran while one was open for 0% of the time, Pallas kernels for 9%

profile of v3, /device:TPU:1, one launch (start us, length us, event | category | flops | bytes accessed | tf_op | source)
XLA Modules:
  0.0 265.5 jit_solution(2025540794759989894)
XLA Ops:
  0.7 0.8 iota_compare_fusion
  1.4 0.7 add_select_fusion
  2.2 11.9 %all_gather.63 = s32[4,12,128]{2,1,0:T(8,128)S(1)} all-gather(s32[1,12,128]{2,1,0:T(8,128)S(1)} %select_n.31), channel_id=1, replica_groups=mesh['z'=16,'y'=4,'h'=2,'l'=2,'c'=2] {'l','c'}, dimensions={0}, use_global_device_ids=true | all-gather | bytes 30720 | tf_op jit(solution)/shard_map/all_gather | solution.py:432
  14.2 0.1 reshape.110
  14.3 0.1 reshape.111
  14.4 1.9 collective-permute-start
  16.3 0.5 fusion.1.ids_ref
  16.9 5.4 %shard_map.120.rel_ref = f32[1,400,128]{2,1,0:T(8,128)} custom-call(s32[1]{0:T(128)} %bitcast.s_ref, s32[1,1,128]{2,1,0:T(1,128)} %fusion.1.ids_ref, f32[400,2560]{1,0:T(8,128)} %bitcast.50), custom_call_target="tpu_custom_call" | custom-call | flops 524288000 | bytes 5242880 | tf_op jit(solution)/shard_map/pallas_call | solution.py:137
  22.2 2.4 all-gather
  24.6 2.7 %collective-permute-done.other_ref = f32[400,256]{1,0:T(8,128)S(1)} collective-permute-done((f32[400,256]{1,0:T(8,128)}, f32[400,256]{1,0:T(8,128)S(1)}, u32[]{:S(2)}, u32[]{:S(2)}) %collective-permute-start) | collective-permute-done | bytes 409632 | tf_op jit(solution)/shard_map/ppermute | solution.py:38
  27.3 3.0 %all-gather.1 = f32[800,256]{1,0:T(8,128)S(1)} all-gather(f32[400,256]{1,0:T(8,128)S(1)} %collective-permute-done.other_ref), channel_id=3, replica_groups=mesh['z'=16,'y'=4,'h'=2,'l'=2,'c'=2] {'c'}, dimensions={0}, use_global_device_ids=true | all-gather | bytes 1228800 | tf_op jit(solution)/shard_map/all_gather | solution.py:453
  30.4 0.9 copy-done.3
  31.3 0.7 shard_map.121
  32.0 10.1 %collective-permute-start.1 = (f32[368,128]{1,0:T(8,128)S(1)}, f32[368,128]{1,0:T(8,128)S(1)}, u32[]{:S(2)}, u32[]{:S(2)}) collective-permute-start(f32[368,128]{1,0:T(8,128)S(1)} %get-tuple-element.57), channel_id=1, source_target_pairs={{0,256},{32,288},{64,320},{96,352},{128,384},{160,416},{192,448},{... | collective-permute-start | bytes 565256 | tf_op jit(solution)/shard_map/ppermute | solution.py:38
  42.1 8.7 %all-gather.2 = f32[1408,128]{1,0:T(8,128)S(1)} all-gather(f32[352,128]{1,0:T(8,128)S(1)} %get-tuple-element.58), channel_id=4, replica_groups=mesh['z'=16,'y'=4,'h'=2,'l'=2,'c'=2] {'l','c'}, dimensions={0}, use_global_device_ids=true | all-gather | bytes 901120 | tf_op jit(solution)/shard_map/all_gather | solution.py:457
  50.9 8.2 %shard_map.122.rel_ref = f32[2,400,256]{2,1,0:T(8,128)} custom-call(s32[1]{0:T(128)} %bitcast.s_ref, s32[2,1,256]{2,1,0:T(1,128)} %bitcast.79, f32[400,2560]{1,0:T(8,128)} %bitcast.51), custom_call_target="tpu_custom_call" | custom-call | flops 2097152000 | bytes 5242880 | tf_op jit(solution)/shard_map/pallas_call | solution.py:137
  59.0 2.1 all-gather.3
  61.1 2.0 shard_map.123
  63.1 0.7 copy-done.4
  63.9 2.1 collective-permute-start.2
  66.0 1.2 collective-permute-done.2
  67.2 4.4 %collective-permute-start.3 = (s32[16,128]{1,0:T(8,128)S(1)}, s32[16,128]{1,0:T(8,128)S(1)}, u32[]{:S(2)}, u32[]{:S(2)}) collective-permute-start(s32[16,128]{1,0:T(8,128)S(1)} %pad_add_fusion.1), channel_id=1, source_target_pairs={{0,4},{4,0},{1,5},{5,1},{2,6},{6,2},{3,7},{7,3},{8,12},{12,8},{9,1... | collective-permute-start | bytes 24584 | tf_op jit(solution)/shard_map/ppermute | solution.py:38
  71.5 0.1 pad_add_fusion.2.s_ref
  71.6 2.1 collective-permute-start.5
  73.8 1.9 collective-permute-start.4
  75.7 0.6 fusion.ids_ref
  76.3 5.5 %shard_map.124.rel_ref = f32[1,400,256]{2,1,0:T(8,128)} custom-call(s32[1]{0:T(128)} %bitcast.s_ref, s32[1,1,256]{2,1,0:T(1,128)} %fusion.ids_ref, f32[400,2560]{1,0:T(8,128)} %bitcast.52), custom_call_target="tpu_custom_call" | custom-call | flops 1048576000 | bytes 5242880 | tf_op jit(solution)/shard_map/pallas_call | solution.py:137
  81.8 7.9 %collective-permute-done.4 = f32[352,128]{1,0:T(8,128)S(1)} collective-permute-done((f32[352,128]{1,0:T(8,128)S(1)}, f32[352,128]{1,0:T(8,128)S(1)}, u32[]{:S(2)}, u32[]{:S(2)}) %collective-permute-start.4) | collective-permute-done | bytes 180256 | tf_op jit(solution)/shard_map/ppermute | solution.py:38
  89.7 10.0 %all-gather.4 = f32[1408,128]{1,0:T(8,128)S(1)} all-gather(f32[352,128]{1,0:T(8,128)S(1)} %collective-permute-done.4), channel_id=6, replica_groups=mesh['z'=16,'y'=4,'h'=2,'l'=2,'c'=2] {'l','c'}, dimensions={0}, use_global_device_ids=true | all-gather | bytes 901120 | tf_op jit(solution)/shard_map/all_gather | solution.py:466
  99.8 1.0 copy-done.7
  100.8 0.6 shard_map.125
  101.4 2.3 collective-permute-start.6
  103.8 1.2 shard_map.126.before_ref
  104.9 2.5 all-gather.5
  107.4 7.0 %collective-permute-done.6.other_ref = f32[400,256]{1,0:T(8,128)S(1)} collective-permute-done((f32[400,256]{1,0:T(8,128)S(1)}, f32[400,256]{1,0:T(8,128)S(1)}, u32[]{:S(2)}, u32[]{:S(2)}) %collective-permute-start.6) | collective-permute-done | bytes 409632 | tf_op jit(solution)/shard_map/ppermute | solution.py:38
  114.3 3.0 %all-gather.6 = f32[800,256]{1,0:T(8,128)S(1)} all-gather(f32[400,256]{1,0:T(8,128)S(1)} %collective-permute-done.6.other_ref), channel_id=8, replica_groups=mesh['z'=16,'y'=4,'h'=2,'l'=2,'c'=2] {'c'}, dimensions={0}, use_global_device_ids=true | all-gather | bytes 1228800 | tf_op jit(solution)/shard_map/all_gather | solution.py:473
  117.3 0.7 shard_map.127
  118.0 9.9 %all-gather.7 = f32[1408,128]{1,0:T(8,128)S(1)} all-gather(f32[352,128]{1,0:T(8,128)S(1)} %shard_map.127), channel_id=9, replica_groups=mesh['z'=16,'y'=4,'h'=2,'l'=2,'c'=2] {'h','c'}, dimensions={0}, use_global_device_ids=true | all-gather | bytes 901120 | tf_op jit(solution)/shard_map/all_gather | solution.py:474
  127.9 2.7 %shard_map.128 = (f32[352,128]{1,0:T(8,128)S(1)}, f32[352,128]{1,0:T(8,128)S(1)}, f32[400,256]{1,0:T(8,128)S(1)}, f32[400,256]{1,0:T(8,128)S(1)}, f32[400,128]{1,0:T(8,128)S(1)}, /*index=5*/f32[400,128]{1,0:T(8,128)S(1)}) custom-call(s32[2]{0:T(128)S(1)} %pad_add_fusion.2.s_ref, s32[1,256]{1,0:T(1,128)S(1)} %constant_dynamic-slice_fusion.3.target_ref, ...), custom_call_target="tpu_custom_call" | custom-call | flops 1073741824 | bytes 5242880 | tf_op jit(solution)/shard_map/pallas_call | solution.py:252
  130.6 2.1 collective-permute-start.7
  132.6 1.2 collective-permute-done.7.got_ref
  133.9 0.3 shard_map.129
  134.2 2.4 collective-permute-start.8
  136.6 10.9 %all-gather.8 = f32[1408,128]{1,0:T(8,128)S(1)} all-gather(f32[352,128]{1,0:T(8,128)S(1)} %get-tuple-element.78), channel_id=10, replica_groups=mesh['z'=16,'y'=4,'h'=2,'l'=2,'c'=2] {'l','c'}, dimensions={0}, use_global_device_ids=true | all-gather | bytes 901120 | tf_op jit(solution)/shard_map/all_gather | solution.py:478
  147.5 0.9 shard_map.130
  148.4 23.0 %all_to_all.20 = f32[8,256,128]{2,1,0:T(8,128)S(1)} all-to-all(f32[8,256,128]{2,1,0:T(8,128)S(1)} %bitcast.59), channel_id=1, replica_groups=mesh['z'=16,'y'=4,'h'=2,'l'=2,'c'=2] {'y','h'}, dimensions={0} | all-to-all | bytes 2097152 | tf_op jit(solution)/shard_map/all_to_all | solution.py:481
  171.4 0.7 reduce_sum.18
  172.2 19.7 %all-to-all-start.1 = ((f32[16,16,128]{2,1,0:T(8,128)}), f32[16,16,128]{2,1,0:T(8,128)S(1)}, u32[]{:S(2)}, u32[]{:S(2)}) async-start(f32[16,16,128]{2,1,0:T(8,128)} %bitcast.31), calls=%async_computation.1 | async-start | bytes 262144 | tf_op jit(solution)/shard_map/all_to_all | solution.py:482
  191.9 3.3 %all-gather.9 = f32[704,128]{1,0:T(8,128)S(1)} all-gather(f32[352,128]{1,0:T(8,128)S(1)} %collective-permute-done.8), channel_id=11, replica_groups=mesh['z'=16,'y'=4,'h'=2,'l'=2,'c'=2] {'c'}, dimensions={0}, use_global_device_ids=true | all-gather | bytes 540672 | tf_op jit(solution)/shard_map/all_gather | solution.py:483
  195.2 0.4 shard_map.131
  195.6 8.3 %all-to-all-done.1 = f32[16,16,128]{2,1,0:T(8,128)S(1)} async-done(((f32[16,16,128]{2,1,0:T(8,128)}), f32[16,16,128]{2,1,0:T(8,128)S(1)}, u32[]{:S(2)}, u32[]{:S(2)}) %all-to-all-start.1) | async-done | bytes 131104 | tf_op jit(solution)/shard_map/all_to_all | solution.py:482
  203.9 0.7 broadcast_in_dim.36
  204.6 5.4 %all-to-all-start.2 = ((f32[16,16,128]{2,1,0:T(8,128)}), f32[16,16,128]{2,1,0:T(8,128)S(1)}, u32[]{:S(2)}, u32[]{:S(2)}) async-start(f32[16,16,128]{2,1,0:T(8,128)} %broadcast_in_dim.36), calls=%async_computation.2 | async-start | bytes 262144 | tf_op jit(solution)/shard_map/all_to_all | solution.py:486
  210.0 1.9 collective-permute-start.9
  211.9 8.8 %collective-permute-done.9.got_ref = f32[400,256]{1,0:T(8,128)S(1)} collective-permute-done((f32[400,256]{1,0:T(8,128)S(1)}, f32[400,256]{1,0:T(8,128)S(1)}, u32[]{:S(2)}, u32[]{:S(2)}) %collective-permute-start.9) | collective-permute-done | bytes 409632 | tf_op jit(solution)/shard_map/ppermute | solution.py:38
  220.8 1.2 all-to-all-done.2
  222.0 1.5 broadcast_in_dim.37
  223.5 3.7 %all-to-all-start.3 = ((f32[16,256,128]{2,1,0:T(8,128)}), f32[16,256,128]{2,1,0:T(8,128)S(1)}, u32[]{:S(2)}, u32[]{:S(2)}) async-start(f32[16,256,128]{2,1,0:T(8,128)} %broadcast_in_dim.37), calls=%async_computation.3 | async-start | bytes 4194304 | tf_op jit(solution)/shard_map/all_to_all | solution.py:489
  227.2 0.9 shard_map.132
  228.1 24.6 %all-to-all-done.3 = f32[16,256,128]{2,1,0:T(8,128)S(1)} async-done(((f32[16,256,128]{2,1,0:T(8,128)}), f32[16,256,128]{2,1,0:T(8,128)S(1)}, u32[]{:S(2)}, u32[]{:S(2)}) %all-to-all-start.3) | async-done | bytes 2097184 | tf_op jit(solution)/shard_map/all_to_all | solution.py:489
  252.7 6.2 %collective-permute-start.10 = (f32[2,2048,128]{2,1,0:T(8,128)S(1)}, f32[2,2048,128]{2,1,0:T(8,128)}, u32[]{:S(2)}, u32[]{:S(2)}) collective-permute-start(f32[2,2048,128]{2,1,0:T(8,128)S(1)} %bitcast.55), channel_id=1, source_target_pairs={{0,1},{1,0},{2,3},{3,2},{4,5},{5,4},{6,7},{7,6},{8,9},{9,8},{10,11... | collective-permute-start | bytes 6291464 | tf_op jit(solution)/shard_map/ppermute | solution.py:38
  258.9 2.2 copy-done
  261.0 1.7 shard_map.133
  262.7 2.8 %shard_map.134 = (f32[400,2560]{1,0:T(8,128)}, f32[20,128]{1,0:T(8,128)}) custom-call(s32[1]{0:T(128)} %bitcast.37.core_ref, f32[2,2048,128]{2,1,0:T(8,128)} %collective-permute-done.10.grad_ref, f32[400,2560]{1,0:T(8,128)S(1)} %bitcast.54, f32[20,128]{1,0:T(8,128)S(1)} %bitcast.74, ...), custom_call_target="tpu_custom_call", output_to_operand_aliasing={{0}: (4, {})} | custom-call | flops 5120000 | bytes 6291456 | tf_op jit(solution)/shard_map/pallas_call | solution.py:415
  (54 shorter events, 0.4 us)
Async XLA Ops:
  0.6 21.6 %copy-start.1 = (f32[256,400]{0,1:T(8,128)S(1)}, f32[256,400]{0,1:T(8,128)}, u32[]{:S(2)}) copy-start(f32[256,400]{0,1:T(8,128)} %param.9) | copy-start | bytes 1228804
  0.6 24.0 %copy-start.13 = (s32[1,2,1024]{2,1,0:T(2,128)S(1)}, s32[1,2,1024]{2,1,0:T(2,128)}, u32[]{:S(2)}) copy-start(s32[1,2,1024]{2,1,0:T(2,128)} %param.17) | copy-start | bytes 24580
  14.4 13.0 %collective-permute-start = (f32[400,256]{1,0:T(8,128)}, f32[400,256]{1,0:T(8,128)S(1)}, u32[]{:S(2)}, u32[]{:S(2)}) collective-permute-start(f32[400,256]{1,0:T(8,128)} %bitcast.66), channel_id=1, source_target_pairs={{0,2},{2,0},{1,3},{3,1},{4,6},{6,4},{5,7},{7,5},{8,10},{10,8},{9,1... | collective-permute-start | bytes 1228808 | tf_op jit(solution)/shard_map/ppermute | solution.py:38
  16.3 15.7 %copy-start.10 = (s32[1,512]{1,0:T(1,128)}, s32[1,512]{1,0:T(1,128)S(1)}, u32[]{:S(2)}) copy-start(s32[1,512]{1,0:T(1,128)S(1)} %get-tuple-element.105.ids_ref) | copy-start | bytes 6148
  30.4 0.9 copy-start.3
  32.0 27.0 %collective-permute-start.1 = (f32[368,128]{1,0:T(8,128)S(1)}, f32[368,128]{1,0:T(8,128)S(1)}, u32[]{:S(2)}, u32[]{:S(2)}) collective-permute-start(f32[368,128]{1,0:T(8,128)S(1)} %get-tuple-element.57), channel_id=1, source_target_pairs={{0,256},{32,288},{64,320},{96,352},{128,384},{160,416},{192,448},{... | collective-permute-start | bytes 565256 | tf_op jit(solution)/shard_map/ppermute | solution.py:38
  61.1 38.6 %copy-start.2 = (f32[2,400,256]{2,1,0:T(8,128)S(1)}, f32[2,400,256]{2,1,0:T(8,128)}, u32[]{:S(2)}) copy-start(f32[2,400,256]{2,1,0:T(8,128)} %shard_map.122.rel_ref) | copy-start | bytes 2457604
  61.1 38.6 %copy-start.12 = (f32[256]{0:T(256)S(1)}, f32[256]{0:T(256)}, u32[]{:S(2)}) copy-start(f32[256]{0:T(256)} %param.10) | copy-start | bytes 3076
  63.1 0.8 copy-start.4
  63.9 3.3 %collective-permute-start.2 = (f32[352,128]{1,0:T(8,128)S(1)}, f32[352,128]{1,0:T(8,128)S(1)}, u32[]{:S(2)}, u32[]{:S(2)}) collective-permute-start(f32[352,128]{1,0:T(8,128)S(1)} %get-tuple-element.62), channel_id=1, source_target_pairs={{0,1},{1,0},{2,3},{3,2},{4,5},{5,4},{6,7},{7,6},{8,9},{9,8},{10,11... | collective-permute-start | bytes 540680 | tf_op jit(solution)/shard_map/ppermute | solution.py:38
  67.2 8.5 %collective-permute-start.3 = (s32[16,128]{1,0:T(8,128)S(1)}, s32[16,128]{1,0:T(8,128)S(1)}, u32[]{:S(2)}, u32[]{:S(2)}) collective-permute-start(s32[16,128]{1,0:T(8,128)S(1)} %pad_add_fusion.1), channel_id=1, source_target_pairs={{0,4},{4,0},{1,5},{5,1},{2,6},{6,2},{3,7},{7,3},{8,12},{12,8},{9,1... | collective-permute-start | bytes 24584 | tf_op jit(solution)/shard_map/ppermute | solution.py:38
  71.6 18.1 %collective-permute-start.5 = (f32[400,256]{1,0:T(8,128)S(1)}, f32[400,256]{1,0:T(8,128)S(1)}, u32[]{:S(2)}, u32[]{:S(2)}) collective-permute-start(f32[400,256]{1,0:T(8,128)S(1)} %get-tuple-element.65), channel_id=1, source_target_pairs={{0,2},{2,0},{1,3},{3,1},{4,6},{6,4},{5,7},{7,5},{8,10},{10,8},{9,1... | collective-permute-start | bytes 1228808 | tf_op jit(solution)/shard_map/ppermute | solution.py:38
  73.8 16.0 %collective-permute-start.4 = (f32[352,128]{1,0:T(8,128)S(1)}, f32[352,128]{1,0:T(8,128)S(1)}, u32[]{:S(2)}, u32[]{:S(2)}) collective-permute-start(f32[352,128]{1,0:T(8,128)S(1)} %add.22), channel_id=1, source_target_pairs={{0,256},{32,288},{64,320},{96,352},{128,384},{160,416},{192,448},{... | collective-permute-start | bytes 540680 | tf_op jit(solution)/shard_map/ppermute | solution.py:38
  75.7 24.0 %copy-start.5 = (f32[400,256]{1,0:T(8,128)S(1)}, f32[400,256]{1,0:T(8,128)}, u32[]{:S(2)}) copy-start(f32[400,256]{1,0:T(8,128)} %copy-done.4) | copy-start | bytes 1228804
  76.3 27.4 %copy-start.11 = (s32[1,512]{1,0:T(1,128)S(1)}, s32[1,512]{1,0:T(1,128)}, u32[]{:S(2)}) copy-start(s32[1,512]{1,0:T(1,128)} %copy-done.10) | copy-start | bytes 6148
  89.7 10.0 %copy-start.6 = (f32[400,256]{1,0:T(8,128)}, f32[400,256]{1,0:T(8,128)S(1)}, u32[]{:S(2)}) copy-start(f32[400,256]{1,0:T(8,128)S(1)} %collective-permute-done.5.got_ref) | copy-start | bytes 1228804
  99.8 1.0 copy-start.7
  101.4 26.5 %copy-start.8 = (f32[1,400,256]{2,1,0:T(8,128)S(1)}, f32[1,400,256]{2,1,0:T(8,128)}, u32[]{:S(2)}) copy-start(f32[1,400,256]{2,1,0:T(8,128)} %shard_map.124.rel_ref) | copy-start | bytes 1228804
  101.4 12.9 %collective-permute-start.6 = (f32[400,256]{1,0:T(8,128)S(1)}, f32[400,256]{1,0:T(8,128)S(1)}, u32[]{:S(2)}, u32[]{:S(2)}) collective-permute-start(f32[400,256]{1,0:T(8,128)S(1)} %get-tuple-element.70.own_ref), channel_id=1, source_target_pairs={{0,2},{2,0},{1,3},{3,1},{4,6},{6,4},{5,7},{7,5},{8,10},{10,8},{9,1... | collective-permute-start | bytes 1228808 | tf_op jit(solution)/shard_map/ppermute | solution.py:38
  130.6 3.3 %collective-permute-start.7 = (f32[352,128]{1,0:T(8,128)S(1)}, f32[352,128]{1,0:T(8,128)S(1)}, u32[]{:S(2)}, u32[]{:S(2)}) collective-permute-start(f32[352,128]{1,0:T(8,128)S(1)} %get-tuple-element.75), channel_id=1, source_target_pairs={{0,1},{1,0},{2,3},{3,2},{4,5},{5,4},{6,7},{7,6},{8,9},{9,8},{10,11... | collective-permute-start | bytes 540680 | tf_op jit(solution)/shard_map/ppermute | solution.py:38
  134.2 13.3 %collective-permute-start.8 = (f32[352,128]{1,0:T(8,128)S(1)}, f32[352,128]{1,0:T(8,128)S(1)}, u32[]{:S(2)}, u32[]{:S(2)}) collective-permute-start(f32[352,128]{1,0:T(8,128)S(1)} %get-tuple-element.79), channel_id=1, source_target_pairs={{0,4},{4,0},{1,5},{5,1},{2,6},{6,2},{3,7},{7,3},{8,12},{12,8},{9,1... | collective-permute-start | bytes 540680 | tf_op jit(solution)/shard_map/ppermute | solution.py:38
  172.2 31.7 %all-to-all-start.1 = ((f32[16,16,128]{2,1,0:T(8,128)}), f32[16,16,128]{2,1,0:T(8,128)S(1)}, u32[]{:S(2)}, u32[]{:S(2)}) async-start(f32[16,16,128]{2,1,0:T(8,128)} %bitcast.31), calls=%async_computation.1 | async-start | bytes 262144 | tf_op jit(solution)/shard_map/all_to_all | solution.py:482
  203.9 55.0 %copy-start.9 = (f32[2560]{0:T(1024)S(1)}, f32[2560]{0:T(1024)}, u32[]{:S(2)}) copy-start(f32[2560]{0:T(1024)} %param.12) | copy-start | bytes 30724
  204.6 17.4 %all-to-all-start.2 = ((f32[16,16,128]{2,1,0:T(8,128)}), f32[16,16,128]{2,1,0:T(8,128)S(1)}, u32[]{:S(2)}, u32[]{:S(2)}) async-start(f32[16,16,128]{2,1,0:T(8,128)} %broadcast_in_dim.36), calls=%async_computation.2 | async-start | bytes 262144 | tf_op jit(solution)/shard_map/all_to_all | solution.py:486
  210.0 10.8 %collective-permute-start.9 = (f32[400,256]{1,0:T(8,128)S(1)}, f32[400,256]{1,0:T(8,128)S(1)}, u32[]{:S(2)}, u32[]{:S(2)}) collective-permute-start(f32[400,256]{1,0:T(8,128)S(1)} %get-tuple-element.88), channel_id=1, source_target_pairs={{0,2},{2,0},{1,3},{3,1},{4,6},{6,4},{5,7},{7,5},{8,10},{10,8},{9,1... | collective-permute-start | bytes 1228808 | tf_op jit(solution)/shard_map/ppermute | solution.py:38
  223.5 29.2 %all-to-all-start.3 = ((f32[16,256,128]{2,1,0:T(8,128)}), f32[16,256,128]{2,1,0:T(8,128)S(1)}, u32[]{:S(2)}, u32[]{:S(2)}) async-start(f32[16,256,128]{2,1,0:T(8,128)} %broadcast_in_dim.37), calls=%async_computation.3 | async-start | bytes 4194304 | tf_op jit(solution)/shard_map/all_to_all | solution.py:489
  252.7 10.1 %collective-permute-start.10 = (f32[2,2048,128]{2,1,0:T(8,128)S(1)}, f32[2,2048,128]{2,1,0:T(8,128)}, u32[]{:S(2)}, u32[]{:S(2)}) collective-permute-start(f32[2,2048,128]{2,1,0:T(8,128)S(1)} %bitcast.55), channel_id=1, source_target_pairs={{0,1},{1,0},{2,3},{3,2},{4,5},{5,4},{6,7},{7,6},{8,9},{9,8},{10,11... | collective-permute-start | bytes 6291464 | tf_op jit(solution)/shard_map/ppermute | solution.py:38
  258.8 2.2 copy-start

commit v4 on v3

--- a/solution.py
+++ b/solution.py
@@ -160,9 +160,17 @@
     pack(out_ref, chunk_rows(s_ref[0], ids_ref[...], near_ref, far_ref))
 
 
-def letter_kernel(s_ref, ids_ref, near_ref, far_ref, rel_ref, target_ref, neg_ref, head_ref, out_ref, work_ref, a_ref):
-    a_ref[...] = chunk_rows(s_ref[0], ids_ref[...], near_ref, far_ref)
-    pack(head_ref, a_ref[...])
+def halves_kernel(s_ref, ids_ref, near_ref, mine_ref, theirs_ref):
+    first = s_ref[0] & 2
+    rows = [split(near_ref[k]) for k in range(2)]
+    for which, out_ref in enumerate((mine_ref, theirs_ref)):
+        ids = ids_ref[which : which + 1, :]
+        pack(out_ref, sum(dot2(rows[k], hot(ROWS, ids, ROWS * (first + k)), (1, 0)) for k in range(2)))
+
+
+def letter_kernel(s_ref, mine_ref, got_ref, rel_ref, target_ref, neg_ref, head_ref, out_ref, work_ref, a_ref):
+    head_ref[...] = mine_ref[...] + got_ref[...]
+    unpack(a_ref, EVERY, head_ref[...])
     times(work_ref, EVERY, a_ref[:HALF, :], a_ref[HALF:, :], rel_ref[0, :HALF, :], rel_ref[0, HALF:, :])
     pack(out_ref, work_ref[...])
     out_ref[SENT : SENT + 8, :] = jnp.broadcast_to(target_ref[...], (8, CHUNK)).astype(F32)
@@ -177,15 +185,24 @@
     return call(heads_kernel, shape(SENT, CHUNK), HEADS_IN, whole(SENT, CHUNK), [], *HEADS_COST)(s, ids, near, far)
 
 
-def letter(s, ids, near, far, rel_rows, target, negatives):
+def halves(s, ids, near):
+    sent = whole(SENT, CHUNK)
+    return call(halves_kernel, [shape(SENT, CHUNK)] * 2, [whole(2, CHUNK), whole(2, D, ROWS)], [sent] * 2, [], *HEADS_COST)(
+        s, ids, near
+    )
+
+
+def letter(s, mine, got, rel_rows, target, negatives):
+    sent = whole(SENT, CHUNK)
     return call(
         letter_kernel,
         [shape(SENT, CHUNK), shape(LETTER, CHUNK)],
-        HEADS_IN + [whole(1, D, CHUNK), whole(1, CHUNK), whole(8, 128)],
-        [whole(SENT, CHUNK), whole(LETTER, CHUNK)],
+        [sent, sent, whole(1, D, CHUNK), whole(1, CHUNK), whole(8, 128)],
+        [sent, whole(LETTER, CHUNK)],
         [WORK] * 2,
-        *HEADS_COST,
-    )(s, ids, near, far, rel_rows, target, negatives)
+        10 * D * CHUNK,
+        20 * D * CHUNK,
+    )(s, mine, got, rel_rows, target, negatives)
 
 
 def weigh(s_ref, h_ref, target, negatives, own_ref, other_ref, keep_ref, send_ref, grad_ref, grad_send_ref):
@@ -444,41 +461,41 @@
     table = relations.T
     pick = lambda lists, rows, at: lax.dynamic_slice_in_dim(lists.reshape(rows, -1), at, 1, 0)
 
+    near = lax.all_gather(own, "c", axis=0)
     slots = slot_lists(src_rows, rel_ids, dst_rows, live_count)
-    own, slots = tied((own, slots))
+    chunk_ids, chunk_kinds, chunk_targets = [pick(slots[k], 4, place) for k in range(3)]
+    mine, theirs = halves(s, jnp.concatenate([chunk_ids, pick(slots[0], 4, place ^ 2)]), near)
+    chunk_rel = lookup(s, chunk_kinds[None], table)
+    head, mail = letter(s, mine, flip(theirs, "l"), chunk_rel, chunk_targets, neg_rows[0, 0].reshape(8, 128))
+    mail, head, own, bucket_kinds = tied((mail, head, own, slots[1]))
     other = flip(own, "l")
-    near = lax.all_gather(own, "c", axis=0)
-    chunk_ids, chunk_kinds, chunk_targets = [pick(slots[k], 4, place) for k in range(3)]
-    chunk_rel = lookup(s, chunk_kinds[None], table)
-    far = lax.all_gather(other, "c", axis=0)
-    head, mail = letter(s, chunk_ids, near, far, chunk_rel, chunk_targets, neg_rows[0, 0].reshape(8, 128))
-    mail, head, bucket_kinds = tied((mail, head, slots[1]))
     rel_rows = lookup(s, bucket_kinds.reshape(2, 1, PAIR), table)
-    mail, head_rows, rel_rows = tied((flip(mail, "z", 8), lax.all_gather(head, REL, axis=0), rel_rows))
+    mail, other, rel_rows = tied((flip(mail, "z", 8), other, rel_rows))
     keep, send, grad, grad_send = answer(s, lax.all_gather(mail, "c", axis=0), own, other)
     reply = keep + flip(send, "c")
+    reply, head = tied((reply, head))
+    head_rows = lax.all_gather(head, REL, axis=0)
     sent = jnp.concatenate([slots[4:6].reshape(8, 128), neg_rows[0, 1].reshape(8, 128)], axis=0)
-    reply, sent = tied((reply, sent))
-    got = flip(sent, "h")
+    head_rows, sent = tied((head_rows, sent))
+    reply, grad_got, got = tied((flip(reply, "z", 8), flip(grad_send, "l"), flip(sent, "h")))
     kind_ids, target_ids, negatives = got[:4].reshape(1, SLOTS), got[4:8], got[8:]
-    later_rows = lookup(s, pick(kind_ids, 2, chip)[None], table)
-    reply, grad_got, later_rows = tied((flip(reply, "z", 8), flip(grad_send, "l"), later_rows))
     answers = lax.all_gather(reply, REL, axis=0)
     own, state = update_answered(s, slots[0:1], answers, rel_rows, grad, grad_got, own, state)
     total = kinds_answered(s, slots[1:2], answers, head_rows)
 
     other = flip(own, "l")
     near = lax.all_gather(own, "c", axis=0)
-    other, total = tied((other, total))
+    later_rows = lookup(s, pick(kind_ids, 2, chip)[None], table)
+    other, total, later_rows = tied((other, total, later_rows))
     chunk = heads(s, pick(slots[3], 4, place), near, lax.all_gather(other, "c", axis=0))
     head_rows = lax.all_gather(chunk, ("h", "c"), axis=0)
     beyond = jnp.stack([place, 2 * (1 - side)])
     keep, send, grad, grad_send, head, kind = score(beyond, pick(target_ids, 2, chip), negatives, head_rows, later_rows, own, other)
     d_head, d_kind = chunk_back(s, keep, flip(send, "c"), head, kind)
-    d_kinds, d_head = tied((lax.all_gather(d_kind, REL, axis=0), flip(d_head, "h")))
-    total = kinds(s, kind_ids, d_kinds, total)
-
-    shares = lax.all_to_all(total.reshape(8, 256, 128), SPREAD, 0, 0)
+    total = kinds(s, kind_ids, lax.all_gather(d_kind, REL, axis=0), total)
+
+    total, d_head = tied((total, d_head))
+    shares, d_head = tied((lax.all_to_all(total.reshape(8, 256, 128), SPREAD, 0, 0), flip(d_head, "h")))
     pieces = lax.all_to_all(jnp.sum(shares, axis=0).reshape(16, 16, 128), "z", 0, 0)
     grad, grad_send = join(s, pick(slots[3], 2, chip), lax.all_gather(d_head, "c", axis=0), grad, grad_send)
     pieces, grad, grad_send = tied((pieces, grad, grad_send))

time: 267 us -> 259 us (0.970)
  blocking collectives: 90.5 us -> 62.7 us
  starting transfers between devices: 66.1 us -> 88.4 us
    all_to_all x1 -> x0, blocking collectives: 23 us -> none  [local(): shares = lax.all_to_all(total.reshape(8, 256, 128), SPREAD, 0, 0)]
    ppermute x11 -> x12, starting transfers between devices: 37.3 us -> 51.4 us  [flip(): return lax.ppermute(block, axis, [(i, i ^ mask) for i in range(count)])]
    all_gather x3 -> x2, blocking collectives: 22.6 us -> 17.4 us  [the longest x1 9.04 us: local(): head_rows = lax.all_gather(head, REL, axis=0)]
    all_to_all x0 -> x1, starting transfers between devices: none -> 4.8 us  [local(): lax.all_to_all(total.reshape(8, 256, 128), SPREAD, 0, 0)]
    all_to_all x1, starting transfers between devices: 19.7 us -> 22.4 us  [local(): lax.all_to_all(jnp.sum(shares, axis=0).reshape(16, 16, 128), 'z', 0, 0)]
    ppermute x11 -> x12, waiting for transfers between devices: 28.9 us -> 26.5 us  [flip(): return lax.ppermute(block, axis, [(i, i ^ mask) for i in range(count)])]
  transfers between devices with their start and end apart: 14 -> 16, of which waited for: 9 -> 8; matrix products, arithmetic and copies ran while one was open for 0% -> 0% of each run, Pallas kernels for 9% -> 9%
where the time goes in v4:
time: 259 us; the launch traced here: 258 us
  starting transfers between devices  88.4 us (34%)
  blocking collectives  62.7 us (24%)
  waiting for transfers between devices  60.5 us (23%)
  Pallas kernels  35.8 us (14%)
  local copies, waits for them, and re-layouts  7.27 us (3%)
    ppermute x12, starting transfers between devices, flip(): return lax.ppermute(block, axis, [(i, i ^ mask) for i in range(count)])  51.4 us
    ppermute x12, waiting for transfers between devices, flip(): return lax.ppermute(block, axis, [(i, i ^ mask) for i in range(count)])  26.5 us
    all_to_all x1, waiting for transfers between devices, local(): lax.all_to_all(jnp.broadcast_to(share[None], (16, 256, 128)), ('l',) + SP...  24.6 us
    all_to_all x1, starting transfers between devices, local(): lax.all_to_all(jnp.sum(shares, axis=0).reshape(16, 16, 128), 'z', 0, 0)  22.4 us
    pallas_call x3, Pallas kernels, lookup(): call(lookup_kernel, shape(lists, D, width), [whole(lists, 1, width), pl.B...  19.1 us
    all_gather x1, blocking collectives, slot_lists(): lax.all_gather(lists.reshape(12, 128), REL, axis=0).reshape(4, 6, CAP)  11.9 us
    all_gather x1, blocking collectives, local(): head_rows = lax.all_gather(chunk, ('h', 'c'), axis=0)  9.87 us
    all_gather x1, blocking collectives, local(): head_rows = lax.all_gather(head, REL, axis=0)  9.04 us
  transfers between devices with their start and end apart: 16, of which 8 were waited for; matrix products, arithmetic and copies ran while one was open for 0% of the time, Pallas kernels for 9%

profile of v4, /device:TPU:1, one launch (start us, length us, event | category | flops | bytes accessed | tf_op | source)
XLA Modules:
  0.0 258.0 jit_solution(5419817641723959912)
XLA Ops:
  0.7 0.8 iota_compare_fusion
  1.4 0.7 add_select_fusion
  2.2 11.9 %all_gather.57 = s32[4,12,128]{2,1,0:T(8,128)S(1)} all-gather(s32[1,12,128]{2,1,0:T(8,128)S(1)} %select_n.34), channel_id=1, replica_groups=mesh['z'=16,'y'=4,'h'=2,'l'=2,'c'=2] {'l','c'}, dimensions={0}, use_global_device_ids=true | all-gather | bytes 30720 | tf_op jit(solution)/shard_map/all_gather | solution.py:449
  14.1 0.1 slice_reduce_fusion
  14.2 0.1 reshape.126
  14.3 0.1 reshape.127
  14.3 0.6 pad_slice_fusion
  14.9 2.6 %all-gather = f32[800,256]{1,0:T(8,128)S(1)} all-gather(f32[400,256]{1,0:T(8,128)} %bitcast.64), channel_id=2, replica_groups=mesh['z'=16,'y'=4,'h'=2,'l'=2,'c'=2] {'c'}, dimensions={0}, use_global_device_ids=true | all-gather | bytes 1228800 | tf_op jit(solution)/shard_map/all_gather | solution.py:464
  17.5 0.7 shard_map.120
  18.3 1.9 collective-permute-start
  20.2 0.5 constant_dynamic-slice_fusion.5.ids_ref
  20.8 5.4 %shard_map.121.rel_ref = f32[1,400,128]{2,1,0:T(8,128)} custom-call(s32[1]{0:T(128)} %bitcast.s_ref, s32[1,1,128]{2,1,0:T(1,128)} %constant_dynamic-slice_fusion.5.ids_ref, f32[400,2560]{1,0:T(8,128)} %bitcast.50), custom_call_target="tpu_custom_call" | custom-call | flops 524288000 | bytes 5242880 | tf_op jit(solution)/shard_map/pallas_call | solution.py:137
  26.2 0.9 copy-done.3
  27.1 0.2 shard_map.122
  27.4 3.4 %collective-permute-start.2 = (f32[400,256]{1,0:T(8,128)S(1)}, f32[400,256]{1,0:T(8,128)S(1)}, u32[]{:S(2)}, u32[]{:S(2)}) collective-permute-start(f32[400,256]{1,0:T(8,128)S(1)} %bitcast.65), channel_id=1, source_target_pairs={{0,2},{2,0},{1,3},{3,1},{4,6},{6,4},{5,7},{7,5},{8,10},{10,8},{9,1... | collective-permute-start | bytes 1228808 | tf_op jit(solution)/shard_map/ppermute | solution.py:38
  30.7 10.1 %collective-permute-start.1 = (f32[368,128]{1,0:T(8,128)S(1)}, f32[368,128]{1,0:T(8,128)S(1)}, u32[]{:S(2)}, u32[]{:S(2)}) collective-permute-start(f32[368,128]{1,0:T(8,128)S(1)} %get-tuple-element.63), channel_id=1, source_target_pairs={{0,256},{32,288},{64,320},{96,352},{128,384},{160,416},{192,448},{... | collective-permute-start | bytes 565256 | tf_op jit(solution)/shard_map/ppermute | solution.py:38
  40.8 8.2 %shard_map.123.rel_ref = f32[2,400,256]{2,1,0:T(8,128)} custom-call(s32[1]{0:T(128)} %bitcast.s_ref, s32[2,1,256]{2,1,0:T(1,128)} %bitcast.85, f32[400,2560]{1,0:T(8,128)} %bitcast.51), custom_call_target="tpu_custom_call" | custom-call | flops 2097152000 | bytes 5242880 | tf_op jit(solution)/shard_map/pallas_call | solution.py:137
  49.0 3.1 %all-gather.1 = f32[736,128]{1,0:T(8,128)S(1)} all-gather(f32[368,128]{1,0:T(8,128)S(1)} %collective-permute-done.1), channel_id=3, replica_groups=mesh['z'=16,'y'=4,'h'=2,'l'=2,'c'=2] {'c'}, dimensions={0}, use_global_device_ids=true | all-gather | bytes 565248 | tf_op jit(solution)/shard_map/all_gather | solution.py:474
  52.2 2.7 %shard_map.124 = (f32[352,128]{1,0:T(8,128)S(1)}, f32[352,128]{1,0:T(8,128)S(1)}, f32[400,256]{1,0:T(8,128)S(1)}, f32[400,256]{1,0:T(8,128)}) custom-call(s32[1]{0:T(128)} %bitcast.s_ref, f32[2,368,128]{2,1,0:T(8,128)S(1)} %bitcast.70, f32[400,256]{1,0:T(8,128)S(1)} %bitcast.66, f32[400,256]{1,0:T(8,128)S(1)} %collective-permute-done.2.other_ref), custom_call_target="tpu_custom_call" | custom-call | flops 1073741824 | bytes 5242880 | tf_op jit(solution)/shard_map/pallas_call | solution.py:244
  54.8 2.3 collective-permute-start.3
  57.1 2.8 %collective-permute-start.5 = (f32[400,256]{1,0:T(8,128)}, f32[400,256]{1,0:T(8,128)S(1)}, u32[]{:S(2)}, u32[]{:S(2)}) collective-permute-start(f32[400,256]{1,0:T(8,128)} %get-tuple-element.72), channel_id=1, source_target_pairs={{0,2},{2,0},{1,3},{3,1},{4,6},{6,4},{5,7},{7,5},{8,10},{10,8},{9,1... | collective-permute-start | bytes 1228808 | tf_op jit(solution)/shard_map/ppermute | solution.py:38
  60.0 0.1 pad_add_fusion.3.s_ref
  60.1 9.5 %collective-permute-start.4 = (f32[352,128]{1,0:T(8,128)S(1)}, f32[352,128]{1,0:T(8,128)S(1)}, u32[]{:S(2)}, u32[]{:S(2)}) collective-permute-start(f32[352,128]{1,0:T(8,128)S(1)} %add.26), channel_id=1, source_target_pairs={{0,256},{32,288},{64,320},{96,352},{128,384},{160,416},{192,448},{... | collective-permute-start | bytes 540680 | tf_op jit(solution)/shard_map/ppermute | solution.py:38
  69.5 9.0 %all-gather.2 = f32[1408,128]{1,0:T(8,128)S(1)} all-gather(f32[352,128]{1,0:T(8,128)S(1)} %get-tuple-element.73), channel_id=4, replica_groups=mesh['z'=16,'y'=4,'h'=2,'l'=2,'c'=2] {'l','c'}, dimensions={0}, use_global_device_ids=true | all-gather | bytes 901120 | tf_op jit(solution)/shard_map/all_gather | solution.py:477
  78.6 2.9 %collective-permute-start.6 = (s32[16,128]{1,0:T(8,128)S(1)}, s32[16,128]{1,0:T(8,128)S(1)}, u32[]{:S(2)}, u32[]{:S(2)}) collective-permute-start(s32[16,128]{1,0:T(8,128)S(1)} %pad_add_fusion.1), channel_id=1, source_target_pairs={{0,4},{4,0},{1,5},{5,1},{2,6},{6,2},{3,7},{7,3},{8,12},{12,8},{9,1... | collective-permute-start | bytes 24584 | tf_op jit(solution)/shard_map/ppermute | solution.py:38
  81.5 3.0 %collective-permute-done.6 = s32[16,128]{1,0:T(8,128)S(1)} collective-permute-done((s32[16,128]{1,0:T(8,128)S(1)}, s32[16,128]{1,0:T(8,128)S(1)}, u32[]{:S(2)}, u32[]{:S(2)}) %collective-permute-start.6) | collective-permute-done | bytes 8224 | tf_op jit(solution)/shard_map/ppermute | solution.py:38
  84.5 9.0 %all-gather.3 = f32[1408,128]{1,0:T(8,128)S(1)} all-gather(f32[352,128]{1,0:T(8,128)S(1)} %collective-permute-done.4), channel_id=5, replica_groups=mesh['z'=16,'y'=4,'h'=2,'l'=2,'c'=2] {'l','c'}, dimensions={0}, use_global_device_ids=true | all-gather | bytes 901120 | tf_op jit(solution)/shard_map/all_gather | solution.py:482
  93.5 0.6 shard_map.125
  94.1 2.6 %collective-permute-start.7 = (f32[400,256]{1,0:T(8,128)S(1)}, f32[400,256]{1,0:T(8,128)S(1)}, u32[]{:S(2)}, u32[]{:S(2)}) collective-permute-start(f32[400,256]{1,0:T(8,128)S(1)} %get-tuple-element.80.own_ref), channel_id=1, source_target_pairs={{0,2},{2,0},{1,3},{3,1},{4,6},{6,4},{5,7},{7,5},{8,10},{10,8},{9,1... | collective-permute-start | bytes 1228808 | tf_op jit(solution)/shard_map/ppermute | solution.py:38
  96.7 0.6 fusion.ids_ref
  97.3 1.2 shard_map.126.before_ref
  98.5 5.5 %shard_map.127.rel_ref = f32[1,400,256]{2,1,0:T(8,128)} custom-call(s32[1]{0:T(128)} %bitcast.s_ref, s32[1,1,256]{2,1,0:T(1,128)} %fusion.ids_ref, f32[400,2560]{1,0:T(8,128)} %bitcast.52), custom_call_target="tpu_custom_call" | custom-call | flops 1048576000 | bytes 5242880 | tf_op jit(solution)/shard_map/pallas_call | solution.py:137
  104.0 2.6 %all-gather.4 = f32[800,256]{1,0:T(8,128)S(1)} all-gather(f32[400,256]{1,0:T(8,128)S(1)} %get-tuple-element.80.own_ref), channel_id=6, replica_groups=mesh['z'=16,'y'=4,'h'=2,'l'=2,'c'=2] {'c'}, dimensions={0}, use_global_device_ids=true | all-gather | bytes 1228800 | tf_op jit(solution)/shard_map/all_gather | solution.py:487
  106.6 0.4 collective-permute-done.7.other_ref
  106.9 3.0 %all-gather.5 = f32[800,256]{1,0:T(8,128)S(1)} all-gather(f32[400,256]{1,0:T(8,128)S(1)} %collective-permute-done.7.other_ref), channel_id=7, replica_groups=mesh['z'=16,'y'=4,'h'=2,'l'=2,'c'=2] {'c'}, dimensions={0}, use_global_device_ids=true | all-gather | bytes 1228800 | tf_op jit(solution)/shard_map/all_gather | solution.py:490
  109.9 0.7 shard_map.128
  110.6 9.9 %all-gather.6 = f32[1408,128]{1,0:T(8,128)S(1)} all-gather(f32[352,128]{1,0:T(8,128)S(1)} %shard_map.128), channel_id=8, replica_groups=mesh['z'=16,'y'=4,'h'=2,'l'=2,'c'=2] {'h','c'}, dimensions={0}, use_global_device_ids=true | all-gather | bytes 901120 | tf_op jit(solution)/shard_map/all_gather | solution.py:491
  120.5 2.7 %shard_map.129 = (f32[352,128]{1,0:T(8,128)S(1)}, f32[352,128]{1,0:T(8,128)S(1)}, f32[400,256]{1,0:T(8,128)S(1)}, f32[400,256]{1,0:T(8,128)S(1)}, f32[400,128]{1,0:T(8,128)S(1)}, /*index=5*/f32[400,128]{1,0:T(8,128)S(1)}) custom-call(s32[2]{0:T(128)S(1)} %pad_add_fusion.3.s_ref, s32[1,256]{1,0:T(1,128)S(1)} %constant_dynamic-slice_fusion.3.target_ref, ...), custom_call_target="tpu_custom_call" | custom-call | flops 1073741824 | bytes 5242880 | tf_op jit(solution)/shard_map/pallas_call | solution.py:269
  123.1 2.1 collective-permute-start.8
  125.2 1.2 collective-permute-done.8.got_ref
  126.5 0.3 shard_map.130
  126.7 8.4 %all-gather.7 = f32[1408,128]{1,0:T(8,128)S(1)} all-gather(f32[352,128]{1,0:T(8,128)S(1)} %get-tuple-element.88), channel_id=9, replica_groups=mesh['z'=16,'y'=4,'h'=2,'l'=2,'c'=2] {'l','c'}, dimensions={0}, use_global_device_ids=true | all-gather | bytes 901120 | tf_op jit(solution)/shard_map/all_gather | solution.py:495
  135.1 1.9 shard_map.131
  137.0 4.8 %all-to-all-start = ((f32[8,256,128]{2,1,0:T(8,128)}), f32[8,256,128]{2,1,0:T(8,128)S(1)}, u32[]{:S(2)}, u32[]{:S(2)}) async-start(f32[8,256,128]{2,1,0:T(8,128)} %bitcast.31), calls=%async_computation | async-start | bytes 2097152 | tf_op jit(solution)/shard_map/all_to_all | solution.py:498
  141.8 4.9 %collective-permute-start.9 = (f32[352,128]{1,0:T(8,128)S(1)}, f32[352,128]{1,0:T(8,128)S(1)}, u32[]{:S(2)}, u32[]{:S(2)}) collective-permute-start(f32[352,128]{1,0:T(8,128)S(1)} %get-tuple-element.92), channel_id=1, source_target_pairs={{0,4},{4,0},{1,5},{5,1},{2,6},{6,2},{3,7},{7,3},{8,12},{12,8},{9,1... | collective-permute-start | bytes 540680 | tf_op jit(solution)/shard_map/ppermute | solution.py:38
  146.6 13.8 %collective-permute-done.9 = f32[352,128]{1,0:T(8,128)S(1)} collective-permute-done((f32[352,128]{1,0:T(8,128)S(1)}, f32[352,128]{1,0:T(8,128)S(1)}, u32[]{:S(2)}, u32[]{:S(2)}) %collective-permute-start.9) | collective-permute-done | bytes 180256 | tf_op jit(solution)/shard_map/ppermute | solution.py:38
  160.4 0.7 reduce_sum.18
  161.1 22.4 %all-to-all-start.1 = ((f32[16,16,128]{2,1,0:T(8,128)}), f32[16,16,128]{2,1,0:T(8,128)S(1)}, u32[]{:S(2)}, u32[]{:S(2)}) async-start(f32[16,16,128]{2,1,0:T(8,128)} %bitcast.32), calls=%async_computation.1 | async-start | bytes 262144 | tf_op jit(solution)/shard_map/all_to_all | solution.py:499
  183.5 3.3 %all-gather.8 = f32[704,128]{1,0:T(8,128)S(1)} all-gather(f32[352,128]{1,0:T(8,128)S(1)} %collective-permute-done.9), channel_id=10, replica_groups=mesh['z'=16,'y'=4,'h'=2,'l'=2,'c'=2] {'c'}, dimensions={0}, use_global_device_ids=true | all-gather | bytes 540672 | tf_op jit(solution)/shard_map/all_gather | solution.py:500
  186.8 0.4 shard_map.132
  187.2 8.3 %all-to-all-done.1 = f32[16,16,128]{2,1,0:T(8,128)S(1)} async-done(((f32[16,16,128]{2,1,0:T(8,128)}), f32[16,16,128]{2,1,0:T(8,128)S(1)}, u32[]{:S(2)}, u32[]{:S(2)}) %all-to-all-start.1) | async-done | bytes 131104 | tf_op jit(solution)/shard_map/all_to_all | solution.py:499
  195.5 0.7 broadcast_in_dim.33
  196.2 5.4 %all-to-all-start.2 = ((f32[16,16,128]{2,1,0:T(8,128)}), f32[16,16,128]{2,1,0:T(8,128)S(1)}, u32[]{:S(2)}, u32[]{:S(2)}) async-start(f32[16,16,128]{2,1,0:T(8,128)} %broadcast_in_dim.33), calls=%async_computation.2 | async-start | bytes 262144 | tf_op jit(solution)/shard_map/all_to_all | solution.py:503
  201.6 2.7 %collective-permute-start.10 = (f32[400,256]{1,0:T(8,128)S(1)}, f32[400,256]{1,0:T(8,128)S(1)}, u32[]{:S(2)}, u32[]{:S(2)}) collective-permute-start(f32[400,256]{1,0:T(8,128)S(1)} %get-tuple-element.100), channel_id=1, source_target_pairs={{0,2},{2,0},{1,3},{3,1},{4,6},{6,4},{5,7},{7,5},{8,10},{10,8},{9,1... | collective-permute-start | bytes 1228808 | tf_op jit(solution)/shard_map/ppermute | solution.py:38
  204.3 8.1 %collective-permute-done.10.got_ref = f32[400,256]{1,0:T(8,128)S(1)} collective-permute-done((f32[400,256]{1,0:T(8,128)S(1)}, f32[400,256]{1,0:T(8,128)S(1)}, u32[]{:S(2)}, u32[]{:S(2)}) %collective-permute-start.10) | collective-permute-done | bytes 409632 | tf_op jit(solution)/shard_map/ppermute | solution.py:38
  212.4 1.2 all-to-all-done.2
  213.6 1.5 broadcast_in_dim.34
  215.1 4.4 %all-to-all-start.3 = ((f32[16,256,128]{2,1,0:T(8,128)}), f32[16,256,128]{2,1,0:T(8,128)S(1)}, u32[]{:S(2)}, u32[]{:S(2)}) async-start(f32[16,256,128]{2,1,0:T(8,128)} %broadcast_in_dim.34), calls=%async_computation.3 | async-start | bytes 4194304 | tf_op jit(solution)/shard_map/all_to_all | solution.py:506
  219.5 0.9 shard_map.133
  220.4 24.6 %all-to-all-done.3 = f32[16,256,128]{2,1,0:T(8,128)S(1)} async-done(((f32[16,256,128]{2,1,0:T(8,128)}), f32[16,256,128]{2,1,0:T(8,128)S(1)}, u32[]{:S(2)}, u32[]{:S(2)}) %all-to-all-start.3) | async-done | bytes 2097184 | tf_op jit(solution)/shard_map/all_to_all | solution.py:506
  245.0 6.4 %collective-permute-start.11 = (f32[2,2048,128]{2,1,0:T(8,128)S(1)}, f32[2,2048,128]{2,1,0:T(8,128)}, u32[]{:S(2)}, u32[]{:S(2)}) collective-permute-start(f32[2,2048,128]{2,1,0:T(8,128)S(1)} %bitcast.55), channel_id=1, source_target_pairs={{0,1},{1,0},{2,3},{3,2},{4,5},{5,4},{6,7},{7,6},{8,9},{9,8},{10,11... | collective-permute-start | bytes 6291464 | tf_op jit(solution)/shard_map/ppermute | solution.py:38
  251.4 2.2 copy-done
  253.6 1.7 shard_map.134
  255.3 2.8 %shard_map.135 = (f32[400,2560]{1,0:T(8,128)}, f32[20,128]{1,0:T(8,128)}) custom-call(s32[1]{0:T(128)} %bitcast.38.core_ref, f32[2,2048,128]{2,1,0:T(8,128)} %collective-permute-done.11.grad_ref, f32[400,2560]{1,0:T(8,128)S(1)} %bitcast.54, f32[20,128]{1,0:T(8,128)S(1)} %bitcast.72, ...), custom_call_target="tpu_custom_call", output_to_operand_aliasing={{0}: (4, {})} | custom-call | flops 5120000 | bytes 6291456 | tf_op jit(solution)/shard_map/pallas_call | solution.py:432
  (44 shorter events, 0.3 us)
Async XLA Ops:
  0.6 26.7 %copy-start.1 = (f32[256,400]{0,1:T(8,128)S(1)}, f32[256,400]{0,1:T(8,128)}, u32[]{:S(2)}) copy-start(f32[256,400]{0,1:T(8,128)} %param.9) | copy-start | bytes 1228804
  0.6 25.5 %copy-start.7 = (s32[1,2,1024]{2,1,0:T(2,128)S(1)}, s32[1,2,1024]{2,1,0:T(2,128)}, u32[]{:S(2)}) copy-start(s32[1,2,1024]{2,1,0:T(2,128)} %param.17) | copy-start | bytes 24580
  18.3 7.9 %collective-permute-start = (f32[352,128]{1,0:T(8,128)S(1)}, f32[352,128]{1,0:T(8,128)S(1)}, u32[]{:S(2)}, u32[]{:S(2)}) collective-permute-start(f32[352,128]{1,0:T(8,128)S(1)} %get-tuple-element.60), channel_id=1, source_target_pairs={{0,2},{2,0},{1,3},{3,1},{4,6},{6,4},{5,7},{7,5},{8,10},{10,8},{9,1... | collective-permute-start | bytes 540680 | tf_op jit(solution)/shard_map/ppermute | solution.py:38
  26.2 0.9 copy-start.3
  27.4 21.7 %collective-permute-start.2 = (f32[400,256]{1,0:T(8,128)S(1)}, f32[400,256]{1,0:T(8,128)S(1)}, u32[]{:S(2)}, u32[]{:S(2)}) collective-permute-start(f32[400,256]{1,0:T(8,128)S(1)} %bitcast.65), channel_id=1, source_target_pairs={{0,2},{2,0},{1,3},{3,1},{4,6},{6,4},{5,7},{7,5},{8,10},{10,8},{9,1... | collective-permute-start | bytes 1228808 | tf_op jit(solution)/shard_map/ppermute | solution.py:38
  30.7 18.3 %collective-permute-start.1 = (f32[368,128]{1,0:T(8,128)S(1)}, f32[368,128]{1,0:T(8,128)S(1)}, u32[]{:S(2)}, u32[]{:S(2)}) collective-permute-start(f32[368,128]{1,0:T(8,128)S(1)} %get-tuple-element.63), channel_id=1, source_target_pairs={{0,256},{32,288},{64,320},{96,352},{128,384},{160,416},{192,448},{... | collective-permute-start | bytes 565256 | tf_op jit(solution)/shard_map/ppermute | solution.py:38
  49.0 44.5 %copy-start.2 = (f32[2,400,256]{2,1,0:T(8,128)S(1)}, f32[2,400,256]{2,1,0:T(8,128)}, u32[]{:S(2)}) copy-start(f32[2,400,256]{2,1,0:T(8,128)} %shard_map.123.rel_ref) | copy-start | bytes 2457604
  49.0 44.5 %copy-start.6 = (f32[256]{0:T(256)S(1)}, f32[256]{0:T(256)}, u32[]{:S(2)}) copy-start(f32[256]{0:T(256)} %param.10) | copy-start | bytes 3076
  54.8 5.2 %collective-permute-start.3 = (f32[352,128]{1,0:T(8,128)S(1)}, f32[352,128]{1,0:T(8,128)S(1)}, u32[]{:S(2)}, u32[]{:S(2)}) collective-permute-start(f32[352,128]{1,0:T(8,128)S(1)} %get-tuple-element.69), channel_id=1, source_target_pairs={{0,1},{1,0},{2,3},{3,2},{4,5},{5,4},{6,7},{7,6},{8,9},{9,8},{10,11... | collective-permute-start | bytes 540680 | tf_op jit(solution)/shard_map/ppermute | solution.py:38
  57.1 27.3 %collective-permute-start.5 = (f32[400,256]{1,0:T(8,128)}, f32[400,256]{1,0:T(8,128)S(1)}, u32[]{:S(2)}, u32[]{:S(2)}) collective-permute-start(f32[400,256]{1,0:T(8,128)} %get-tuple-element.72), channel_id=1, source_target_pairs={{0,2},{2,0},{1,3},{3,1},{4,6},{6,4},{5,7},{7,5},{8,10},{10,8},{9,1... | collective-permute-start | bytes 1228808 | tf_op jit(solution)/shard_map/ppermute | solution.py:38
  60.1 24.4 %collective-permute-start.4 = (f32[352,128]{1,0:T(8,128)S(1)}, f32[352,128]{1,0:T(8,128)S(1)}, u32[]{:S(2)}, u32[]{:S(2)}) collective-permute-start(f32[352,128]{1,0:T(8,128)S(1)} %add.26), channel_id=1, source_target_pairs={{0,256},{32,288},{64,320},{96,352},{128,384},{160,416},{192,448},{... | collective-permute-start | bytes 540680 | tf_op jit(solution)/shard_map/ppermute | solution.py:38
  78.6 5.9 %collective-permute-start.6 = (s32[16,128]{1,0:T(8,128)S(1)}, s32[16,128]{1,0:T(8,128)S(1)}, u32[]{:S(2)}, u32[]{:S(2)}) collective-permute-start(s32[16,128]{1,0:T(8,128)S(1)} %pad_add_fusion.1), channel_id=1, source_target_pairs={{0,4},{4,0},{1,5},{5,1},{2,6},{6,2},{3,7},{7,3},{8,12},{12,8},{9,1... | collective-permute-start | bytes 24584 | tf_op jit(solution)/shard_map/ppermute | solution.py:38
  94.1 12.8 %collective-permute-start.7 = (f32[400,256]{1,0:T(8,128)S(1)}, f32[400,256]{1,0:T(8,128)S(1)}, u32[]{:S(2)}, u32[]{:S(2)}) collective-permute-start(f32[400,256]{1,0:T(8,128)S(1)} %get-tuple-element.80.own_ref), channel_id=1, source_target_pairs={{0,2},{2,0},{1,3},{3,1},{4,6},{6,4},{5,7},{7,5},{8,10},{10,8},{9,1... | collective-permute-start | bytes 1228808 | tf_op jit(solution)/shard_map/ppermute | solution.py:38
  104.0 16.5 %copy-start.4 = (f32[1,400,256]{2,1,0:T(8,128)S(1)}, f32[1,400,256]{2,1,0:T(8,128)}, u32[]{:S(2)}) copy-start(f32[1,400,256]{2,1,0:T(8,128)} %shard_map.127.rel_ref) | copy-start | bytes 1228804
  123.1 3.3 %collective-permute-start.8 = (f32[352,128]{1,0:T(8,128)S(1)}, f32[352,128]{1,0:T(8,128)S(1)}, u32[]{:S(2)}, u32[]{:S(2)}) collective-permute-start(f32[352,128]{1,0:T(8,128)S(1)} %get-tuple-element.85), channel_id=1, source_target_pairs={{0,1},{1,0},{2,3},{3,2},{4,5},{5,4},{6,7},{7,6},{8,9},{9,8},{10,11... | collective-permute-start | bytes 540680 | tf_op jit(solution)/shard_map/ppermute | solution.py:38
  137.0 23.4 %all-to-all-start = ((f32[8,256,128]{2,1,0:T(8,128)}), f32[8,256,128]{2,1,0:T(8,128)S(1)}, u32[]{:S(2)}, u32[]{:S(2)}) async-start(f32[8,256,128]{2,1,0:T(8,128)} %bitcast.31), calls=%async_computation | async-start | bytes 2097152 | tf_op jit(solution)/shard_map/all_to_all | solution.py:498
  141.8 18.6 %collective-permute-start.9 = (f32[352,128]{1,0:T(8,128)S(1)}, f32[352,128]{1,0:T(8,128)S(1)}, u32[]{:S(2)}, u32[]{:S(2)}) collective-permute-start(f32[352,128]{1,0:T(8,128)S(1)} %get-tuple-element.92), channel_id=1, source_target_pairs={{0,4},{4,0},{1,5},{5,1},{2,6},{6,2},{3,7},{7,3},{8,12},{12,8},{9,1... | collective-permute-start | bytes 540680 | tf_op jit(solution)/shard_map/ppermute | solution.py:38
  161.1 34.4 %all-to-all-start.1 = ((f32[16,16,128]{2,1,0:T(8,128)}), f32[16,16,128]{2,1,0:T(8,128)S(1)}, u32[]{:S(2)}, u32[]{:S(2)}) async-start(f32[16,16,128]{2,1,0:T(8,128)} %bitcast.32), calls=%async_computation.1 | async-start | bytes 262144 | tf_op jit(solution)/shard_map/all_to_all | solution.py:499
  195.5 55.9 %copy-start.5 = (f32[2560]{0:T(1024)S(1)}, f32[2560]{0:T(1024)}, u32[]{:S(2)}) copy-start(f32[2560]{0:T(1024)} %param.12) | copy-start | bytes 30724
  196.2 17.4 %all-to-all-start.2 = ((f32[16,16,128]{2,1,0:T(8,128)}), f32[16,16,128]{2,1,0:T(8,128)S(1)}, u32[]{:S(2)}, u32[]{:S(2)}) async-start(f32[16,16,128]{2,1,0:T(8,128)} %broadcast_in_dim.33), calls=%async_computation.2 | async-start | bytes 262144 | tf_op jit(solution)/shard_map/all_to_all | solution.py:503
  201.6 10.8 %collective-permute-start.10 = (f32[400,256]{1,0:T(8,128)S(1)}, f32[400,256]{1,0:T(8,128)S(1)}, u32[]{:S(2)}, u32[]{:S(2)}) collective-permute-start(f32[400,256]{1,0:T(8,128)S(1)} %get-tuple-element.100), channel_id=1, source_target_pairs={{0,2},{2,0},{1,3},{3,1},{4,6},{6,4},{5,7},{7,5},{8,10},{10,8},{9,1... | collective-permute-start | bytes 1228808 | tf_op jit(solution)/shard_map/ppermute | solution.py:38
  215.1 29.8 %all-to-all-start.3 = ((f32[16,256,128]{2,1,0:T(8,128)}), f32[16,256,128]{2,1,0:T(8,128)S(1)}, u32[]{:S(2)}, u32[]{:S(2)}) async-start(f32[16,256,128]{2,1,0:T(8,128)} %broadcast_in_dim.34), calls=%async_computation.3 | async-start | bytes 4194304 | tf_op jit(solution)/shard_map/all_to_all | solution.py:506
  245.0 10.3 %collective-permute-start.11 = (f32[2,2048,128]{2,1,0:T(8,128)S(1)}, f32[2,2048,128]{2,1,0:T(8,128)}, u32[]{:S(2)}, u32[]{:S(2)}) collective-permute-start(f32[2,2048,128]{2,1,0:T(8,128)S(1)} %bitcast.55), channel_id=1, source_target_pairs={{0,1},{1,0},{2,3},{3,2},{4,5},{5,4},{6,7},{7,6},{8,9},{9,8},{10,11... | collective-permute-start | bytes 6291464 | tf_op jit(solution)/shard_map/ppermute | solution.py:38
  251.4 2.2 copy-start

commit v5 on v4

--- a/solution.py
+++ b/solution.py
@@ -132,7 +132,7 @@
             out_ref[k] += found
 
 
-def lookup(s, ids, table):
+def lookup(s, ids, table, room=56):
     lists, _, width = ids.shape
     return call(
         lookup_kernel,
@@ -143,7 +143,7 @@
         4 * D * RELATIONS * lists * width,
         5 * 1024 * 1024,
         grid=(RELATIONS // PART,),
-        room=56,
+        room=room,
     )(s, ids, table)
 
 
@@ -465,7 +465,7 @@
     slots = slot_lists(src_rows, rel_ids, dst_rows, live_count)
     chunk_ids, chunk_kinds, chunk_targets = [pick(slots[k], 4, place) for k in range(3)]
     mine, theirs = halves(s, jnp.concatenate([chunk_ids, pick(slots[0], 4, place ^ 2)]), near)
-    chunk_rel = lookup(s, chunk_kinds[None], table)
+    chunk_rel = lookup(s, chunk_kinds[None], table, room=40)
     head, mail = letter(s, mine, flip(theirs, "l"), chunk_rel, chunk_targets, neg_rows[0, 0].reshape(8, 128))
     mail, head, own, bucket_kinds = tied((mail, head, own, slots[1]))
     other = flip(own, "l")

time: 259 us -> 257 us (level)
  Pallas kernels: 35.8 us -> 32.8 us
    pallas_call x3, Pallas kernels: 19.1 us -> 16.1 us  [lookup(): call(lookup_kernel, shape(lists, D, width), [whole(lists, 1, width), pl.B...]
  transfers between devices with their start and end apart: 16 -> 16, of which waited for: 8 -> 9; matrix products, arithmetic and copies ran while one was open for 0% -> 0% of each run, Pallas kernels for 9% -> 8%
where the time goes in v5:
time: 257 us; the launch traced here: 256 us
  starting transfers between devices  87.6 us (34%)
  waiting for transfers between devices  62.3 us (24%)
  blocking collectives  62.1 us (24%)
  Pallas kernels  32.8 us (13%)
  local copies, waits for them, and re-layouts  7.99 us (3%)
    ppermute x12, starting transfers between devices, flip(): return lax.ppermute(block, axis, [(i, i ^ mask) for i in range(count)])  50.6 us
    ppermute x12, waiting for transfers between devices, flip(): return lax.ppermute(block, axis, [(i, i ^ mask) for i in range(count)])  28.3 us
    all_to_all x1, waiting for transfers between devices, local(): lax.all_to_all(jnp.broadcast_to(share[None], (16, 256, 128)), ('l',) + SP...  24.6 us
    all_to_all x1, starting transfers between devices, local(): lax.all_to_all(jnp.sum(shares, axis=0).reshape(16, 16, 128), 'z', 0, 0)  22.6 us
    pallas_call x3, Pallas kernels, lookup(): call(lookup_kernel, shape(lists, D, width), [whole(lists, 1, width), pl.B...  16.1 us
    all_gather x1, blocking collectives, slot_lists(): lax.all_gather(lists.reshape(12, 128), REL, axis=0).reshape(4, 6, CAP)  11.9 us
    all_gather x1, blocking collectives, local(): head_rows = lax.all_gather(chunk, ('h', 'c'), axis=0)  9.87 us
    all_gather x1, blocking collectives, local(): answers = lax.all_gather(reply, REL, axis=0)  8.86 us
  transfers between devices with their start and end apart: 16, of which 9 were waited for; matrix products, arithmetic and copies ran while one was open for 0% of the time, Pallas kernels for 8%

profile of v5, /device:TPU:1, one launch (start us, length us, event | category | flops | bytes accessed | tf_op | source)
XLA Modules:
  0.0 256.3 jit_solution(2414386489267465192)
XLA Ops:
  0.7 0.8 iota_compare_fusion
  1.4 0.7 add_select_fusion
  2.2 11.9 %all_gather.57 = s32[4,12,128]{2,1,0:T(8,128)S(1)} all-gather(s32[1,12,128]{2,1,0:T(8,128)S(1)} %select_n.34), channel_id=1, replica_groups=mesh['z'=16,'y'=4,'h'=2,'l'=2,'c'=2] {'l','c'}, dimensions={0}, use_global_device_ids=true | all-gather | bytes 30720 | tf_op jit(solution)/shard_map/all_gather | solution.py:449
  14.1 0.1 slice_reduce_fusion
  14.2 0.1 reshape.126
  14.3 0.1 reshape.127
  14.3 0.6 pad_slice_fusion
  14.9 2.6 %all-gather = f32[800,256]{1,0:T(8,128)S(1)} all-gather(f32[400,256]{1,0:T(8,128)} %bitcast.64), channel_id=2, replica_groups=mesh['z'=16,'y'=4,'h'=2,'l'=2,'c'=2] {'c'}, dimensions={0}, use_global_device_ids=true | all-gather | bytes 1228800 | tf_op jit(solution)/shard_map/all_gather | solution.py:464
  17.5 0.7 shard_map.120
  18.3 1.9 collective-permute-start
  20.3 2.2 copy-done
  22.4 2.4 shard_map.121.rel_ref
  24.8 1.3 collective-permute-done.got_ref
  26.2 0.2 shard_map.122
  26.4 2.2 collective-permute-start.2
  28.6 11.0 %collective-permute-start.1 = (f32[368,128]{1,0:T(8,128)S(1)}, f32[368,128]{1,0:T(8,128)S(1)}, u32[]{:S(2)}, u32[]{:S(2)}) collective-permute-start(f32[368,128]{1,0:T(8,128)S(1)} %get-tuple-element.63), channel_id=1, source_target_pairs={{0,256},{32,288},{64,320},{96,352},{128,384},{160,416},{192,448},{... | collective-permute-start | bytes 565256 | tf_op jit(solution)/shard_map/ppermute | solution.py:38
  39.6 8.2 %shard_map.123.rel_ref = f32[2,400,256]{2,1,0:T(8,128)} custom-call(s32[1]{0:T(128)} %bitcast.s_ref, s32[2,1,256]{2,1,0:T(1,128)} %bitcast.85, f32[400,2560]{1,0:T(8,128)} %bitcast.50), custom_call_target="tpu_custom_call" | custom-call | flops 2097152000 | bytes 5242880 | tf_op jit(solution)/shard_map/pallas_call | solution.py:137
  47.8 3.4 %all-gather.1 = f32[736,128]{1,0:T(8,128)S(1)} all-gather(f32[368,128]{1,0:T(8,128)S(1)} %collective-permute-done.1), channel_id=3, replica_groups=mesh['z'=16,'y'=4,'h'=2,'l'=2,'c'=2] {'c'}, dimensions={0}, use_global_device_ids=true | all-gather | bytes 565248 | tf_op jit(solution)/shard_map/all_gather | solution.py:474
  51.2 2.7 %shard_map.124 = (f32[352,128]{1,0:T(8,128)S(1)}, f32[352,128]{1,0:T(8,128)S(1)}, f32[400,256]{1,0:T(8,128)S(1)}, f32[400,256]{1,0:T(8,128)}) custom-call(s32[1]{0:T(128)} %bitcast.s_ref, f32[2,368,128]{2,1,0:T(8,128)S(1)} %bitcast.70, f32[400,256]{1,0:T(8,128)S(1)} %bitcast.66, f32[400,256]{1,0:T(8,128)S(1)} %collective-permute-done.2.other_ref), custom_call_target="tpu_custom_call" | custom-call | flops 1073741824 | bytes 5242880 | tf_op jit(solution)/shard_map/pallas_call | solution.py:244
  53.9 2.3 collective-permute-start.3
  56.2 2.2 collective-permute-start.5
  58.4 0.1 pad_add_fusion.3.s_ref
  58.5 10.1 %collective-permute-start.4 = (f32[352,128]{1,0:T(8,128)S(1)}, f32[352,128]{1,0:T(8,128)S(1)}, u32[]{:S(2)}, u32[]{:S(2)}) collective-permute-start(f32[352,128]{1,0:T(8,128)S(1)} %add.26), channel_id=1, source_target_pairs={{0,256},{32,288},{64,320},{96,352},{128,384},{160,416},{192,448},{... | collective-permute-start | bytes 540680 | tf_op jit(solution)/shard_map/ppermute | solution.py:38
  68.6 8.4 %all-gather.2 = f32[1408,128]{1,0:T(8,128)S(1)} all-gather(f32[352,128]{1,0:T(8,128)S(1)} %get-tuple-element.73), channel_id=4, replica_groups=mesh['z'=16,'y'=4,'h'=2,'l'=2,'c'=2] {'l','c'}, dimensions={0}, use_global_device_ids=true | all-gather | bytes 901120 | tf_op jit(solution)/shard_map/all_gather | solution.py:477
  77.0 2.8 %collective-permute-start.6 = (s32[16,128]{1,0:T(8,128)S(1)}, s32[16,128]{1,0:T(8,128)S(1)}, u32[]{:S(2)}, u32[]{:S(2)}) collective-permute-start(s32[16,128]{1,0:T(8,128)S(1)} %pad_add_fusion.1), channel_id=1, source_target_pairs={{0,4},{4,0},{1,5},{5,1},{2,6},{6,2},{3,7},{7,3},{8,12},{12,8},{9,1... | collective-permute-start | bytes 24584 | tf_op jit(solution)/shard_map/ppermute | solution.py:38
  79.8 3.1 %collective-permute-done.6 = s32[16,128]{1,0:T(8,128)S(1)} collective-permute-done((s32[16,128]{1,0:T(8,128)S(1)}, s32[16,128]{1,0:T(8,128)S(1)}, u32[]{:S(2)}, u32[]{:S(2)}) %collective-permute-start.6) | collective-permute-done | bytes 8224 | tf_op jit(solution)/shard_map/ppermute | solution.py:38
  82.9 8.9 %all-gather.3 = f32[1408,128]{1,0:T(8,128)S(1)} all-gather(f32[352,128]{1,0:T(8,128)S(1)} %collective-permute-done.4), channel_id=5, replica_groups=mesh['z'=16,'y'=4,'h'=2,'l'=2,'c'=2] {'l','c'}, dimensions={0}, use_global_device_ids=true | all-gather | bytes 901120 | tf_op jit(solution)/shard_map/all_gather | solution.py:482
  91.8 0.6 shard_map.125
  92.4 2.7 %collective-permute-start.7 = (f32[400,256]{1,0:T(8,128)S(1)}, f32[400,256]{1,0:T(8,128)S(1)}, u32[]{:S(2)}, u32[]{:S(2)}) collective-permute-start(f32[400,256]{1,0:T(8,128)S(1)} %get-tuple-element.80.own_ref), channel_id=1, source_target_pairs={{0,2},{2,0},{1,3},{3,1},{4,6},{6,4},{5,7},{7,5},{8,10},{10,8},{9,1... | collective-permute-start | bytes 1228808 | tf_op jit(solution)/shard_map/ppermute | solution.py:38
  95.1 0.6 fusion.ids_ref
  95.7 1.2 shard_map.126.before_ref
  96.8 5.5 %shard_map.127.rel_ref = f32[1,400,256]{2,1,0:T(8,128)} custom-call(s32[1]{0:T(128)} %bitcast.s_ref, s32[1,1,256]{2,1,0:T(1,128)} %fusion.ids_ref, f32[400,2560]{1,0:T(8,128)} %bitcast.51), custom_call_target="tpu_custom_call" | custom-call | flops 1048576000 | bytes 5242880 | tf_op jit(solution)/shard_map/pallas_call | solution.py:137
  102.4 2.6 %all-gather.4 = f32[800,256]{1,0:T(8,128)S(1)} all-gather(f32[400,256]{1,0:T(8,128)S(1)} %get-tuple-element.80.own_ref), channel_id=6, replica_groups=mesh['z'=16,'y'=4,'h'=2,'l'=2,'c'=2] {'c'}, dimensions={0}, use_global_device_ids=true | all-gather | bytes 1228800 | tf_op jit(solution)/shard_map/all_gather | solution.py:487
  105.0 0.3 collective-permute-done.7.other_ref
  105.2 3.0 %all-gather.5 = f32[800,256]{1,0:T(8,128)S(1)} all-gather(f32[400,256]{1,0:T(8,128)S(1)} %collective-permute-done.7.other_ref), channel_id=7, replica_groups=mesh['z'=16,'y'=4,'h'=2,'l'=2,'c'=2] {'c'}, dimensions={0}, use_global_device_ids=true | all-gather | bytes 1228800 | tf_op jit(solution)/shard_map/all_gather | solution.py:490
  108.2 0.7 shard_map.128
  108.9 9.9 %all-gather.6 = f32[1408,128]{1,0:T(8,128)S(1)} all-gather(f32[352,128]{1,0:T(8,128)S(1)} %shard_map.128), channel_id=8, replica_groups=mesh['z'=16,'y'=4,'h'=2,'l'=2,'c'=2] {'h','c'}, dimensions={0}, use_global_device_ids=true | all-gather | bytes 901120 | tf_op jit(solution)/shard_map/all_gather | solution.py:491
  118.8 2.7 %shard_map.129 = (f32[352,128]{1,0:T(8,128)S(1)}, f32[352,128]{1,0:T(8,128)S(1)}, f32[400,256]{1,0:T(8,128)S(1)}, f32[400,256]{1,0:T(8,128)S(1)}, f32[400,128]{1,0:T(8,128)S(1)}, /*index=5*/f32[400,128]{1,0:T(8,128)S(1)}) custom-call(s32[2]{0:T(128)S(1)} %pad_add_fusion.3.s_ref, s32[1,256]{1,0:T(1,128)S(1)} %constant_dynamic-slice_fusion.3.target_ref, ...), custom_call_target="tpu_custom_call" | custom-call | flops 1073741824 | bytes 5242880 | tf_op jit(solution)/shard_map/pallas_call | solution.py:269
  121.4 2.1 collective-permute-start.8
  123.5 1.2 collective-permute-done.8.got_ref
  124.7 0.3 shard_map.130
  125.0 8.4 %all-gather.7 = f32[1408,128]{1,0:T(8,128)S(1)} all-gather(f32[352,128]{1,0:T(8,128)S(1)} %get-tuple-element.88), channel_id=9, replica_groups=mesh['z'=16,'y'=4,'h'=2,'l'=2,'c'=2] {'l','c'}, dimensions={0}, use_global_device_ids=true | all-gather | bytes 901120 | tf_op jit(solution)/shard_map/all_gather | solution.py:495
  133.4 1.9 shard_map.131
  135.3 4.9 %all-to-all-start = ((f32[8,256,128]{2,1,0:T(8,128)}), f32[8,256,128]{2,1,0:T(8,128)S(1)}, u32[]{:S(2)}, u32[]{:S(2)}) async-start(f32[8,256,128]{2,1,0:T(8,128)} %bitcast.31), calls=%async_computation | async-start | bytes 2097152 | tf_op jit(solution)/shard_map/all_to_all | solution.py:498
  140.1 4.9 %collective-permute-start.9 = (f32[352,128]{1,0:T(8,128)S(1)}, f32[352,128]{1,0:T(8,128)S(1)}, u32[]{:S(2)}, u32[]{:S(2)}) collective-permute-start(f32[352,128]{1,0:T(8,128)S(1)} %get-tuple-element.92), channel_id=1, source_target_pairs={{0,4},{4,0},{1,5},{5,1},{2,6},{6,2},{3,7},{7,3},{8,12},{12,8},{9,1... | collective-permute-start | bytes 540680 | tf_op jit(solution)/shard_map/ppermute | solution.py:38
  145.0 13.8 %collective-permute-done.9 = f32[352,128]{1,0:T(8,128)S(1)} collective-permute-done((f32[352,128]{1,0:T(8,128)S(1)}, f32[352,128]{1,0:T(8,128)S(1)}, u32[]{:S(2)}, u32[]{:S(2)}) %collective-permute-start.9) | collective-permute-done | bytes 180256 | tf_op jit(solution)/shard_map/ppermute | solution.py:38
  158.8 0.7 reduce_sum.18
  159.5 22.6 %all-to-all-start.1 = ((f32[16,16,128]{2,1,0:T(8,128)}), f32[16,16,128]{2,1,0:T(8,128)S(1)}, u32[]{:S(2)}, u32[]{:S(2)}) async-start(f32[16,16,128]{2,1,0:T(8,128)} %bitcast.32), calls=%async_computation.1 | async-start | bytes 262144 | tf_op jit(solution)/shard_map/all_to_all | solution.py:499
  182.1 3.3 %all-gather.8 = f32[704,128]{1,0:T(8,128)S(1)} all-gather(f32[352,128]{1,0:T(8,128)S(1)} %collective-permute-done.9), channel_id=10, replica_groups=mesh['z'=16,'y'=4,'h'=2,'l'=2,'c'=2] {'c'}, dimensions={0}, use_global_device_ids=true | all-gather | bytes 540672 | tf_op jit(solution)/shard_map/all_gather | solution.py:500
  185.3 0.4 shard_map.132
  185.8 8.3 %all-to-all-done.1 = f32[16,16,128]{2,1,0:T(8,128)S(1)} async-done(((f32[16,16,128]{2,1,0:T(8,128)}), f32[16,16,128]{2,1,0:T(8,128)S(1)}, u32[]{:S(2)}, u32[]{:S(2)}) %all-to-all-start.1) | async-done | bytes 131104 | tf_op jit(solution)/shard_map/all_to_all | solution.py:499
  194.1 0.7 broadcast_in_dim.33
  194.7 5.5 %all-to-all-start.2 = ((f32[16,16,128]{2,1,0:T(8,128)}), f32[16,16,128]{2,1,0:T(8,128)S(1)}, u32[]{:S(2)}, u32[]{:S(2)}) async-start(f32[16,16,128]{2,1,0:T(8,128)} %broadcast_in_dim.33), calls=%async_computation.2 | async-start | bytes 262144 | tf_op jit(solution)/shard_map/all_to_all | solution.py:503
  200.2 2.2 collective-permute-start.10
  202.4 8.6 %collective-permute-done.10.got_ref = f32[400,256]{1,0:T(8,128)S(1)} collective-permute-done((f32[400,256]{1,0:T(8,128)S(1)}, f32[400,256]{1,0:T(8,128)S(1)}, u32[]{:S(2)}, u32[]{:S(2)}) %collective-permute-start.10) | collective-permute-done | bytes 409632 | tf_op jit(solution)/shard_map/ppermute | solution.py:38
  211.1 1.2 all-to-all-done.2
  212.2 1.5 broadcast_in_dim.34
  213.7 4.1 %all-to-all-start.3 = ((f32[16,256,128]{2,1,0:T(8,128)}), f32[16,256,128]{2,1,0:T(8,128)S(1)}, u32[]{:S(2)}, u32[]{:S(2)}) async-start(f32[16,256,128]{2,1,0:T(8,128)} %broadcast_in_dim.34), calls=%async_computation.3 | async-start | bytes 4194304 | tf_op jit(solution)/shard_map/all_to_all | solution.py:506
  217.8 0.9 shard_map.133
  218.7 24.6 %all-to-all-done.3 = f32[16,256,128]{2,1,0:T(8,128)S(1)} async-done(((f32[16,256,128]{2,1,0:T(8,128)}), f32[16,256,128]{2,1,0:T(8,128)S(1)}, u32[]{:S(2)}, u32[]{:S(2)}) %all-to-all-start.3) | async-done | bytes 2097184 | tf_op jit(solution)/shard_map/all_to_all | solution.py:506
  243.3 6.4 %collective-permute-start.11 = (f32[2,2048,128]{2,1,0:T(8,128)S(1)}, f32[2,2048,128]{2,1,0:T(8,128)}, u32[]{:S(2)}, u32[]{:S(2)}) collective-permute-start(f32[2,2048,128]{2,1,0:T(8,128)S(1)} %bitcast.55), channel_id=1, source_target_pairs={{0,1},{1,0},{2,3},{3,2},{4,5},{5,4},{6,7},{7,6},{8,9},{9,8},{10,11... | collective-permute-start | bytes 6291464 | tf_op jit(solution)/shard_map/ppermute | solution.py:38
  249.7 2.2 copy-done.1
  251.8 1.7 shard_map.134
  253.5 2.8 %shard_map.135 = (f32[400,2560]{1,0:T(8,128)}, f32[20,128]{1,0:T(8,128)}) custom-call(s32[1]{0:T(128)} %bitcast.38.core_ref, f32[2,2048,128]{2,1,0:T(8,128)} %collective-permute-done.11.grad_ref, f32[400,2560]{1,0:T(8,128)S(1)} %bitcast.54, f32[20,128]{1,0:T(8,128)S(1)} %bitcast.72, ...), custom_call_target="tpu_custom_call", output_to_operand_aliasing={{0}: (4, {})} | custom-call | flops 5120000 | bytes 6291456 | tf_op jit(solution)/shard_map/pallas_call | solution.py:432
  (44 shorter events, 0.3 us)
Async XLA Ops:
  0.6 25.8 %copy-start.2 = (f32[256,400]{0,1:T(8,128)S(1)}, f32[256,400]{0,1:T(8,128)}, u32[]{:S(2)}) copy-start(f32[256,400]{0,1:T(8,128)} %param.9) | copy-start | bytes 1228804
  0.6 24.2 %copy-start.7 = (s32[1,2,1024]{2,1,0:T(2,128)S(1)}, s32[1,2,1024]{2,1,0:T(2,128)}, u32[]{:S(2)}) copy-start(s32[1,2,1024]{2,1,0:T(2,128)} %param.17) | copy-start | bytes 24580
  18.3 7.9 %collective-permute-start = (f32[352,128]{1,0:T(8,128)S(1)}, f32[352,128]{1,0:T(8,128)S(1)}, u32[]{:S(2)}, u32[]{:S(2)}) collective-permute-start(f32[352,128]{1,0:T(8,128)S(1)} %get-tuple-element.60), channel_id=1, source_target_pairs={{0,2},{2,0},{1,3},{3,1},{4,6},{6,4},{5,7},{7,5},{8,10},{10,8},{9,1... | collective-permute-start | bytes 540680 | tf_op jit(solution)/shard_map/ppermute | solution.py:38
  20.3 2.2 copy-start
  26.4 21.4 %collective-permute-start.2 = (f32[400,256]{1,0:T(8,128)S(1)}, f32[400,256]{1,0:T(8,128)S(1)}, u32[]{:S(2)}, u32[]{:S(2)}) collective-permute-start(f32[400,256]{1,0:T(8,128)S(1)} %bitcast.65), channel_id=1, source_target_pairs={{0,2},{2,0},{1,3},{3,1},{4,6},{6,4},{5,7},{7,5},{8,10},{10,8},{9,1... | collective-permute-start | bytes 1228808 | tf_op jit(solution)/shard_map/ppermute | solution.py:38
  28.6 19.2 %collective-permute-start.1 = (f32[368,128]{1,0:T(8,128)S(1)}, f32[368,128]{1,0:T(8,128)S(1)}, u32[]{:S(2)}, u32[]{:S(2)}) collective-permute-start(f32[368,128]{1,0:T(8,128)S(1)} %get-tuple-element.63), channel_id=1, source_target_pairs={{0,256},{32,288},{64,320},{96,352},{128,384},{160,416},{192,448},{... | collective-permute-start | bytes 565256 | tf_op jit(solution)/shard_map/ppermute | solution.py:38
  47.8 44.0 %copy-start.3 = (f32[2,400,256]{2,1,0:T(8,128)S(1)}, f32[2,400,256]{2,1,0:T(8,128)}, u32[]{:S(2)}) copy-start(f32[2,400,256]{2,1,0:T(8,128)} %shard_map.123.rel_ref) | copy-start | bytes 2457604
  47.8 44.0 %copy-start.6 = (f32[256]{0:T(256)S(1)}, f32[256]{0:T(256)}, u32[]{:S(2)}) copy-start(f32[256]{0:T(256)} %param.10) | copy-start | bytes 3076
  53.9 4.5 %collective-permute-start.3 = (f32[352,128]{1,0:T(8,128)S(1)}, f32[352,128]{1,0:T(8,128)S(1)}, u32[]{:S(2)}, u32[]{:S(2)}) collective-permute-start(f32[352,128]{1,0:T(8,128)S(1)} %get-tuple-element.69), channel_id=1, source_target_pairs={{0,1},{1,0},{2,3},{3,2},{4,5},{5,4},{6,7},{7,6},{8,9},{9,8},{10,11... | collective-permute-start | bytes 540680 | tf_op jit(solution)/shard_map/ppermute | solution.py:38
  56.2 26.7 %collective-permute-start.5 = (f32[400,256]{1,0:T(8,128)}, f32[400,256]{1,0:T(8,128)S(1)}, u32[]{:S(2)}, u32[]{:S(2)}) collective-permute-start(f32[400,256]{1,0:T(8,128)} %get-tuple-element.72), channel_id=1, source_target_pairs={{0,2},{2,0},{1,3},{3,1},{4,6},{6,4},{5,7},{7,5},{8,10},{10,8},{9,1... | collective-permute-start | bytes 1228808 | tf_op jit(solution)/shard_map/ppermute | solution.py:38
  58.5 24.4 %collective-permute-start.4 = (f32[352,128]{1,0:T(8,128)S(1)}, f32[352,128]{1,0:T(8,128)S(1)}, u32[]{:S(2)}, u32[]{:S(2)}) collective-permute-start(f32[352,128]{1,0:T(8,128)S(1)} %add.26), channel_id=1, source_target_pairs={{0,256},{32,288},{64,320},{96,352},{128,384},{160,416},{192,448},{... | collective-permute-start | bytes 540680 | tf_op jit(solution)/shard_map/ppermute | solution.py:38
  77.0 5.9 %collective-permute-start.6 = (s32[16,128]{1,0:T(8,128)S(1)}, s32[16,128]{1,0:T(8,128)S(1)}, u32[]{:S(2)}, u32[]{:S(2)}) collective-permute-start(s32[16,128]{1,0:T(8,128)S(1)} %pad_add_fusion.1), channel_id=1, source_target_pairs={{0,4},{4,0},{1,5},{5,1},{2,6},{6,2},{3,7},{7,3},{8,12},{12,8},{9,1... | collective-permute-start | bytes 24584 | tf_op jit(solution)/shard_map/ppermute | solution.py:38
  92.4 12.8 %collective-permute-start.7 = (f32[400,256]{1,0:T(8,128)S(1)}, f32[400,256]{1,0:T(8,128)S(1)}, u32[]{:S(2)}, u32[]{:S(2)}) collective-permute-start(f32[400,256]{1,0:T(8,128)S(1)} %get-tuple-element.80.own_ref), channel_id=1, source_target_pairs={{0,2},{2,0},{1,3},{3,1},{4,6},{6,4},{5,7},{7,5},{8,10},{10,8},{9,1... | collective-permute-start | bytes 1228808 | tf_op jit(solution)/shard_map/ppermute | solution.py:38
  102.4 16.4 %copy-start.4 = (f32[1,400,256]{2,1,0:T(8,128)S(1)}, f32[1,400,256]{2,1,0:T(8,128)}, u32[]{:S(2)}) copy-start(f32[1,400,256]{2,1,0:T(8,128)} %shard_map.127.rel_ref) | copy-start | bytes 1228804
  121.4 3.3 %collective-permute-start.8 = (f32[352,128]{1,0:T(8,128)S(1)}, f32[352,128]{1,0:T(8,128)S(1)}, u32[]{:S(2)}, u32[]{:S(2)}) collective-permute-start(f32[352,128]{1,0:T(8,128)S(1)} %get-tuple-element.85), channel_id=1, source_target_pairs={{0,1},{1,0},{2,3},{3,2},{4,5},{5,4},{6,7},{7,6},{8,9},{9,8},{10,11... | collective-permute-start | bytes 540680 | tf_op jit(solution)/shard_map/ppermute | solution.py:38
  135.3 23.5 %all-to-all-start = ((f32[8,256,128]{2,1,0:T(8,128)}), f32[8,256,128]{2,1,0:T(8,128)S(1)}, u32[]{:S(2)}, u32[]{:S(2)}) async-start(f32[8,256,128]{2,1,0:T(8,128)} %bitcast.31), calls=%async_computation | async-start | bytes 2097152 | tf_op jit(solution)/shard_map/all_to_all | solution.py:498
  140.1 18.6 %collective-permute-start.9 = (f32[352,128]{1,0:T(8,128)S(1)}, f32[352,128]{1,0:T(8,128)S(1)}, u32[]{:S(2)}, u32[]{:S(2)}) collective-permute-start(f32[352,128]{1,0:T(8,128)S(1)} %get-tuple-element.92), channel_id=1, source_target_pairs={{0,4},{4,0},{1,5},{5,1},{2,6},{6,2},{3,7},{7,3},{8,12},{12,8},{9,1... | collective-permute-start | bytes 540680 | tf_op jit(solution)/shard_map/ppermute | solution.py:38
  159.5 34.5 %all-to-all-start.1 = ((f32[16,16,128]{2,1,0:T(8,128)}), f32[16,16,128]{2,1,0:T(8,128)S(1)}, u32[]{:S(2)}, u32[]{:S(2)}) async-start(f32[16,16,128]{2,1,0:T(8,128)} %bitcast.32), calls=%async_computation.1 | async-start | bytes 262144 | tf_op jit(solution)/shard_map/all_to_all | solution.py:499
  194.0 55.6 %copy-start.5 = (f32[2560]{0:T(1024)S(1)}, f32[2560]{0:T(1024)}, u32[]{:S(2)}) copy-start(f32[2560]{0:T(1024)} %param.12) | copy-start | bytes 30724
  194.7 17.5 %all-to-all-start.2 = ((f32[16,16,128]{2,1,0:T(8,128)}), f32[16,16,128]{2,1,0:T(8,128)S(1)}, u32[]{:S(2)}, u32[]{:S(2)}) async-start(f32[16,16,128]{2,1,0:T(8,128)} %broadcast_in_dim.33), calls=%async_computation.2 | async-start | bytes 262144 | tf_op jit(solution)/shard_map/all_to_all | solution.py:503
  200.2 10.8 %collective-permute-start.10 = (f32[400,256]{1,0:T(8,128)S(1)}, f32[400,256]{1,0:T(8,128)S(1)}, u32[]{:S(2)}, u32[]{:S(2)}) collective-permute-start(f32[400,256]{1,0:T(8,128)S(1)} %get-tuple-element.100), channel_id=1, source_target_pairs={{0,2},{2,0},{1,3},{3,1},{4,6},{6,4},{5,7},{7,5},{8,10},{10,8},{9,1... | collective-permute-start | bytes 1228808 | tf_op jit(solution)/shard_map/ppermute | solution.py:38
  213.7 29.5 %all-to-all-start.3 = ((f32[16,256,128]{2,1,0:T(8,128)}), f32[16,256,128]{2,1,0:T(8,128)S(1)}, u32[]{:S(2)}, u32[]{:S(2)}) async-start(f32[16,256,128]{2,1,0:T(8,128)} %broadcast_in_dim.34), calls=%async_computation.3 | async-start | bytes 4194304 | tf_op jit(solution)/shard_map/all_to_all | solution.py:506
  243.3 10.3 %collective-permute-start.11 = (f32[2,2048,128]{2,1,0:T(8,128)S(1)}, f32[2,2048,128]{2,1,0:T(8,128)}, u32[]{:S(2)}, u32[]{:S(2)}) collective-permute-start(f32[2,2048,128]{2,1,0:T(8,128)S(1)} %bitcast.55), channel_id=1, source_target_pairs={{0,1},{1,0},{2,3},{3,2},{4,5},{5,4},{6,7},{7,6},{8,9},{9,8},{10,11... | collective-permute-start | bytes 6291464 | tf_op jit(solution)/shard_map/ppermute | solution.py:38
  249.6 2.2 copy-start.1
